TPU v7x, 256 devices: a whole 4x4x8 slice. The times are simulated.
256 devices in a mesh: section: 8 (over x_lo, y), dp: 32 (over x_hi, z, core).
Axes of the slice: x: 4 (x_hi: 2, x_lo: 2; x = x_hi * 2 + x_lo), y: 4, z: 8, core: 2. Of those that a mesh axis runs over, the one named last changes fastest.
Arguments:
- features: bfloat16 [2, 32, 16, 16, 256], P(None, 'dp'), may hold values from -6 to 6
- timesteps: int32 [2, 32], P(None, 'dp'), may hold values from 0 to 999
- codes: bfloat16 [8, 2, 2304, 256], P('section', None, 'dp'), may hold values from -0.125 to 0.125
- scales: float32 [8, 2, 18, 2], P('section'), may hold values from 0.5 to 2
- time_weight: bfloat16 [8, 256, 512], P('section'), may hold values from -0.375 to 0.375
Outputs:
- block_outputs: bfloat16 [8, 2, 32, 16, 16, 256], P('section', None, 'dp')
All inputs are finite; a program needn't handle non-finite values.
Results may differ from a plain program's by a relative error of at most 0.017.
Values may be sent and summed in bfloat16 or wider, within the bound.
No kernel may reach another device: no remote copies, remote signals or barrier semaphores. Data moves between devices by JAX's collectives and lax.ppermute only.
A program may use at most 64 MiB of HBM per device.

v0:
```python
import math

import jax
import jax.numpy as jnp
from jax import lax
from jax.sharding import PartitionSpec as P

GROUPS = 32
QB = 128


def swapped(array, axis, apart):
    return lax.ppermute(array, axis, [(i, i ^ 1 << apart) for i in range(lax.axis_size(axis))])


def from_behind(value, axis, steps):
    count = lax.axis_size(axis)
    leading, last = (max(0, -steps), min(count, count - steps))
    return lax.ppermute(value, axis, [(source, source + steps) for source in range(leading, last)])


def sinusoid(steps_in, channels):
    half_point = channels // 2
    freqs = jnp.exp(-math.log(10000.0) * jnp.arange(half_point, dtype=jnp.float32) / half_point)
    angles = steps_in.astype(jnp.float32)[:, None] * freqs[None, :]
    return jnp.concatenate([jnp.cos(angles), jnp.sin(angles)], axis=-1)


def group_norm(values, groups):
    samples_n, height, width_px, channels = values.shape
    grouped = values.reshape(samples_n, height * width_px, groups, channels // groups)
    mean_val = jnp.mean(grouped, axis=(1, 3), keepdims=True)
    centred = grouped - mean_val
    var_val = jnp.mean(centred * centred, axis=(1, 3), keepdims=True)
    return (centred * lax.rsqrt(var_val + 1e-05)).reshape(samples_n, height, width_px, channels)


def patches(activation):
    samples_n, height, width_px, channels = activation.shape
    padded = jnp.pad(activation, ((0, 0), (1, 1), (1, 1), (0, 0)))
    taps = [
        padded[:, row_off : row_off + height, col_off : col_off + width_px, :]
        for row_off in range(3)
        for col_off in range(3)
    ]
    return jnp.concatenate(taps, axis=-1).reshape(samples_n * height * width_px, 9 * channels)


def fold_term(columns, scale_part, shard_rows):
    dequantized = (shard_rows.astype(jnp.float32) * scale_part).astype(jnp.bfloat16)
    return jnp.dot(columns, dequantized, preferred_element_type=jnp.float32)


def shards(features, timesteps, codes, scales, time_weight):
    rescale = 0.7071067811865476
    sections = lax.axis_size("section")
    section_no = lax.axis_index("section")
    micro_count = features.shape[0]
    channels = features.shape[4]
    code_local = codes[0]
    scale_full = jnp.repeat(jnp.repeat(scales[0], QB, axis=1), QB, axis=2)
    t_weight = time_weight[0]

    def conv_first(columns):
        return fold_term(
            columns, scale_full[0], lax.all_gather(code_local[0], "dp", axis=0, tiled=True)
        )

    def conv_second(columns):
        return fold_term(
            columns, scale_full[1], lax.all_gather(code_local[1], "dp", axis=0, tiled=True)
        )

    def res_block(block_in, embedding):
        first_in = jax.nn.silu(group_norm(block_in, GROUPS)).astype(jnp.bfloat16)
        hidden = conv_first(patches(first_in)).reshape(block_in.shape)
        emb_act = jax.nn.silu(embedding).astype(jnp.bfloat16)
        modulation = jnp.dot(emb_act, t_weight, preferred_element_type=jnp.float32)
        scale_mod = modulation[:, :channels][:, None, None, :]
        shift_mod = modulation[:, channels:][:, None, None, :]
        second_in = jax.nn.silu(group_norm(hidden, GROUPS) * (1.0 + scale_mod) + shift_mod).astype(
            jnp.bfloat16
        )
        branch = conv_second(patches(second_in)).reshape(block_in.shape)
        return (block_in + branch).astype(jnp.bfloat16)

    decoder = section_no >= sections // 2
    mirrored = sections - 1 - section_no

    def tick(carry, tick_no):
        incoming, skip_buffer, out_buffer = carry
        micro_idx = tick_no - section_no
        valid = (micro_idx >= 0) & (micro_idx < micro_count)
        clipped = jnp.clip(micro_idx, 0, micro_count - 1)
        feed_in = lax.dynamic_index_in_dim(features, clipped, 0, keepdims=False)
        entering = jnp.where(section_no == 0, feed_in, incoming)
        skip_in = lax.dynamic_index_in_dim(skip_buffer, clipped, 0, keepdims=False)
        block_in = jnp.where(
            decoder,
            (entering.astype(jnp.float32) + skip_in.astype(jnp.float32)) * rescale,
            entering.astype(jnp.float32),
        )
        embedding = sinusoid(
            lax.dynamic_index_in_dim(timesteps, clipped, 0, keepdims=False), channels
        )
        block_out = res_block(block_in, embedding)
        written = lax.dynamic_update_index_in_dim(out_buffer, block_out, clipped, 0)
        out_buffer = jnp.where(valid, written, out_buffer)
        payload = block_out
        for bit_index in range(sections.bit_length() - 1):
            payload = swapped(payload, "section", bit_index)
        source_tick = tick_no - mirrored
        storing = decoder & (source_tick >= 0) & (source_tick < micro_count)
        source_slot = jnp.clip(source_tick, 0, micro_count - 1)
        filled = lax.dynamic_update_index_in_dim(skip_buffer, payload, source_slot, 0)
        skip_buffer = jnp.where(storing, filled, skip_buffer)
        incoming = from_behind(block_out, "section", 1)
        return ((incoming, skip_buffer, out_buffer), None)

    start_in = jnp.zeros(features.shape[1:], jnp.bfloat16)
    start_buf = jnp.zeros(features.shape, jnp.bfloat16)
    ticks = jnp.arange(sections + micro_count - 1, dtype=jnp.int32)
    final, unused = lax.scan(tick, (start_in, start_buf, start_buf), ticks)
    return final[2][None]


def solution(mesh):
    in_specs = (
        P(None, "dp", None, None, None),
        P(None, "dp"),
        P("section", None, "dp", None),
        P("section", None, None, None),
        P("section", None, None),
    )
    out_specs = P("section", None, "dp", None, None, None)
    return jax.shard_map(shards, mesh=mesh, in_specs=in_specs, out_specs=out_specs, check_vma=False)
```

profile of v0, /device:TPU:26, one launch (start us, length us, event | category | flops | bytes accessed | tf_op | source)
XLA Modules:
  0.0 1643.9 jit_solution(13791172567707269804)
XLA Ops:
  7.5 6.7 broadcast_in_dim.41
  14.2 7.3 reshape.362
  21.6 1614.8 %while.17 = (s32[]{:T(128)}, bf16[1,16,16,256]{3,2,1,0:T(8,128)(2,1)S(1)}, bf16[2,1,16,16,256]{4,3,2,1,0:T(8,128)(2,1)S(1)}, bf16[2,1,16,16,256]{4,3,2,1,0:T(8,1...) while((s32[]{:T(128)}, ...), condition=%wide.region_9.10_spmd, body=%wide.region_0.9_spmd.sunk | while | flops 611780672 | bytes 28997200 | solution.py:123
  27.4 77.4 %all-gather.11.cloned.1.call-done = bf16[1,2304,256]{2,1,0:T(8,128)(2,1)} async-done(((bf16[1,72,256]{2,1,0:T(8,128)(2,1)}), bf16[1,2304,256]{2,1,0:T(8,128)(2,1)}) %all-gather.11.cloned.1.call-update) | async-done | bytes 1179664 | tf_op jit(solution)/shard_map/while/body/eval_jaxpr/all_gather | solution.py:66
  108.6 73.4 %all-gather.9.cloned.1.call-done = bf16[1,2304,256]{2,1,0:T(8,128)(2,1)} async-done(((bf16[1,72,256]{2,1,0:T(8,128)(2,1)}), bf16[1,2304,256]{2,1,0:T(8,128)(2,1)}) %all-gather.9.cloned.1.call-update) | async-done | bytes 1179664 | tf_op jit(solution)/shard_map/while/body/eval_jaxpr/all_gather | solution.py:71
  191.7 5.1 collective-permute-done.2
  211.5 72.4 %all-gather.11.cloned.1.call-done = bf16[1,2304,256]{2,1,0:T(8,128)(2,1)} async-done(((bf16[1,72,256]{2,1,0:T(8,128)(2,1)}), bf16[1,2304,256]{2,1,0:T(8,128)(2,1)}) %all-gather.11.cloned.1.call-update) | async-done | bytes 1179664 | tf_op jit(solution)/shard_map/while/body/eval_jaxpr/all_gather | solution.py:66
  287.7 73.3 %all-gather.9.cloned.1.call-done = bf16[1,2304,256]{2,1,0:T(8,128)(2,1)} async-done(((bf16[1,72,256]{2,1,0:T(8,128)(2,1)}), bf16[1,2304,256]{2,1,0:T(8,128)(2,1)}) %all-gather.9.cloned.1.call-update) | async-done | bytes 1179664 | tf_op jit(solution)/shard_map/while/body/eval_jaxpr/all_gather | solution.py:71
  390.3 72.1 %all-gather.11.cloned.1.call-done = bf16[1,2304,256]{2,1,0:T(8,128)(2,1)} async-done(((bf16[1,72,256]{2,1,0:T(8,128)(2,1)}), bf16[1,2304,256]{2,1,0:T(8,128)(2,1)}) %all-gather.11.cloned.1.call-update) | async-done | bytes 1179664 | tf_op jit(solution)/shard_map/while/body/eval_jaxpr/all_gather | solution.py:66
  466.3 73.3 %all-gather.9.cloned.1.call-done = bf16[1,2304,256]{2,1,0:T(8,128)(2,1)} async-done(((bf16[1,72,256]{2,1,0:T(8,128)(2,1)}), bf16[1,2304,256]{2,1,0:T(8,128)(2,1)}) %all-gather.9.cloned.1.call-update) | async-done | bytes 1179664 | tf_op jit(solution)/shard_map/while/body/eval_jaxpr/all_gather | solution.py:71
  569.2 72.2 %all-gather.11.cloned.1.call-done = bf16[1,2304,256]{2,1,0:T(8,128)(2,1)} async-done(((bf16[1,72,256]{2,1,0:T(8,128)(2,1)}), bf16[1,2304,256]{2,1,0:T(8,128)(2,1)}) %all-gather.11.cloned.1.call-update) | async-done | bytes 1179664 | tf_op jit(solution)/shard_map/while/body/eval_jaxpr/all_gather | solution.py:66
  645.2 73.4 %all-gather.9.cloned.1.call-done = bf16[1,2304,256]{2,1,0:T(8,128)(2,1)} async-done(((bf16[1,72,256]{2,1,0:T(8,128)(2,1)}), bf16[1,2304,256]{2,1,0:T(8,128)(2,1)}) %all-gather.9.cloned.1.call-update) | async-done | bytes 1179664 | tf_op jit(solution)/shard_map/while/body/eval_jaxpr/all_gather | solution.py:71
  728.3 5.1 collective-permute-done.2
  748.1 72.4 %all-gather.11.cloned.1.call-done = bf16[1,2304,256]{2,1,0:T(8,128)(2,1)} async-done(((bf16[1,72,256]{2,1,0:T(8,128)(2,1)}), bf16[1,2304,256]{2,1,0:T(8,128)(2,1)}) %all-gather.11.cloned.1.call-update) | async-done | bytes 1179664 | tf_op jit(solution)/shard_map/while/body/eval_jaxpr/all_gather | solution.py:66
  824.3 73.3 %all-gather.9.cloned.1.call-done = bf16[1,2304,256]{2,1,0:T(8,128)(2,1)} async-done(((bf16[1,72,256]{2,1,0:T(8,128)(2,1)}), bf16[1,2304,256]{2,1,0:T(8,128)(2,1)}) %all-gather.9.cloned.1.call-update) | async-done | bytes 1179664 | tf_op jit(solution)/shard_map/while/body/eval_jaxpr/all_gather | solution.py:71
  927.0 72.4 %all-gather.11.cloned.1.call-done = bf16[1,2304,256]{2,1,0:T(8,128)(2,1)} async-done(((bf16[1,72,256]{2,1,0:T(8,128)(2,1)}), bf16[1,2304,256]{2,1,0:T(8,128)(2,1)}) %all-gather.11.cloned.1.call-update) | async-done | bytes 1179664 | tf_op jit(solution)/shard_map/while/body/eval_jaxpr/all_gather | solution.py:66
  1003.2 73.3 %all-gather.9.cloned.1.call-done = bf16[1,2304,256]{2,1,0:T(8,128)(2,1)} async-done(((bf16[1,72,256]{2,1,0:T(8,128)(2,1)}), bf16[1,2304,256]{2,1,0:T(8,128)(2,1)}) %all-gather.9.cloned.1.call-update) | async-done | bytes 1179664 | tf_op jit(solution)/shard_map/while/body/eval_jaxpr/all_gather | solution.py:71
  1105.9 72.4 %all-gather.11.cloned.1.call-done = bf16[1,2304,256]{2,1,0:T(8,128)(2,1)} async-done(((bf16[1,72,256]{2,1,0:T(8,128)(2,1)}), bf16[1,2304,256]{2,1,0:T(8,128)(2,1)}) %all-gather.11.cloned.1.call-update) | async-done | bytes 1179664 | tf_op jit(solution)/shard_map/while/body/eval_jaxpr/all_gather | solution.py:66
  1182.1 73.3 %all-gather.9.cloned.1.call-done = bf16[1,2304,256]{2,1,0:T(8,128)(2,1)} async-done(((bf16[1,72,256]{2,1,0:T(8,128)(2,1)}), bf16[1,2304,256]{2,1,0:T(8,128)(2,1)}) %all-gather.9.cloned.1.call-update) | async-done | bytes 1179664 | tf_op jit(solution)/shard_map/while/body/eval_jaxpr/all_gather | solution.py:71
  1265.0 5.1 collective-permute-done.2
  1284.7 72.1 %all-gather.11.cloned.1.call-done = bf16[1,2304,256]{2,1,0:T(8,128)(2,1)} async-done(((bf16[1,72,256]{2,1,0:T(8,128)(2,1)}), bf16[1,2304,256]{2,1,0:T(8,128)(2,1)}) %all-gather.11.cloned.1.call-update) | async-done | bytes 1179664 | tf_op jit(solution)/shard_map/while/body/eval_jaxpr/all_gather | solution.py:66
  1360.7 73.3 %all-gather.9.cloned.1.call-done = bf16[1,2304,256]{2,1,0:T(8,128)(2,1)} async-done(((bf16[1,72,256]{2,1,0:T(8,128)(2,1)}), bf16[1,2304,256]{2,1,0:T(8,128)(2,1)}) %all-gather.9.cloned.1.call-update) | async-done | bytes 1179664 | tf_op jit(solution)/shard_map/while/body/eval_jaxpr/all_gather | solution.py:71
  1463.3 72.1 %all-gather.11.cloned.1.call-done = bf16[1,2304,256]{2,1,0:T(8,128)(2,1)} async-done(((bf16[1,72,256]{2,1,0:T(8,128)(2,1)}), bf16[1,2304,256]{2,1,0:T(8,128)(2,1)}) %all-gather.11.cloned.1.call-update) | async-done | bytes 1179664 | tf_op jit(solution)/shard_map/while/body/eval_jaxpr/all_gather | solution.py:66
  1539.3 73.3 %all-gather.9.cloned.1.call-done = bf16[1,2304,256]{2,1,0:T(8,128)(2,1)} async-done(((bf16[1,72,256]{2,1,0:T(8,128)(2,1)}), bf16[1,2304,256]{2,1,0:T(8,128)(2,1)}) %all-gather.9.cloned.1.call-update) | async-done | bytes 1179664 | tf_op jit(solution)/shard_map/while/body/eval_jaxpr/all_gather | solution.py:71
  (625 shorter events, 270.6 us)
Async XLA Ops:
  21.6 83.2 %all-gather.11.cloned.1.call-start = ((), (), s32[]{:S(2)}) async-start(), calls=%async_computation.1 | async-start | bytes 1216512 | tf_op jit(solution)/shard_map/while/body/eval_jaxpr/all_gather | solution.py:66
  22.3 159.8 %all-gather.9.cloned.1.call-start = ((), (), s32[]{:S(2)}) async-start(), calls=%async_computation | async-start | bytes 1216512 | tf_op jit(solution)/shard_map/while/body/eval_jaxpr/all_gather | solution.py:71
  198.9 6.9 collective-permute-start
  205.8 78.1 %all-gather.11.cloned.1.call-start = ((), (), s32[]{:S(2)}) async-start(), calls=%async_computation.1 | async-start | bytes 1216512 | tf_op jit(solution)/shard_map/while/body/eval_jaxpr/all_gather | solution.py:66
  206.5 154.5 %all-gather.9.cloned.1.call-start = ((), (), s32[]{:S(2)}) async-start(), calls=%async_computation | async-start | bytes 1216512 | tf_op jit(solution)/shard_map/while/body/eval_jaxpr/all_gather | solution.py:71
  377.8 6.9 collective-permute-start
  384.7 77.8 %all-gather.11.cloned.1.call-start = ((), (), s32[]{:S(2)}) async-start(), calls=%async_computation.1 | async-start | bytes 1216512 | tf_op jit(solution)/shard_map/while/body/eval_jaxpr/all_gather | solution.py:66
  385.4 154.2 %all-gather.9.cloned.1.call-start = ((), (), s32[]{:S(2)}) async-start(), calls=%async_computation | async-start | bytes 1216512 | tf_op jit(solution)/shard_map/while/body/eval_jaxpr/all_gather | solution.py:71
  556.4 6.9 collective-permute-start
  563.3 78.1 %all-gather.11.cloned.1.call-start = ((), (), s32[]{:S(2)}) async-start(), calls=%async_computation.1 | async-start | bytes 1216512 | tf_op jit(solution)/shard_map/while/body/eval_jaxpr/all_gather | solution.py:66
  564.0 154.6 %all-gather.9.cloned.1.call-start = ((), (), s32[]{:S(2)}) async-start(), calls=%async_computation | async-start | bytes 1216512 | tf_op jit(solution)/shard_map/while/body/eval_jaxpr/all_gather | solution.py:71
  735.5 6.9 collective-permute-start
  742.4 78.1 %all-gather.11.cloned.1.call-start = ((), (), s32[]{:S(2)}) async-start(), calls=%async_computation.1 | async-start | bytes 1216512 | tf_op jit(solution)/shard_map/while/body/eval_jaxpr/all_gather | solution.py:66
  743.1 154.4 %all-gather.9.cloned.1.call-start = ((), (), s32[]{:S(2)}) async-start(), calls=%async_computation | async-start | bytes 1216512 | tf_op jit(solution)/shard_map/while/body/eval_jaxpr/all_gather | solution.py:71
  914.4 6.9 collective-permute-start
  921.3 78.1 %all-gather.11.cloned.1.call-start = ((), (), s32[]{:S(2)}) async-start(), calls=%async_computation.1 | async-start | bytes 1216512 | tf_op jit(solution)/shard_map/while/body/eval_jaxpr/all_gather | solution.py:66
  922.0 154.5 %all-gather.9.cloned.1.call-start = ((), (), s32[]{:S(2)}) async-start(), calls=%async_computation | async-start | bytes 1216512 | tf_op jit(solution)/shard_map/while/body/eval_jaxpr/all_gather | solution.py:71
  1093.3 6.9 collective-permute-start
  1100.2 78.1 %all-gather.11.cloned.1.call-start = ((), (), s32[]{:S(2)}) async-start(), calls=%async_computation.1 | async-start | bytes 1216512 | tf_op jit(solution)/shard_map/while/body/eval_jaxpr/all_gather | solution.py:66
  1100.9 154.4 %all-gather.9.cloned.1.call-start = ((), (), s32[]{:S(2)}) async-start(), calls=%async_computation | async-start | bytes 1216512 | tf_op jit(solution)/shard_map/while/body/eval_jaxpr/all_gather | solution.py:71
  1279.1 77.8 %all-gather.11.cloned.1.call-start = ((), (), s32[]{:S(2)}) async-start(), calls=%async_computation.1 | async-start | bytes 1216512 | tf_op jit(solution)/shard_map/while/body/eval_jaxpr/all_gather | solution.py:66
  1279.8 154.2 %all-gather.9.cloned.1.call-start = ((), (), s32[]{:S(2)}) async-start(), calls=%async_computation | async-start | bytes 1216512 | tf_op jit(solution)/shard_map/while/body/eval_jaxpr/all_gather | solution.py:71
  1457.7 77.7 %all-gather.11.cloned.1.call-start = ((), (), s32[]{:S(2)}) async-start(), calls=%async_computation.1 | async-start | bytes 1216512 | tf_op jit(solution)/shard_map/while/body/eval_jaxpr/all_gather | solution.py:66
  1458.4 154.2 %all-gather.9.cloned.1.call-start = ((), (), s32[]{:S(2)}) async-start(), calls=%async_computation | async-start | bytes 1216512 | tf_op jit(solution)/shard_map/while/body/eval_jaxpr/all_gather | solution.py:71
  (35 other events, 208.7 us)
Sparse Core Ops, SparseCore 0:
  25.1 79.6 all-gather.10
  107.5 74.5 all-gather.8
  209.3 74.4 all-gather.10
  286.4 74.5 all-gather.8
  387.9 74.4 all-gather.10
  465.0 74.5 all-gather.8
  566.8 74.4 all-gather.10
  644.1 74.5 all-gather.8
  745.9 74.4 all-gather.10
  823.0 74.5 all-gather.8
  924.8 74.4 all-gather.10
  1001.9 74.5 all-gather.8
  1103.7 74.4 all-gather.10
  1180.8 74.5 all-gather.8
  1282.3 74.4 all-gather.10
  1359.4 74.5 all-gather.8
  1460.9 74.4 all-gather.10
  1538.0 74.5 all-gather.8
where the time goes:
time: 1650 us; the launch traced here: 1640 us
  waiting for transfers between devices  1460 us (88%)
  starting transfers between devices  46.2 us (3%)
  matrix products  45.9 us (3%)
  local copies, waits for them, and re-layouts  40.3 us (2%)
  other arithmetic  23 us (1%)
    all_gather x9, waiting for transfers between devices, conv_second(): lax.all_gather(code_local[1], 'dp', axis=0, tiled=True)  660 us
    all_gather x9, waiting for transfers between devices, conv_first(): lax.all_gather(code_local[0], 'dp', axis=0, tiled=True)  655 us
    ppermute x27, waiting for transfers between devices, swapped(): lax.ppermute(array, axis, [(i, i ^ 1 << apart) for i in range(lax.axis_si...  106 us
    dot_general x18, matrix products, fold_term(): return jnp.dot(columns, dequantized, preferred_element_type=jnp.float32)  44.6 us
    ppermute x27, starting transfers between devices, swapped(): lax.ppermute(array, axis, [(i, i ^ 1 << apart) for i in range(lax.axis_si...  34.1 us
  transfers between devices with their start and end apart: 54, of which 54 were waited for; matrix products, arithmetic and copies ran while one was open for 4% of the time, Pallas kernels for 0%

commit v1 on v0

v1 whole, which is shorter than its diff:
```python
import functools
import math

import jax
import jax.numpy as jnp
from jax import lax
from jax.experimental import pallas as pl
from jax.experimental.pallas import tpu as pltpu
from jax.sharding import PartitionSpec as P

GROUP = 8
QB = 128
SIDE = 16
RING = 8
RESCALE = 0.7071067811865476
VMEM = pl.BlockSpec(memory_space=pltpu.VMEM)
SMEM = pl.BlockSpec(memory_space=pltpu.SMEM)


def across_lanes(values, bit):
    lane = lax.broadcasted_iota(jnp.int32, values.shape, 1)
    return jnp.take_along_axis(values, lane ^ bit, axis=1)


def normalize(values):
    pixels, channels = values.shape
    mean = jnp.sum(values, axis=0, keepdims=True) * (1.0 / pixels)
    spread = values - mean
    square = jnp.sum(spread * spread, axis=0, keepdims=True)
    upper = lax.broadcasted_iota(jnp.int32, (8, channels), 0) < 4
    both = jnp.where(upper, mean, square)
    count = pixels
    for bit in (1, 2, 4):
        halves = [across_lanes(both[:, k : k + 128], bit) for k in range(0, channels, 128)]
        partner = jnp.concatenate(halves, axis=1)
        apart = both - partner
        between = pltpu.roll(apart * apart, 4, 0) * (0.5 * count)
        both = jnp.where(upper, 0.5 * (both + partner), both + partner + between)
        count = 2 * count
    return values - both[0:1], lax.rsqrt(both[4:5] * (1.0 / count) + 1e-05)


def silu(values):
    half = 0.5 * values
    return half + half * jnp.tanh(half)


def conv(activation, rows, weight):
    pixels, channels = activation.shape
    rows[pl.ds(SIDE, pixels), :] = activation.astype(jnp.bfloat16)
    sides = []
    for right in (0, 2, 1):
        total = None
        for down in range(3):
            tap = 3 * down + right
            part = jnp.dot(
                rows[pl.ds(SIDE * down, pixels), :],
                weight[pl.ds(channels * tap, channels), :],
                preferred_element_type=jnp.float32,
            )
            total = part if total is None else total + part
        sides.append(total)
    column = lax.broadcasted_iota(jnp.int32, activation.shape, 0) & (SIDE - 1)
    before = jnp.where(column == 0, 0.0, pltpu.roll(sides[0], 1, 0))
    after = jnp.where(column == SIDE - 1, 0.0, pltpu.roll(sides[1], pixels - 1, 0))
    return sides[2] + before + after


def block_kernel(step, entering, skip, modulation, weights, old, out, rows):
    depth = weights.shape[0] // 2
    channels = entering.shape[1]

    @pl.when(lax.axis_index("section") == step)
    def _():
        edge = jnp.zeros((SIDE, channels), jnp.bfloat16)
        rows[pl.ds(0, SIDE), :] = edge
        rows[pl.ds(rows.shape[0] - SIDE, SIDE), :] = edge
        block_in = entering[...].astype(jnp.float32)
        if skip is not None:
            block_in = (block_in + skip[...].astype(jnp.float32)) * RESCALE
        centred, inverse = normalize(block_in)
        hidden = conv(silu(centred * inverse), rows, weights.at[pl.ds(0, depth), :])
        centred, inverse = normalize(hidden)
        scale = modulation[:, :channels]
        shift = modulation[:, channels:]
        second = silu(centred * (inverse * (1.0 + scale)) + shift)
        branch = conv(second, rows, weights.at[pl.ds(depth, depth), :])
        out[...] = (block_in + branch).astype(jnp.bfloat16)


def res_block(step, entering, skip, modulation, weights, old):
    pixels, channels = entering.shape
    return pl.pallas_call(
        functools.partial(block_kernel, step),
        out_shape=jax.ShapeDtypeStruct(entering.shape, jnp.bfloat16),
        in_specs=[VMEM, None if skip is None else VMEM, VMEM, VMEM, VMEM],
        out_specs=VMEM,
        input_output_aliases={3 if skip is None else 4: 0},
        scratch_shapes=[pltpu.VMEM((pixels + 2 * SIDE, channels), jnp.bfloat16)],
        compiler_params=pltpu.CompilerParams(vmem_limit_bytes=16 * 1024 * 1024),
        cost_estimate=pl.CostEstimate(
            flops=2 * weights.shape[0] * channels * pixels,
            bytes_accessed=3000000,
            transcendentals=2 * pixels * channels,
        ),
    )(entering, skip, modulation, weights, old)


def sinusoid(steps_in, channels):
    half_point = channels // 2
    freqs = jnp.exp(-math.log(10000.0) * jnp.arange(half_point, dtype=jnp.float32) / half_point)
    angles = steps_in.astype(jnp.float32)[:, None] * freqs[None, :]
    return jnp.concatenate([jnp.cos(angles), jnp.sin(angles)], axis=-1)


def dp_place():
    position = lax.axis_index("dp")
    return position // (2 * RING), position // 2 % RING, position % 2


def assemble_kernel(there, chips, scales, mine, theirs, half, half_other, old, out):
    far, along, core = dp_place()
    ahead = 1 - 2 * core
    rows, channels = out.shape[1] // (2 * RING), out.shape[2]
    row = lax.broadcasted_iota(jnp.int32, (rows, channels), 0)

    def place(block, facing, where, number):
        side = 1 - far if facing else far
        position = lax.rem(where + RING, RING)
        first = side * (scales.shape[1] // 2) + position
        here = scales[number, pl.ds(first, 1), :]
        later = scales[number, pl.ds(first + 1, 1), :]
        scale = jnp.where(row < QB - SIDE * position, here, later)
        start = pl.multiple_of(side * (RING * rows) + position * rows, SIDE)
        scaled = (block.astype(jnp.float32) * scale).astype(jnp.bfloat16)
        out[number, pl.ds(start, rows), :] = scaled

    convs = out.shape[0]

    def spread(block, facing, where):
        for number in range(block.shape[0]):
            if number < convs:
                place(block[number], facing, where, number)
            elif block.shape[0] == 2 * convs:
                place(block[number], not facing, where, number - convs)

    for (facing, hops), block in zip(there, mine):
        spread(block, facing, along + ahead * hops)
    for (facing, hops), block in zip(there[len(there) - len(theirs) :], theirs):
        spread(block, facing, along - ahead * hops)
    if half is None:
        half, half_other = mine[-1].at[convs], theirs[-1].at[convs]
    place(half[...], chips, along + RING // 2, core)
    place(half_other[...], chips, along + RING // 2, 1 - core)


def assembled(there, facing, scales, mine, theirs, half, half_other, old):
    rows, channels = mine[0].shape[1:]
    shape = (scales.shape[0], 2 * RING * rows, channels)
    return pl.pallas_call(
        functools.partial(assemble_kernel, there, facing),
        out_shape=jax.ShapeDtypeStruct(shape, jnp.bfloat16),
        in_specs=[
            VMEM,
            [VMEM] * len(mine),
            [VMEM] * len(theirs),
            None if half is None else VMEM,
            None if half is None else VMEM,
            None if old is None else VMEM,
        ],
        out_specs=VMEM,
        input_output_aliases={} if old is None else {1 + len(mine) + len(theirs): 0},
        compiler_params=pltpu.CompilerParams(vmem_limit_bytes=16 * 1024 * 1024),
    )(scales, mine, theirs, half, half_other, old)


def gathered_weights(codes, scales, features, timesteps):
    count = lax.axis_size("dp")
    _, _, core = dp_place()
    convs, rows, channels = codes.shape

    def onward(i, hops):
        step = hops * (2 * (i % 2) - 1)
        return i // (2 * RING) * 2 * RING + (i // 2 + step) % RING * 2 + i % 2

    def along_ring(value, hops):
        return lax.ppermute(value, "dp", [(i, onward(i, hops)) for i in range(count)])

    def facing_side(value):
        return lax.ppermute(value, "dp", [(i, i ^ (2 * RING)) for i in range(count)])

    def other_core(value):
        return lax.ppermute(value, "dp", [(i, i ^ 1) for i in range(count)])

    def merged(mine, theirs):
        axis = mine.ndim - 2
        even = jnp.where(core == 0, mine, theirs)
        odd = jnp.where(core == 0, theirs, mine)
        return jnp.concatenate([even, odd], axis=axis)

    own = merged(codes, other_core(codes))
    part = jnp.where(core == 0, own[0], own[1])
    facing = facing_side(own)
    third = along_ring(own, 3)
    far_part = along_ring(part, RING // 2)
    column = jnp.concatenate([own, facing])
    far_part, third, column, scales, features, timesteps = lax.optimization_barrier(
        (far_part, third, column, scales, features, timesteps)
    )
    first = along_ring(column, 1)
    second = along_ring(column, 2)
    late = facing_side(jnp.concatenate([third, far_part[None]]))
    wide = jnp.repeat(jnp.pad(scales, ((0, 0), (0, 1), (0, 0))), QB, axis=2)
    weights = assembled(
        [(False, 0), (False, 3)],
        False,
        wide,
        [column, third],
        [other_core(third)],
        far_part,
        other_core(far_part),
        None,
    )
    weights = assembled(
        [(False, 1), (False, 2), (True, 3)],
        True,
        wide,
        [first, second, late],
        [other_core(first), other_core(second), other_core(late)],
        None,
        None,
        weights,
    )
    return weights.reshape(-1, channels), features, timesteps


def route(step, sections):
    half = sections // 2
    if step == half - 1:
        return [(s, sections - 1 - s) for s in range(sections)]
    pairs = {s: s ^ 1 for s in range(sections)}
    if step % 2:
        first = step // half * half
        pairs.update({first + k: first + (k + 1) % half for k in range(half)})
    return list(pairs.items())


def shards(features, timesteps, codes, scales, time_weight):
    sections = lax.axis_size("section")
    micros = features.shape[0]
    channels = features.shape[4]
    pixels = SIDE * SIDE
    half = sections // 2
    weights, features, timesteps = gathered_weights(codes[0], scales[0], features, timesteps)
    embedding = jax.nn.silu(sinusoid(timesteps[:, 0], channels)).astype(jnp.bfloat16)
    modulation = jnp.dot(embedding, time_weight[0], preferred_element_type=jnp.float32)
    entering = [features[m].reshape(pixels, channels) for m in range(micros)]
    outs = list(entering)
    skips = None
    for step in range(sections):
        sent = []
        for m in range(micros):
            skip = None if step < half else entering[m] if step == half else skips[m]
            outs[m] = res_block(step, entering[m], skip, modulation[m : m + 1], weights, outs[m])
            if step < sections - 1:
                sent.append(lax.ppermute(outs[m], "section", route(step, sections)))
        if step == half - 1:
            skips = sent
        entering = sent
    return jnp.stack(outs).reshape((1, micros, 1, SIDE, SIDE, channels))


def solution(mesh):
    in_specs = (
        P(None, "dp", None, None, None),
        P(None, "dp"),
        P("section", None, "dp", None),
        P("section", None, None, None),
        P("section", None, None),
    )
    out_specs = P("section", None, "dp", None, None, None)
    return jax.shard_map(shards, mesh=mesh, in_specs=in_specs, out_specs=out_specs, check_vma=False)
```

time: 1650 us -> 89 us (0.05)
  waiting for transfers between devices: 1460 us -> 41.3 us
  matrix products: 45.9 us -> 0.14 us
  local copies, waits for them, and re-layouts: 40.3 us -> 1.29 us
  other arithmetic: 23 us -> 2.48 us
    all_gather x18 -> x0, waiting for transfers between devices: 1320 us -> none  [the longest x9 660 us: conv_second(): lax.all_gather(code_local[1], 'dp', axis=0, tiled=True)]
    ppermute x36 -> x26, waiting for transfers between devices: 139 us -> 41.3 us  [the longest x14 23.6 us: shards(): sent.append(lax.ppermute(outs[m], 'section', route(step, sections)))]
    dot_general x27 -> x1, matrix products: 45.9 us -> 0.14 us  [shards(): jnp.dot(embedding, time_weight[0], preferred_element_type=jnp.float32)]
    ppermute x36 -> x26, starting transfers between devices: 45.8 us -> 38.6 us  [the longest x14 22.7 us: shards(): sent.append(lax.ppermute(outs[m], 'section', route(step, sections)))]
  transfers between devices with their start and end apart: 54 -> 26, of which waited for: 54 -> 17; matrix products, arithmetic and copies ran while one was open for 4% -> 3% of each run, Pallas kernels for 0% -> 2%
where the time goes in v1:
time: 89 us; the launch traced here: 88.5 us
  waiting for transfers between devices  41.3 us (46%)
  starting transfers between devices  38.6 us (43%)
  Pallas kernels  4.49 us (5%)
  other arithmetic  2.48 us (3%)
  local copies, waits for them, and re-layouts  1.29 us (1%)
    ppermute x14, waiting for transfers between devices, shards(): sent.append(lax.ppermute(outs[m], 'section', route(step, sections)))  23.6 us
    ppermute x14, starting transfers between devices, shards(): sent.append(lax.ppermute(outs[m], 'section', route(step, sections)))  22.7 us
    ppermute x4, waiting for transfers between devices, along_ring(): lax.ppermute(value, 'dp', [(i, onward(i, hops)) for i in range(count)])  14.8 us
    ppermute x4, starting transfers between devices, along_ring(): lax.ppermute(value, 'dp', [(i, onward(i, hops)) for i in range(count)])  11.6 us
    ppermute x2, starting transfers between devices, facing_side(): return lax.ppermute(value, 'dp', [(i, i ^ 2 * RING) for i in range(count)])  3.7 us
    pallas_call x16, Pallas kernels, res_block(): pl.pallas_call(functools.partial(block_kernel, step), out_shape=jax.Shape...  3.62 us
    ppermute x6, waiting for transfers between devices, other_core(): return lax.ppermute(value, 'dp', [(i, i ^ 1) for i in range(count)])  2.3 us
  transfers between devices with their start and end apart: 26, of which 17 were waited for; matrix products, arithmetic and copies ran while one was open for 3% of the time, Pallas kernels for 2%

profile of v1, /device:TPU:26, one launch (start us, length us, event | category | flops | bytes accessed | tf_op | source)
XLA Modules:
  0.0 88.5 jit_solution(17322782948046103982)
XLA Ops:
  0.0 1.5 %collective-permute-done = bf16[2,72,256]{2,1,0:T(8,128)(2,1)S(1)} collective-permute-done((bf16[2,72,256]{2,1,0:T(8,128)(2,1)}, bf16[2,72,256]{2,1,0:T(8,128)(2,1)S(1)}, u32[]{:S(2)}, u32[]{:S(2)}) %collective-permute-start) | collective-permute-done | bytes 73760 | tf_op jit(solution)/shard_map/ppermute | solution.py:193
  2.4 2.2 %collective-permute-start.3 = (bf16[2,144,256]{2,1,0:T(8,128)(2,1)S(1)}, bf16[2,144,256]{2,1,0:T(8,128)(2,1)S(1)}, u32[]{:S(2)}, u32[]{:S(2)}) collective-permute-start(bf16[2,144,256]{2,1,0:T(8,128)(2,1)S(1)} %pad_maximum_fusion.3), channel_id=1, source_target_pairs={{0,16},{1,17},{2,18},{3,19},{4,20},{5,21},{6,22},{7,23},{8,24},{9,... | collective-permute-start | bytes 442376 | tf_op jit(solution)/shard_map/ppermute | solution.py:190
  4.6 6.7 %collective-permute-start.2 = (bf16[2,144,256]{2,1,0:T(8,128)(2,1)S(1)}, bf16[2,144,256]{2,1,0:T(8,128)(2,1)S(1)}, u32[]{:S(2)}, u32[]{:S(2)}) collective-permute-start(bf16[2,144,256]{2,1,0:T(8,128)(2,1)S(1)} %pad_maximum_fusion.3), channel_id=1, source_target_pairs={{0,10},{1,7},{2,12},{3,9},{4,14},{5,11},{6,0},{7,13},{8,2},{9,15},... | collective-permute-start | bytes 442376 | tf_op jit(solution)/shard_map/ppermute | solution.py:187
  12.0 10.0 %collective-permute-done.1.half = bf16[144,256]{1,0:T(8,128)(2,1)S(1)} collective-permute-done((bf16[144,256]{1,0:T(8,128)(2,1)S(1)}, bf16[144,256]{1,0:T(8,128)(2,1)S(1)}, u32[]{:S(2)}, u32[]{:S(2)}) %collective-permute-start.1) | collective-permute-done | bytes 73760 | tf_op jit(solution)/shard_map/ppermute | solution.py:187
  22.0 4.4 %collective-permute-start.5 = (bf16[4,144,256]{2,1,0:T(8,128)(2,1)S(1)}, bf16[4,144,256]{2,1,0:T(8,128)(2,1)S(1)}, u32[]{:S(2)}, u32[]{:S(2)}) collective-permute-start(bf16[4,144,256]{2,1,0:T(8,128)(2,1)S(1)} %pad_maximum_fusion.mine_0_), channel_id=1, source_target_pairs={{0,12},{1,5},{2,14},{3,7},{4,0},{5,9},{6,2},{7,11},{8,4},{9,13},{1... | collective-permute-start | bytes 884744 | tf_op jit(solution)/shard_map/ppermute | solution.py:187
  26.9 1.5 %collective-permute-start.6 = (bf16[3,144,256]{2,1,0:T(8,128)(2,1)S(1)}, bf16[3,144,256]{2,1,0:T(8,128)(2,1)S(1)}, u32[]{:S(2)}, u32[]{:S(2)}) collective-permute-start(bf16[3,144,256]{2,1,0:T(8,128)(2,1)S(1)} %pad_maximum_fusion.2), channel_id=1, source_target_pairs={{0,16},{1,17},{2,18},{3,19},{4,20},{5,21},{6,22},{7,23},{8,24},{9,... | collective-permute-start | bytes 663560 | tf_op jit(solution)/shard_map/ppermute | solution.py:190
  30.2 4.8 %collective-permute-done.5.mine_1_ = bf16[4,144,256]{2,1,0:T(8,128)(2,1)S(1)} collective-permute-done((bf16[4,144,256]{2,1,0:T(8,128)(2,1)S(1)}, bf16[4,144,256]{2,1,0:T(8,128)(2,1)S(1)}, u32[]{:S(2)}, u32[]{:S(2)}) %collective-permute-start.5) | collective-permute-done | bytes 294944 | tf_op jit(solution)/shard_map/ppermute | solution.py:187
  38.7 1.3 %collective-permute-start.19 = (bf16[256,256]{1,0:T(8,128)(2,1)S(1)}, bf16[256,256]{1,0:T(8,128)(2,1)S(1)}, u32[]{:S(2)}, u32[]{:S(2)}) collective-permute-start(bf16[256,256]{1,0:T(8,128)(2,1)S(1)} %shard_map.65.old), channel_id=1, source_target_pairs={{0,32},{32,0},{64,96},{96,64},{128,160},{160,128},{192,224},{224,1... | collective-permute-start | bytes 393224 | tf_op jit(solution)/shard_map/ppermute | solution.py:266
  40.0 4.3 %collective-permute-done.12.entering = bf16[256,256]{1,0:T(8,128)(2,1)S(1)} collective-permute-done((bf16[256,256]{1,0:T(8,128)(2,1)S(1)}, bf16[256,256]{1,0:T(8,128)(2,1)S(1)}, u32[]{:S(2)}, u32[]{:S(2)}) %collective-permute-start.12) | collective-permute-done | bytes 131104 | tf_op jit(solution)/shard_map/ppermute | solution.py:266
  45.1 2.1 %collective-permute-done.19.entering = bf16[256,256]{1,0:T(8,128)(2,1)S(1)} collective-permute-done((bf16[256,256]{1,0:T(8,128)(2,1)S(1)}, bf16[256,256]{1,0:T(8,128)(2,1)S(1)}, u32[]{:S(2)}, u32[]{:S(2)}) %collective-permute-start.19) | collective-permute-done | bytes 131104 | tf_op jit(solution)/shard_map/ppermute | solution.py:266
  47.9 2.6 %collective-permute-done.13.entering = bf16[256,256]{1,0:T(8,128)(2,1)S(1)} collective-permute-done((bf16[256,256]{1,0:T(8,128)(2,1)S(1)}, bf16[256,256]{1,0:T(8,128)(2,1)S(1)}, u32[]{:S(2)}, u32[]{:S(2)}) %collective-permute-start.13) | collective-permute-done | bytes 131104 | tf_op jit(solution)/shard_map/ppermute | solution.py:266
  51.2 2.4 %collective-permute-done.20.entering = bf16[256,256]{1,0:T(8,128)(2,1)S(1)} collective-permute-done((bf16[256,256]{1,0:T(8,128)(2,1)S(1)}, bf16[256,256]{1,0:T(8,128)(2,1)S(1)}, u32[]{:S(2)}, u32[]{:S(2)}) %collective-permute-start.20) | collective-permute-done | bytes 131104 | tf_op jit(solution)/shard_map/ppermute | solution.py:266
  54.3 2.0 %collective-permute-done.14.entering = bf16[256,256]{1,0:T(8,128)(2,1)S(1)} collective-permute-done((bf16[256,256]{1,0:T(8,128)(2,1)S(1)}, bf16[256,256]{1,0:T(8,128)(2,1)S(1)}, u32[]{:S(2)}, u32[]{:S(2)}) %collective-permute-start.14) | collective-permute-done | bytes 131104 | tf_op jit(solution)/shard_map/ppermute | solution.py:266
  56.3 4.3 %collective-permute-start.15 = (bf16[256,256]{1,0:T(8,128)(2,1)S(1)}, bf16[256,256]{1,0:T(8,128)(2,1)S(1)}, u32[]{:S(2)}, u32[]{:S(2)}) collective-permute-start(bf16[256,256]{1,0:T(8,128)(2,1)S(1)} %shard_map.60.old), channel_id=1, source_target_pairs={{0,224},{32,192},{64,160},{96,128},{128,96},{160,64},{192,32},{224... | collective-permute-start | bytes 393224 | tf_op jit(solution)/shard_map/ppermute | solution.py:266
  60.6 1.4 %collective-permute-start.22 = (bf16[256,256]{1,0:T(8,128)(2,1)S(1)}, bf16[256,256]{1,0:T(8,128)(2,1)S(1)}, u32[]{:S(2)}, u32[]{:S(2)}) collective-permute-start(bf16[256,256]{1,0:T(8,128)(2,1)S(1)} %shard_map.68.old), channel_id=1, source_target_pairs={{0,224},{32,192},{64,160},{96,128},{128,96},{160,64},{192,32},{224... | collective-permute-start | bytes 393224 | tf_op jit(solution)/shard_map/ppermute | solution.py:266
  62.0 2.1 %collective-permute-done.15.entering.skip = bf16[256,256]{1,0:T(8,128)(2,1)S(1)} collective-permute-done((bf16[256,256]{1,0:T(8,128)(2,1)S(1)}, bf16[256,256]{1,0:T(8,128)(2,1)S(1)}, u32[]{:S(2)}, u32[]{:S(2)}) %collective-permute-start.15) | collective-permute-done | bytes 131104 | tf_op jit(solution)/shard_map/ppermute | solution.py:266
  64.1 3.6 %collective-permute-done.22.entering.skip = bf16[256,256]{1,0:T(8,128)(2,1)S(1)} collective-permute-done((bf16[256,256]{1,0:T(8,128)(2,1)S(1)}, bf16[256,256]{1,0:T(8,128)(2,1)S(1)}, u32[]{:S(2)}, u32[]{:S(2)}) %collective-permute-start.22) | collective-permute-done | bytes 131104 | tf_op jit(solution)/shard_map/ppermute | solution.py:266
  67.7 2.5 %collective-permute-done.16.entering = bf16[256,256]{1,0:T(8,128)(2,1)S(1)} collective-permute-done((bf16[256,256]{1,0:T(8,128)(2,1)S(1)}, bf16[256,256]{1,0:T(8,128)(2,1)S(1)}, u32[]{:S(2)}, u32[]{:S(2)}) %collective-permute-start.16) | collective-permute-done | bytes 131104 | tf_op jit(solution)/shard_map/ppermute | solution.py:266
  70.2 3.1 %collective-permute-start.17 = (bf16[256,256]{1,0:T(8,128)(2,1)S(1)}, bf16[256,256]{1,0:T(8,128)(2,1)S(1)}, u32[]{:S(2)}, u32[]{:S(2)}) collective-permute-start(bf16[256,256]{1,0:T(8,128)(2,1)S(1)} %shard_map.62.old), channel_id=1, source_target_pairs={{0,32},{32,0},{64,96},{96,64},{128,160},{160,192},{192,224},{224,1... | collective-permute-start | bytes 393224 | tf_op jit(solution)/shard_map/ppermute | solution.py:266
  73.8 1.9 %collective-permute-start.24 = (bf16[256,256]{1,0:T(8,128)(2,1)S(1)}, bf16[256,256]{1,0:T(8,128)(2,1)S(1)}, u32[]{:S(2)}, u32[]{:S(2)}) collective-permute-start(bf16[256,256]{1,0:T(8,128)(2,1)S(1)} %shard_map.70.old), channel_id=1, source_target_pairs={{0,32},{32,0},{64,96},{96,64},{128,160},{160,192},{192,224},{224,1... | collective-permute-start | bytes 393224 | tf_op jit(solution)/shard_map/ppermute | solution.py:266
  76.2 4.2 %collective-permute-start.18 = (bf16[256,256]{1,0:T(8,128)(2,1)S(1)}, bf16[256,256]{1,0:T(8,128)(2,1)S(1)}, u32[]{:S(2)}, u32[]{:S(2)}) collective-permute-start(bf16[256,256]{1,0:T(8,128)(2,1)S(1)} %shard_map.63.old), channel_id=1, source_target_pairs={{0,32},{32,0},{64,96},{96,64},{128,160},{160,128},{192,224},{224,1... | collective-permute-start | bytes 393224 | tf_op jit(solution)/shard_map/ppermute | solution.py:266
  80.3 2.7 %collective-permute-start.25 = (bf16[256,256]{1,0:T(8,128)(2,1)S(1)}, bf16[256,256]{1,0:T(8,128)(2,1)S(1)}, u32[]{:S(2)}, u32[]{:S(2)}) collective-permute-start(bf16[256,256]{1,0:T(8,128)(2,1)S(1)} %shard_map.71.old), channel_id=1, source_target_pairs={{0,32},{32,0},{64,96},{96,64},{128,160},{160,128},{192,224},{224,1... | collective-permute-start | bytes 393224 | tf_op jit(solution)/shard_map/ppermute | solution.py:266
  83.6 1.8 %shard_map.64 = bf16[256,256]{1,0:T(8,128)(2,1)S(1)} custom-call(bf16[256,256]{1,0:T(8,128)(2,1)S(1)} %collective-permute-done.18.entering, bf16[256,256]{1,0:T(8,128)(2,1)S(1)} %collective-permute-done.15.entering.skip, f32[1,512]{1,0:T(1,128)S(1)} %get-tuple-element.21.modulation, bf16[4608,256]{1,0:T(8,128)(2,1)S(1)} %bitcast.33, ...), custom_call_target="tpu_custom_call", output_to_operand_aliasing={{}: (4, {})} | custom-call | flops 603979776 | bytes 3000000 | tf_op jit(solution)/shard_map/pallas_call | solution.py:93
  86.0 1.8 %shard_map.72 = bf16[256,256]{1,0:T(8,128)(2,1)S(1)} custom-call(bf16[256,256]{1,0:T(8,128)(2,1)S(1)} %collective-permute-done.25.entering, bf16[256,256]{1,0:T(8,128)(2,1)S(1)} %collective-permute-done.22.entering.skip, f32[1,512]{1,0:T(1,128)S(1)} %get-tuple-element.22.modulation, bf16[4608,256]{1,0:T(8,128)(2,1)S(1)} %bitcast.34, ...), custom_call_target="tpu_custom_call", output_to_operand_aliasing={{}: (4, {})} | custom-call | flops 603979776 | bytes 3000000 | tf_op jit(solution)/shard_map/pallas_call | solution.py:93
  (69 shorter events, 13.3 us)
Async XLA Ops:
  2.4 9.5 %collective-permute-start.3 = (bf16[2,144,256]{2,1,0:T(8,128)(2,1)S(1)}, bf16[2,144,256]{2,1,0:T(8,128)(2,1)S(1)}, u32[]{:S(2)}, u32[]{:S(2)}) collective-permute-start(bf16[2,144,256]{2,1,0:T(8,128)(2,1)S(1)} %pad_maximum_fusion.3), channel_id=1, source_target_pairs={{0,16},{1,17},{2,18},{3,19},{4,20},{5,21},{6,22},{7,23},{8,24},{9,... | collective-permute-start | bytes 442376 | tf_op jit(solution)/shard_map/ppermute | solution.py:190
  4.6 17.4 %collective-permute-start.2 = (bf16[2,144,256]{2,1,0:T(8,128)(2,1)S(1)}, bf16[2,144,256]{2,1,0:T(8,128)(2,1)S(1)}, u32[]{:S(2)}, u32[]{:S(2)}) collective-permute-start(bf16[2,144,256]{2,1,0:T(8,128)(2,1)S(1)} %pad_maximum_fusion.3), channel_id=1, source_target_pairs={{0,10},{1,7},{2,12},{3,9},{4,14},{5,11},{6,0},{7,13},{8,2},{9,15},... | collective-permute-start | bytes 442376 | tf_op jit(solution)/shard_map/ppermute | solution.py:187
  11.4 10.6 %collective-permute-start.1 = (bf16[144,256]{1,0:T(8,128)(2,1)S(1)}, bf16[144,256]{1,0:T(8,128)(2,1)S(1)}, u32[]{:S(2)}, u32[]{:S(2)}) collective-permute-start(bf16[144,256]{1,0:T(8,128)(2,1)S(1)} %fusion.4), channel_id=1, source_target_pairs={{0,8},{1,9},{2,10},{3,11},{4,12},{5,13},{6,14},{7,15},{8,0},{9,1},... | collective-permute-start | bytes 221192 | tf_op jit(solution)/shard_map/ppermute | solution.py:187
  22.0 8.1 %collective-permute-start.4 = (bf16[4,144,256]{2,1,0:T(8,128)(2,1)S(1)}, bf16[4,144,256]{2,1,0:T(8,128)(2,1)S(1)}, u32[]{:S(2)}, u32[]{:S(2)}) collective-permute-start(bf16[4,144,256]{2,1,0:T(8,128)(2,1)S(1)} %pad_maximum_fusion.mine_0_), channel_id=1, source_target_pairs={{0,14},{1,3},{2,0},{3,5},{4,2},{5,7},{6,4},{7,9},{8,6},{9,11},{10,... | collective-permute-start | bytes 884744 | tf_op jit(solution)/shard_map/ppermute | solution.py:187
  22.0 13.1 %collective-permute-start.5 = (bf16[4,144,256]{2,1,0:T(8,128)(2,1)S(1)}, bf16[4,144,256]{2,1,0:T(8,128)(2,1)S(1)}, u32[]{:S(2)}, u32[]{:S(2)}) collective-permute-start(bf16[4,144,256]{2,1,0:T(8,128)(2,1)S(1)} %pad_maximum_fusion.mine_0_), channel_id=1, source_target_pairs={{0,12},{1,5},{2,14},{3,7},{4,0},{5,9},{6,2},{7,11},{8,4},{9,13},{1... | collective-permute-start | bytes 884744 | tf_op jit(solution)/shard_map/ppermute | solution.py:187
  26.3 9.8 %collective-permute-start.10 = (bf16[2,144,256]{2,1,0:T(8,128)(2,1)S(1)}, bf16[2,144,256]{2,1,0:T(8,128)(2,1)S(1)}, u32[]{:S(2)}, u32[]{:S(2)}) collective-permute-start(bf16[2,144,256]{2,1,0:T(8,128)(2,1)S(1)} %collective-permute-done.2.mine_1_), channel_id=1, source_target_pairs={{0,1},{1,0},{2,3},{3,2},{4,5},{5,4},{6,7},{7,6},{8,9},{9,8},{10,11... | collective-permute-start | bytes 442376 | tf_op jit(solution)/shard_map/ppermute | solution.py:193
  26.3 9.8 %collective-permute-start.11 = (bf16[144,256]{1,0:T(8,128)(2,1)S(1)}, bf16[144,256]{1,0:T(8,128)(2,1)S(1)}, u32[]{:S(2)}, u32[]{:S(2)}) collective-permute-start(bf16[144,256]{1,0:T(8,128)(2,1)S(1)} %collective-permute-done.1.half), channel_id=1, source_target_pairs={{0,1},{1,0},{2,3},{3,2},{4,5},{5,4},{6,7},{7,6},{8,9},{9,8},{10,11... | collective-permute-start | bytes 221192 | tf_op jit(solution)/shard_map/ppermute | solution.py:193
  26.9 8.9 %collective-permute-start.6 = (bf16[3,144,256]{2,1,0:T(8,128)(2,1)S(1)}, bf16[3,144,256]{2,1,0:T(8,128)(2,1)S(1)}, u32[]{:S(2)}, u32[]{:S(2)}) collective-permute-start(bf16[3,144,256]{2,1,0:T(8,128)(2,1)S(1)} %pad_maximum_fusion.2), channel_id=1, source_target_pairs={{0,16},{1,17},{2,18},{3,19},{4,20},{5,21},{6,22},{7,23},{8,24},{9,... | collective-permute-start | bytes 663560 | tf_op jit(solution)/shard_map/ppermute | solution.py:190
  30.1 7.1 %collective-permute-start.7 = (bf16[4,144,256]{2,1,0:T(8,128)(2,1)S(1)}, bf16[4,144,256]{2,1,0:T(8,128)(2,1)S(1)}, u32[]{:S(2)}, u32[]{:S(2)}) collective-permute-start(bf16[4,144,256]{2,1,0:T(8,128)(2,1)S(1)} %collective-permute-done.4.mine_0_), channel_id=1, source_target_pairs={{0,1},{1,0},{2,3},{3,2},{4,5},{5,4},{6,7},{7,6},{8,9},{9,8},{10,11... | collective-permute-start | bytes 884744 | tf_op jit(solution)/shard_map/ppermute | solution.py:193
  35.1 2.2 %collective-permute-start.8 = (bf16[4,144,256]{2,1,0:T(8,128)(2,1)S(1)}, bf16[4,144,256]{2,1,0:T(8,128)(2,1)S(1)}, u32[]{:S(2)}, u32[]{:S(2)}) collective-permute-start(bf16[4,144,256]{2,1,0:T(8,128)(2,1)S(1)} %collective-permute-done.5.mine_1_), channel_id=1, source_target_pairs={{0,1},{1,0},{2,3},{3,2},{4,5},{5,4},{6,7},{7,6},{8,9},{9,8},{10,11... | collective-permute-start | bytes 884744 | tf_op jit(solution)/shard_map/ppermute | solution.py:193
  37.9 6.4 %collective-permute-start.12 = (bf16[256,256]{1,0:T(8,128)(2,1)S(1)}, bf16[256,256]{1,0:T(8,128)(2,1)S(1)}, u32[]{:S(2)}, u32[]{:S(2)}) collective-permute-start(bf16[256,256]{1,0:T(8,128)(2,1)S(1)} %shard_map.57.old), channel_id=1, source_target_pairs={{0,32},{32,0},{64,96},{96,64},{128,160},{160,128},{192,224},{224,1... | collective-permute-start | bytes 393224 | tf_op jit(solution)/shard_map/ppermute | solution.py:266
  38.7 8.4 %collective-permute-start.19 = (bf16[256,256]{1,0:T(8,128)(2,1)S(1)}, bf16[256,256]{1,0:T(8,128)(2,1)S(1)}, u32[]{:S(2)}, u32[]{:S(2)}) collective-permute-start(bf16[256,256]{1,0:T(8,128)(2,1)S(1)} %shard_map.65.old), channel_id=1, source_target_pairs={{0,32},{32,0},{64,96},{96,64},{128,160},{160,128},{192,224},{224,1... | collective-permute-start | bytes 393224 | tf_op jit(solution)/shard_map/ppermute | solution.py:266
  44.3 6.1 %collective-permute-start.13 = (bf16[256,256]{1,0:T(8,128)(2,1)S(1)}, bf16[256,256]{1,0:T(8,128)(2,1)S(1)}, u32[]{:S(2)}, u32[]{:S(2)}) collective-permute-start(bf16[256,256]{1,0:T(8,128)(2,1)S(1)} %shard_map.58.old), channel_id=1, source_target_pairs={{0,32},{32,64},{64,96},{96,0},{128,160},{160,128},{192,224},{224,1... | collective-permute-start | bytes 393224 | tf_op jit(solution)/shard_map/ppermute | solution.py:266
  47.1 6.4 %collective-permute-start.20 = (bf16[256,256]{1,0:T(8,128)(2,1)S(1)}, bf16[256,256]{1,0:T(8,128)(2,1)S(1)}, u32[]{:S(2)}, u32[]{:S(2)}) collective-permute-start(bf16[256,256]{1,0:T(8,128)(2,1)S(1)} %shard_map.66.old), channel_id=1, source_target_pairs={{0,32},{32,64},{64,96},{96,0},{128,160},{160,128},{192,224},{224,1... | collective-permute-start | bytes 393224 | tf_op jit(solution)/shard_map/ppermute | solution.py:266
  50.5 5.9 %collective-permute-start.14 = (bf16[256,256]{1,0:T(8,128)(2,1)S(1)}, bf16[256,256]{1,0:T(8,128)(2,1)S(1)}, u32[]{:S(2)}, u32[]{:S(2)}) collective-permute-start(bf16[256,256]{1,0:T(8,128)(2,1)S(1)} %shard_map.59.old), channel_id=1, source_target_pairs={{0,32},{32,0},{64,96},{96,64},{128,160},{160,128},{192,224},{224,1... | collective-permute-start | bytes 393224 | tf_op jit(solution)/shard_map/ppermute | solution.py:266
  53.6 7.0 %collective-permute-start.21 = (bf16[256,256]{1,0:T(8,128)(2,1)S(1)}, bf16[256,256]{1,0:T(8,128)(2,1)S(1)}, u32[]{:S(2)}, u32[]{:S(2)}) collective-permute-start(bf16[256,256]{1,0:T(8,128)(2,1)S(1)} %shard_map.67.old), channel_id=1, source_target_pairs={{0,32},{32,0},{64,96},{96,64},{128,160},{160,128},{192,224},{224,1... | collective-permute-start | bytes 393224 | tf_op jit(solution)/shard_map/ppermute | solution.py:266
  56.3 7.8 %collective-permute-start.15 = (bf16[256,256]{1,0:T(8,128)(2,1)S(1)}, bf16[256,256]{1,0:T(8,128)(2,1)S(1)}, u32[]{:S(2)}, u32[]{:S(2)}) collective-permute-start(bf16[256,256]{1,0:T(8,128)(2,1)S(1)} %shard_map.60.old), channel_id=1, source_target_pairs={{0,224},{32,192},{64,160},{96,128},{128,96},{160,64},{192,32},{224... | collective-permute-start | bytes 393224 | tf_op jit(solution)/shard_map/ppermute | solution.py:266
  60.6 7.1 %collective-permute-start.22 = (bf16[256,256]{1,0:T(8,128)(2,1)S(1)}, bf16[256,256]{1,0:T(8,128)(2,1)S(1)}, u32[]{:S(2)}, u32[]{:S(2)}) collective-permute-start(bf16[256,256]{1,0:T(8,128)(2,1)S(1)} %shard_map.68.old), channel_id=1, source_target_pairs={{0,224},{32,192},{64,160},{96,128},{128,96},{160,64},{192,32},{224... | collective-permute-start | bytes 393224 | tf_op jit(solution)/shard_map/ppermute | solution.py:266
  64.1 6.1 %collective-permute-start.16 = (bf16[256,256]{1,0:T(8,128)(2,1)S(1)}, bf16[256,256]{1,0:T(8,128)(2,1)S(1)}, u32[]{:S(2)}, u32[]{:S(2)}) collective-permute-start(bf16[256,256]{1,0:T(8,128)(2,1)S(1)} %shard_map.61.old), channel_id=1, source_target_pairs={{0,32},{32,0},{64,96},{96,64},{128,160},{160,128},{192,224},{224,1... | collective-permute-start | bytes 393224 | tf_op jit(solution)/shard_map/ppermute | solution.py:266
  67.7 6.2 %collective-permute-start.23 = (bf16[256,256]{1,0:T(8,128)(2,1)S(1)}, bf16[256,256]{1,0:T(8,128)(2,1)S(1)}, u32[]{:S(2)}, u32[]{:S(2)}) collective-permute-start(bf16[256,256]{1,0:T(8,128)(2,1)S(1)} %shard_map.69.old), channel_id=1, source_target_pairs={{0,32},{32,0},{64,96},{96,64},{128,160},{160,128},{192,224},{224,1... | collective-permute-start | bytes 393224 | tf_op jit(solution)/shard_map/ppermute | solution.py:266
  70.2 6.0 %collective-permute-start.17 = (bf16[256,256]{1,0:T(8,128)(2,1)S(1)}, bf16[256,256]{1,0:T(8,128)(2,1)S(1)}, u32[]{:S(2)}, u32[]{:S(2)}) collective-permute-start(bf16[256,256]{1,0:T(8,128)(2,1)S(1)} %shard_map.62.old), channel_id=1, source_target_pairs={{0,32},{32,0},{64,96},{96,64},{128,160},{160,192},{192,224},{224,1... | collective-permute-start | bytes 393224 | tf_op jit(solution)/shard_map/ppermute | solution.py:266
  73.8 6.5 %collective-permute-start.24 = (bf16[256,256]{1,0:T(8,128)(2,1)S(1)}, bf16[256,256]{1,0:T(8,128)(2,1)S(1)}, u32[]{:S(2)}, u32[]{:S(2)}) collective-permute-start(bf16[256,256]{1,0:T(8,128)(2,1)S(1)} %shard_map.70.old), channel_id=1, source_target_pairs={{0,32},{32,0},{64,96},{96,64},{128,160},{160,192},{192,224},{224,1... | collective-permute-start | bytes 393224 | tf_op jit(solution)/shard_map/ppermute | solution.py:266
  76.2 7.4 %collective-permute-start.18 = (bf16[256,256]{1,0:T(8,128)(2,1)S(1)}, bf16[256,256]{1,0:T(8,128)(2,1)S(1)}, u32[]{:S(2)}, u32[]{:S(2)}) collective-permute-start(bf16[256,256]{1,0:T(8,128)(2,1)S(1)} %shard_map.63.old), channel_id=1, source_target_pairs={{0,32},{32,0},{64,96},{96,64},{128,160},{160,128},{192,224},{224,1... | collective-permute-start | bytes 393224 | tf_op jit(solution)/shard_map/ppermute | solution.py:266
  80.3 5.7 %collective-permute-start.25 = (bf16[256,256]{1,0:T(8,128)(2,1)S(1)}, bf16[256,256]{1,0:T(8,128)(2,1)S(1)}, u32[]{:S(2)}, u32[]{:S(2)}) collective-permute-start(bf16[256,256]{1,0:T(8,128)(2,1)S(1)} %shard_map.71.old), channel_id=1, source_target_pairs={{0,32},{32,0},{64,96},{96,64},{128,160},{160,128},{192,224},{224,1... | collective-permute-start | bytes 393224 | tf_op jit(solution)/shard_map/ppermute | solution.py:266
  (4 other events, 73.8 us)

commit v2 on v1

--- a/solution.py
+++ b/solution.py
@@ -24,20 +24,26 @@
 
 def normalize(values):
     pixels, channels = values.shape
-    mean = jnp.sum(values, axis=0, keepdims=True) * (1.0 / pixels)
-    spread = values - mean
-    square = jnp.sum(spread * spread, axis=0, keepdims=True)
-    upper = lax.broadcasted_iota(jnp.int32, (8, channels), 0) < 4
-    both = jnp.where(upper, mean, square)
-    count = pixels
-    for bit in (1, 2, 4):
-        halves = [across_lanes(both[:, k : k + 128], bit) for k in range(0, channels, 128)]
-        partner = jnp.concatenate(halves, axis=1)
-        apart = both - partner
-        between = pltpu.roll(apart * apart, 4, 0) * (0.5 * count)
-        both = jnp.where(upper, 0.5 * (both + partner), both + partner + between)
-        count = 2 * count
-    return values - both[0:1], lax.rsqrt(both[4:5] * (1.0 / count) + 1e-05)
+    origin = values[0:1]
+    moved = values - origin
+    total = jnp.sum(moved, axis=0, keepdims=True) * (1.0 / pixels)
+    square = jnp.sum(moved * moved, axis=0, keepdims=True) - total * total * pixels
+    means = []
+    squares = []
+    for k in range(0, channels, 128):
+        mean = jnp.broadcast_to((origin + total)[:, k : k + 128], (8, 128))
+        spread = jnp.broadcast_to(square[:, k : k + 128], (8, 128))
+        count = pixels
+        for bit in (1, 2, 4):
+            other = across_lanes(mean, bit)
+            apart = mean - other
+            spread = spread + across_lanes(spread, bit) + apart * apart * (0.5 * count)
+            mean = 0.5 * (mean + other)
+            count = 2 * count
+        means.append(mean[0:1])
+        squares.append(spread[0:1])
+    variance = jnp.maximum(jnp.concatenate(squares, axis=1) * (1.0 / count), 0.0)
+    return values - jnp.concatenate(means, axis=1), lax.rsqrt(variance + 1e-05)
 
 
 def silu(values):
@@ -202,31 +208,32 @@
     part = jnp.where(core == 0, own[0], own[1])
     facing = facing_side(own)
     third = along_ring(own, 3)
+    second = along_ring(own, 2)
     far_part = along_ring(part, RING // 2)
     column = jnp.concatenate([own, facing])
-    far_part, third, column, scales, features, timesteps = lax.optimization_barrier(
-        (far_part, third, column, scales, features, timesteps)
+    far_part, third, second, column, scales, features, timesteps = lax.optimization_barrier(
+        (far_part, third, second, column, scales, features, timesteps)
     )
     first = along_ring(column, 1)
-    second = along_ring(column, 2)
+    facing_second = along_ring(column[convs:], 2)
     late = facing_side(jnp.concatenate([third, far_part[None]]))
     wide = jnp.repeat(jnp.pad(scales, ((0, 0), (0, 1), (0, 0))), QB, axis=2)
     weights = assembled(
-        [(False, 0), (False, 3)],
+        [(False, 0), (False, 2), (False, 3)],
         False,
         wide,
-        [column, third],
-        [other_core(third)],
+        [column, second, third],
+        [other_core(second), other_core(third)],
         far_part,
         other_core(far_part),
         None,
     )
     weights = assembled(
-        [(False, 1), (False, 2), (True, 3)],
+        [(False, 1), (True, 2), (True, 3)],
         True,
         wide,
-        [first, second, late],
-        [other_core(first), other_core(second), other_core(late)],
+        [first, facing_second, late],
+        [other_core(first), other_core(facing_second), other_core(late)],
         None,
         None,
         weights,

time: 89 us -> 88 us (0.989)
  starting transfers between devices: 38.6 us -> 44.1 us
  waiting for transfers between devices: 41.3 us -> 35.9 us
  local copies, waits for them, and re-layouts: 1.29 us -> 0.34 us
    ppermute x4 -> x5, waiting for transfers between devices: 14.8 us -> 9.49 us  [along_ring(): lax.ppermute(value, 'dp', [(i, onward(i, hops)) for i in range(count)])]
    ppermute x4 -> x5, starting transfers between devices: 11.6 us -> 16.7 us  [along_ring(): lax.ppermute(value, 'dp', [(i, onward(i, hops)) for i in range(count)])]
    slice x1, local copies, waits for them, and re-layouts: 0.99 us -> 0.02 us  [shards(): entering = [features[m].reshape(pixels, channels) for m in range(micros)]]
    ppermute x6 -> x7, starting transfers between devices: 0.61 us -> 1.57 us  [other_core(): return lax.ppermute(value, 'dp', [(i, i ^ 1) for i in range(count)])]
    ppermute x6 -> x7, waiting for transfers between devices: 2.3 us -> 2.33 us  [other_core(): return lax.ppermute(value, 'dp', [(i, i ^ 1) for i in range(count)])]
  transfers between devices with their start and end apart: 26 -> 28, of which waited for: 17 -> 18; matrix products, arithmetic and copies ran while one was open for 3% -> 1% of each run, Pallas kernels for 2% -> 2%
where the time goes in v2:
time: 88 us; the launch traced here: 87.5 us
  starting transfers between devices  44.1 us (50%)
  waiting for transfers between devices  35.9 us (41%)
  Pallas kernels  4.34 us (5%)
  other arithmetic  2.48 us (3%)
    ppermute x14, waiting for transfers between devices, shards(): sent.append(lax.ppermute(outs[m], 'section', route(step, sections)))  23.8 us
    ppermute x14, starting transfers between devices, shards(): sent.append(lax.ppermute(outs[m], 'section', route(step, sections)))  22.1 us
    ppermute x5, starting transfers between devices, along_ring(): lax.ppermute(value, 'dp', [(i, onward(i, hops)) for i in range(count)])  16.7 us
    ppermute x5, waiting for transfers between devices, along_ring(): lax.ppermute(value, 'dp', [(i, onward(i, hops)) for i in range(count)])  9.49 us
    ppermute x2, starting transfers between devices, facing_side(): return lax.ppermute(value, 'dp', [(i, i ^ 2 * RING) for i in range(count)])  3.7 us
    pallas_call x16, Pallas kernels, res_block(): pl.pallas_call(functools.partial(block_kernel, step), out_shape=jax.Shape...  3.48 us
    ppermute x7, waiting for transfers between devices, other_core(): return lax.ppermute(value, 'dp', [(i, i ^ 1) for i in range(count)])  2.33 us
  transfers between devices with their start and end apart: 28, of which 18 were waited for; matrix products, arithmetic and copies ran while one was open for 1% of the time, Pallas kernels for 2%

profile of v2, /device:TPU:26, one launch (start us, length us, event | category | flops | bytes accessed | tf_op | source)
XLA Modules:
  0.0 87.5 jit_solution(17584945924691007702)
XLA Ops:
  0.1 1.5 %collective-permute-done = bf16[2,72,256]{2,1,0:T(8,128)(2,1)S(1)} collective-permute-done((bf16[2,72,256]{2,1,0:T(8,128)(2,1)}, bf16[2,72,256]{2,1,0:T(8,128)(2,1)S(1)}, u32[]{:S(2)}, u32[]{:S(2)}) %collective-permute-start) | collective-permute-done | bytes 73760 | tf_op jit(solution)/shard_map/ppermute | solution.py:199
  2.5 2.2 %collective-permute-start.4 = (bf16[2,144,256]{2,1,0:T(8,128)(2,1)S(1)}, bf16[2,144,256]{2,1,0:T(8,128)(2,1)S(1)}, u32[]{:S(2)}, u32[]{:S(2)}) collective-permute-start(bf16[2,144,256]{2,1,0:T(8,128)(2,1)S(1)} %pad_maximum_fusion.3), channel_id=1, source_target_pairs={{0,16},{1,17},{2,18},{3,19},{4,20},{5,21},{6,22},{7,23},{8,24},{9,... | collective-permute-start | bytes 442376 | tf_op jit(solution)/shard_map/ppermute | solution.py:196
  4.7 6.7 %collective-permute-start.2 = (bf16[2,144,256]{2,1,0:T(8,128)(2,1)S(1)}, bf16[2,144,256]{2,1,0:T(8,128)(2,1)S(1)}, u32[]{:S(2)}, u32[]{:S(2)}) collective-permute-start(bf16[2,144,256]{2,1,0:T(8,128)(2,1)S(1)} %pad_maximum_fusion.3), channel_id=1, source_target_pairs={{0,10},{1,7},{2,12},{3,9},{4,14},{5,11},{6,0},{7,13},{8,2},{9,15},... | collective-permute-start | bytes 442376 | tf_op jit(solution)/shard_map/ppermute | solution.py:193
  12.0 4.6 %collective-permute-start.1 = (bf16[144,256]{1,0:T(8,128)(2,1)S(1)}, bf16[144,256]{1,0:T(8,128)(2,1)S(1)}, u32[]{:S(2)}, u32[]{:S(2)}) collective-permute-start(bf16[144,256]{1,0:T(8,128)(2,1)S(1)} %fusion.4), channel_id=1, source_target_pairs={{0,8},{1,9},{2,10},{3,11},{4,12},{5,13},{6,14},{7,15},{8,0},{9,1},... | collective-permute-start | bytes 221192 | tf_op jit(solution)/shard_map/ppermute | solution.py:193
  16.6 7.1 %collective-permute-done.1.half = bf16[144,256]{1,0:T(8,128)(2,1)S(1)} collective-permute-done((bf16[144,256]{1,0:T(8,128)(2,1)S(1)}, bf16[144,256]{1,0:T(8,128)(2,1)S(1)}, u32[]{:S(2)}, u32[]{:S(2)}) %collective-permute-start.1) | collective-permute-done | bytes 73760 | tf_op jit(solution)/shard_map/ppermute | solution.py:193
  23.8 2.0 %collective-permute-start.5 = (bf16[4,144,256]{2,1,0:T(8,128)(2,1)S(1)}, bf16[4,144,256]{2,1,0:T(8,128)(2,1)S(1)}, u32[]{:S(2)}, u32[]{:S(2)}) collective-permute-start(bf16[4,144,256]{2,1,0:T(8,128)(2,1)S(1)} %pad_maximum_fusion.mine_0_), channel_id=1, source_target_pairs={{0,14},{1,3},{2,0},{3,5},{4,2},{5,7},{6,4},{7,9},{8,6},{9,11},{10,... | collective-permute-start | bytes 884744 | tf_op jit(solution)/shard_map/ppermute | solution.py:193
  26.4 1.5 %collective-permute-start.7 = (bf16[3,144,256]{2,1,0:T(8,128)(2,1)S(1)}, bf16[3,144,256]{2,1,0:T(8,128)(2,1)S(1)}, u32[]{:S(2)}, u32[]{:S(2)}) collective-permute-start(bf16[3,144,256]{2,1,0:T(8,128)(2,1)S(1)} %pad_maximum_fusion.2), channel_id=1, source_target_pairs={{0,16},{1,17},{2,18},{3,19},{4,20},{5,21},{6,22},{7,23},{8,24},{9,... | collective-permute-start | bytes 663560 | tf_op jit(solution)/shard_map/ppermute | solution.py:196
  27.8 2.9 %collective-permute-start.6 = (bf16[2,144,256]{2,1,0:T(8,128)(2,1)S(1)}, bf16[2,144,256]{2,1,0:T(8,128)(2,1)S(1)}, u32[]{:S(2)}, u32[]{:S(2)}) collective-permute-start(bf16[2,144,256]{2,1,0:T(8,128)(2,1)S(1)} %slice.18), channel_id=1, source_target_pairs={{0,12},{1,5},{2,14},{3,7},{4,0},{5,9},{6,2},{7,11},{8,4},{9,13},{1... | collective-permute-start | bytes 442376 | tf_op jit(solution)/shard_map/ppermute | solution.py:193
  32.7 2.4 %collective-permute-done.6.mine_1_ = bf16[2,144,256]{2,1,0:T(8,128)(2,1)S(1)} collective-permute-done((bf16[2,144,256]{2,1,0:T(8,128)(2,1)S(1)}, bf16[2,144,256]{2,1,0:T(8,128)(2,1)S(1)}, u32[]{:S(2)}, u32[]{:S(2)}) %collective-permute-start.6) | collective-permute-done | bytes 147488 | tf_op jit(solution)/shard_map/ppermute | solution.py:193
  39.5 4.3 %collective-permute-done.14.entering = bf16[256,256]{1,0:T(8,128)(2,1)S(1)} collective-permute-done((bf16[256,256]{1,0:T(8,128)(2,1)S(1)}, bf16[256,256]{1,0:T(8,128)(2,1)S(1)}, u32[]{:S(2)}, u32[]{:S(2)}) %collective-permute-start.14) | collective-permute-done | bytes 131104 | tf_op jit(solution)/shard_map/ppermute | solution.py:273
  44.5 2.1 %collective-permute-done.21.entering = bf16[256,256]{1,0:T(8,128)(2,1)S(1)} collective-permute-done((bf16[256,256]{1,0:T(8,128)(2,1)S(1)}, bf16[256,256]{1,0:T(8,128)(2,1)S(1)}, u32[]{:S(2)}, u32[]{:S(2)}) %collective-permute-start.21) | collective-permute-done | bytes 131104 | tf_op jit(solution)/shard_map/ppermute | solution.py:273
  47.3 2.4 %collective-permute-done.15.entering = bf16[256,256]{1,0:T(8,128)(2,1)S(1)} collective-permute-done((bf16[256,256]{1,0:T(8,128)(2,1)S(1)}, bf16[256,256]{1,0:T(8,128)(2,1)S(1)}, u32[]{:S(2)}, u32[]{:S(2)}) %collective-permute-start.15) | collective-permute-done | bytes 131104 | tf_op jit(solution)/shard_map/ppermute | solution.py:273
  50.5 2.6 %collective-permute-done.22.entering = bf16[256,256]{1,0:T(8,128)(2,1)S(1)} collective-permute-done((bf16[256,256]{1,0:T(8,128)(2,1)S(1)}, bf16[256,256]{1,0:T(8,128)(2,1)S(1)}, u32[]{:S(2)}, u32[]{:S(2)}) %collective-permute-start.22) | collective-permute-done | bytes 131104 | tf_op jit(solution)/shard_map/ppermute | solution.py:273
  53.8 2.0 %collective-permute-done.16.entering = bf16[256,256]{1,0:T(8,128)(2,1)S(1)} collective-permute-done((bf16[256,256]{1,0:T(8,128)(2,1)S(1)}, bf16[256,256]{1,0:T(8,128)(2,1)S(1)}, u32[]{:S(2)}, u32[]{:S(2)}) %collective-permute-start.16) | collective-permute-done | bytes 131104 | tf_op jit(solution)/shard_map/ppermute | solution.py:273
  55.8 4.2 %collective-permute-start.17 = (bf16[256,256]{1,0:T(8,128)(2,1)S(1)}, bf16[256,256]{1,0:T(8,128)(2,1)S(1)}, u32[]{:S(2)}, u32[]{:S(2)}) collective-permute-start(bf16[256,256]{1,0:T(8,128)(2,1)S(1)} %shard_map.60.old), channel_id=1, source_target_pairs={{0,224},{32,192},{64,160},{96,128},{128,96},{160,64},{192,32},{224... | collective-permute-start | bytes 393224 | tf_op jit(solution)/shard_map/ppermute | solution.py:273
  61.4 2.2 %collective-permute-done.17.entering.skip = bf16[256,256]{1,0:T(8,128)(2,1)S(1)} collective-permute-done((bf16[256,256]{1,0:T(8,128)(2,1)S(1)}, bf16[256,256]{1,0:T(8,128)(2,1)S(1)}, u32[]{:S(2)}, u32[]{:S(2)}) %collective-permute-start.17) | collective-permute-done | bytes 131104 | tf_op jit(solution)/shard_map/ppermute | solution.py:273
  63.6 3.5 %collective-permute-done.24.entering.skip = bf16[256,256]{1,0:T(8,128)(2,1)S(1)} collective-permute-done((bf16[256,256]{1,0:T(8,128)(2,1)S(1)}, bf16[256,256]{1,0:T(8,128)(2,1)S(1)}, u32[]{:S(2)}, u32[]{:S(2)}) %collective-permute-start.24) | collective-permute-done | bytes 131104 | tf_op jit(solution)/shard_map/ppermute | solution.py:273
  67.1 2.7 %collective-permute-done.18.entering = bf16[256,256]{1,0:T(8,128)(2,1)S(1)} collective-permute-done((bf16[256,256]{1,0:T(8,128)(2,1)S(1)}, bf16[256,256]{1,0:T(8,128)(2,1)S(1)}, u32[]{:S(2)}, u32[]{:S(2)}) %collective-permute-start.18) | collective-permute-done | bytes 131104 | tf_op jit(solution)/shard_map/ppermute | solution.py:273
  69.8 2.7 %collective-permute-start.19 = (bf16[256,256]{1,0:T(8,128)(2,1)S(1)}, bf16[256,256]{1,0:T(8,128)(2,1)S(1)}, u32[]{:S(2)}, u32[]{:S(2)}) collective-permute-start(bf16[256,256]{1,0:T(8,128)(2,1)S(1)} %shard_map.62.old), channel_id=1, source_target_pairs={{0,32},{32,0},{64,96},{96,64},{128,160},{160,192},{192,224},{224,1... | collective-permute-start | bytes 393224 | tf_op jit(solution)/shard_map/ppermute | solution.py:273
  73.2 1.7 %collective-permute-start.26 = (bf16[256,256]{1,0:T(8,128)(2,1)S(1)}, bf16[256,256]{1,0:T(8,128)(2,1)S(1)}, u32[]{:S(2)}, u32[]{:S(2)}) collective-permute-start(bf16[256,256]{1,0:T(8,128)(2,1)S(1)} %shard_map.70.old), channel_id=1, source_target_pairs={{0,32},{32,0},{64,96},{96,64},{128,160},{160,192},{192,224},{224,1... | collective-permute-start | bytes 393224 | tf_op jit(solution)/shard_map/ppermute | solution.py:273
  75.0 4.2 %collective-permute-start.20 = (bf16[256,256]{1,0:T(8,128)(2,1)S(1)}, bf16[256,256]{1,0:T(8,128)(2,1)S(1)}, u32[]{:S(2)}, u32[]{:S(2)}) collective-permute-start(bf16[256,256]{1,0:T(8,128)(2,1)S(1)} %shard_map.63.old), channel_id=1, source_target_pairs={{0,32},{32,0},{64,96},{96,64},{128,160},{160,128},{192,224},{224,1... | collective-permute-start | bytes 393224 | tf_op jit(solution)/shard_map/ppermute | solution.py:273
  79.2 2.8 %collective-permute-start.27 = (bf16[256,256]{1,0:T(8,128)(2,1)S(1)}, bf16[256,256]{1,0:T(8,128)(2,1)S(1)}, u32[]{:S(2)}, u32[]{:S(2)}) collective-permute-start(bf16[256,256]{1,0:T(8,128)(2,1)S(1)} %shard_map.71.old), channel_id=1, source_target_pairs={{0,32},{32,0},{64,96},{96,64},{128,160},{160,128},{192,224},{224,1... | collective-permute-start | bytes 393224 | tf_op jit(solution)/shard_map/ppermute | solution.py:273
  82.2 1.7 %shard_map.64 = bf16[256,256]{1,0:T(8,128)(2,1)S(1)} custom-call(bf16[256,256]{1,0:T(8,128)(2,1)S(1)} %collective-permute-done.20.entering, bf16[256,256]{1,0:T(8,128)(2,1)S(1)} %collective-permute-done.17.entering.skip, f32[1,512]{1,0:T(1,128)S(1)} %get-tuple-element.23.modulation, bf16[4608,256]{1,0:T(8,128)(2,1)S(1)} %bitcast.33, ...), custom_call_target="tpu_custom_call", output_to_operand_aliasing={{}: (4, {})} | custom-call | flops 603979776 | bytes 3000000 | tf_op jit(solution)/shard_map/pallas_call | solution.py:99
  85.0 1.7 %shard_map.72 = bf16[256,256]{1,0:T(8,128)(2,1)S(1)} custom-call(bf16[256,256]{1,0:T(8,128)(2,1)S(1)} %collective-permute-done.27.entering, bf16[256,256]{1,0:T(8,128)(2,1)S(1)} %collective-permute-done.24.entering.skip, f32[1,512]{1,0:T(1,128)S(1)} %get-tuple-element.24.modulation, bf16[4608,256]{1,0:T(8,128)(2,1)S(1)} %bitcast.34, ...), custom_call_target="tpu_custom_call", output_to_operand_aliasing={{}: (4, {})} | custom-call | flops 603979776 | bytes 3000000 | tf_op jit(solution)/shard_map/pallas_call | solution.py:99
  (76 shorter events, 15.7 us)
Async XLA Ops:
  2.5 14.1 %collective-permute-start.4 = (bf16[2,144,256]{2,1,0:T(8,128)(2,1)S(1)}, bf16[2,144,256]{2,1,0:T(8,128)(2,1)S(1)}, u32[]{:S(2)}, u32[]{:S(2)}) collective-permute-start(bf16[2,144,256]{2,1,0:T(8,128)(2,1)S(1)} %pad_maximum_fusion.3), channel_id=1, source_target_pairs={{0,16},{1,17},{2,18},{3,19},{4,20},{5,21},{6,22},{7,23},{8,24},{9,... | collective-permute-start | bytes 442376 | tf_op jit(solution)/shard_map/ppermute | solution.py:196
  4.7 19.0 %collective-permute-start.2 = (bf16[2,144,256]{2,1,0:T(8,128)(2,1)S(1)}, bf16[2,144,256]{2,1,0:T(8,128)(2,1)S(1)}, u32[]{:S(2)}, u32[]{:S(2)}) collective-permute-start(bf16[2,144,256]{2,1,0:T(8,128)(2,1)S(1)} %pad_maximum_fusion.3), channel_id=1, source_target_pairs={{0,10},{1,7},{2,12},{3,9},{4,14},{5,11},{6,0},{7,13},{8,2},{9,15},... | collective-permute-start | bytes 442376 | tf_op jit(solution)/shard_map/ppermute | solution.py:193
  11.5 12.3 %collective-permute-start.3 = (bf16[2,144,256]{2,1,0:T(8,128)(2,1)S(1)}, bf16[2,144,256]{2,1,0:T(8,128)(2,1)S(1)}, u32[]{:S(2)}, u32[]{:S(2)}) collective-permute-start(bf16[2,144,256]{2,1,0:T(8,128)(2,1)S(1)} %pad_maximum_fusion.3), channel_id=1, source_target_pairs={{0,12},{1,5},{2,14},{3,7},{4,0},{5,9},{6,2},{7,11},{8,4},{9,13},{1... | collective-permute-start | bytes 442376 | tf_op jit(solution)/shard_map/ppermute | solution.py:193
  12.0 11.7 %collective-permute-start.1 = (bf16[144,256]{1,0:T(8,128)(2,1)S(1)}, bf16[144,256]{1,0:T(8,128)(2,1)S(1)}, u32[]{:S(2)}, u32[]{:S(2)}) collective-permute-start(bf16[144,256]{1,0:T(8,128)(2,1)S(1)} %fusion.4), channel_id=1, source_target_pairs={{0,8},{1,9},{2,10},{3,11},{4,12},{5,13},{6,14},{7,15},{8,0},{9,1},... | collective-permute-start | bytes 221192 | tf_op jit(solution)/shard_map/ppermute | solution.py:193
  23.8 7.8 %collective-permute-start.5 = (bf16[4,144,256]{2,1,0:T(8,128)(2,1)S(1)}, bf16[4,144,256]{2,1,0:T(8,128)(2,1)S(1)}, u32[]{:S(2)}, u32[]{:S(2)}) collective-permute-start(bf16[4,144,256]{2,1,0:T(8,128)(2,1)S(1)} %pad_maximum_fusion.mine_0_), channel_id=1, source_target_pairs={{0,14},{1,3},{2,0},{3,5},{4,2},{5,7},{6,4},{7,9},{8,6},{9,11},{10,... | collective-permute-start | bytes 884744 | tf_op jit(solution)/shard_map/ppermute | solution.py:193
  25.7 9.9 %collective-permute-start.12 = (bf16[2,144,256]{2,1,0:T(8,128)(2,1)S(1)}, bf16[2,144,256]{2,1,0:T(8,128)(2,1)S(1)}, u32[]{:S(2)}, u32[]{:S(2)}) collective-permute-start(bf16[2,144,256]{2,1,0:T(8,128)(2,1)S(1)} %collective-permute-done.2.mine_2_), channel_id=1, source_target_pairs={{0,1},{1,0},{2,3},{3,2},{4,5},{5,4},{6,7},{7,6},{8,9},{9,8},{10,11... | collective-permute-start | bytes 442376 | tf_op jit(solution)/shard_map/ppermute | solution.py:199
  25.8 6.3 %collective-permute-start.13 = (bf16[144,256]{1,0:T(8,128)(2,1)S(1)}, bf16[144,256]{1,0:T(8,128)(2,1)S(1)}, u32[]{:S(2)}, u32[]{:S(2)}) collective-permute-start(bf16[144,256]{1,0:T(8,128)(2,1)S(1)} %collective-permute-done.1.half), channel_id=1, source_target_pairs={{0,1},{1,0},{2,3},{3,2},{4,5},{5,4},{6,7},{7,6},{8,9},{9,8},{10,11... | collective-permute-start | bytes 221192 | tf_op jit(solution)/shard_map/ppermute | solution.py:199
  26.4 9.0 %collective-permute-start.7 = (bf16[3,144,256]{2,1,0:T(8,128)(2,1)S(1)}, bf16[3,144,256]{2,1,0:T(8,128)(2,1)S(1)}, u32[]{:S(2)}, u32[]{:S(2)}) collective-permute-start(bf16[3,144,256]{2,1,0:T(8,128)(2,1)S(1)} %pad_maximum_fusion.2), channel_id=1, source_target_pairs={{0,16},{1,17},{2,18},{3,19},{4,20},{5,21},{6,22},{7,23},{8,24},{9,... | collective-permute-start | bytes 663560 | tf_op jit(solution)/shard_map/ppermute | solution.py:196
  27.8 7.2 %collective-permute-start.6 = (bf16[2,144,256]{2,1,0:T(8,128)(2,1)S(1)}, bf16[2,144,256]{2,1,0:T(8,128)(2,1)S(1)}, u32[]{:S(2)}, u32[]{:S(2)}) collective-permute-start(bf16[2,144,256]{2,1,0:T(8,128)(2,1)S(1)} %slice.18), channel_id=1, source_target_pairs={{0,12},{1,5},{2,14},{3,7},{4,0},{5,9},{6,2},{7,11},{8,4},{9,13},{1... | collective-permute-start | bytes 442376 | tf_op jit(solution)/shard_map/ppermute | solution.py:193
  31.5 5.3 %collective-permute-start.8 = (bf16[4,144,256]{2,1,0:T(8,128)(2,1)S(1)}, bf16[4,144,256]{2,1,0:T(8,128)(2,1)S(1)}, u32[]{:S(2)}, u32[]{:S(2)}) collective-permute-start(bf16[4,144,256]{2,1,0:T(8,128)(2,1)S(1)} %collective-permute-done.5.mine_0_), channel_id=1, source_target_pairs={{0,1},{1,0},{2,3},{3,2},{4,5},{5,4},{6,7},{7,6},{8,9},{9,8},{10,11... | collective-permute-start | bytes 884744 | tf_op jit(solution)/shard_map/ppermute | solution.py:199
  37.4 6.4 %collective-permute-start.14 = (bf16[256,256]{1,0:T(8,128)(2,1)S(1)}, bf16[256,256]{1,0:T(8,128)(2,1)S(1)}, u32[]{:S(2)}, u32[]{:S(2)}) collective-permute-start(bf16[256,256]{1,0:T(8,128)(2,1)S(1)} %shard_map.57.old), channel_id=1, source_target_pairs={{0,32},{32,0},{64,96},{96,64},{128,160},{160,128},{192,224},{224,1... | collective-permute-start | bytes 393224 | tf_op jit(solution)/shard_map/ppermute | solution.py:273
  38.2 8.4 %collective-permute-start.21 = (bf16[256,256]{1,0:T(8,128)(2,1)S(1)}, bf16[256,256]{1,0:T(8,128)(2,1)S(1)}, u32[]{:S(2)}, u32[]{:S(2)}) collective-permute-start(bf16[256,256]{1,0:T(8,128)(2,1)S(1)} %shard_map.65.old), channel_id=1, source_target_pairs={{0,32},{32,0},{64,96},{96,64},{128,160},{160,128},{192,224},{224,1... | collective-permute-start | bytes 393224 | tf_op jit(solution)/shard_map/ppermute | solution.py:273
  43.8 5.9 %collective-permute-start.15 = (bf16[256,256]{1,0:T(8,128)(2,1)S(1)}, bf16[256,256]{1,0:T(8,128)(2,1)S(1)}, u32[]{:S(2)}, u32[]{:S(2)}) collective-permute-start(bf16[256,256]{1,0:T(8,128)(2,1)S(1)} %shard_map.58.old), channel_id=1, source_target_pairs={{0,32},{32,64},{64,96},{96,0},{128,160},{160,128},{192,224},{224,1... | collective-permute-start | bytes 393224 | tf_op jit(solution)/shard_map/ppermute | solution.py:273
  46.6 6.4 %collective-permute-start.22 = (bf16[256,256]{1,0:T(8,128)(2,1)S(1)}, bf16[256,256]{1,0:T(8,128)(2,1)S(1)}, u32[]{:S(2)}, u32[]{:S(2)}) collective-permute-start(bf16[256,256]{1,0:T(8,128)(2,1)S(1)} %shard_map.66.old), channel_id=1, source_target_pairs={{0,32},{32,64},{64,96},{96,0},{128,160},{160,128},{192,224},{224,1... | collective-permute-start | bytes 393224 | tf_op jit(solution)/shard_map/ppermute | solution.py:273
  49.7 6.1 %collective-permute-start.16 = (bf16[256,256]{1,0:T(8,128)(2,1)S(1)}, bf16[256,256]{1,0:T(8,128)(2,1)S(1)}, u32[]{:S(2)}, u32[]{:S(2)}) collective-permute-start(bf16[256,256]{1,0:T(8,128)(2,1)S(1)} %shard_map.59.old), channel_id=1, source_target_pairs={{0,32},{32,0},{64,96},{96,64},{128,160},{160,128},{192,224},{224,1... | collective-permute-start | bytes 393224 | tf_op jit(solution)/shard_map/ppermute | solution.py:273
  53.0 7.0 %collective-permute-start.23 = (bf16[256,256]{1,0:T(8,128)(2,1)S(1)}, bf16[256,256]{1,0:T(8,128)(2,1)S(1)}, u32[]{:S(2)}, u32[]{:S(2)}) collective-permute-start(bf16[256,256]{1,0:T(8,128)(2,1)S(1)} %shard_map.67.old), channel_id=1, source_target_pairs={{0,32},{32,0},{64,96},{96,64},{128,160},{160,128},{192,224},{224,1... | collective-permute-start | bytes 393224 | tf_op jit(solution)/shard_map/ppermute | solution.py:273
  55.8 7.8 %collective-permute-start.17 = (bf16[256,256]{1,0:T(8,128)(2,1)S(1)}, bf16[256,256]{1,0:T(8,128)(2,1)S(1)}, u32[]{:S(2)}, u32[]{:S(2)}) collective-permute-start(bf16[256,256]{1,0:T(8,128)(2,1)S(1)} %shard_map.60.old), channel_id=1, source_target_pairs={{0,224},{32,192},{64,160},{96,128},{128,96},{160,64},{192,32},{224... | collective-permute-start | bytes 393224 | tf_op jit(solution)/shard_map/ppermute | solution.py:273
  60.0 7.1 %collective-permute-start.24 = (bf16[256,256]{1,0:T(8,128)(2,1)S(1)}, bf16[256,256]{1,0:T(8,128)(2,1)S(1)}, u32[]{:S(2)}, u32[]{:S(2)}) collective-permute-start(bf16[256,256]{1,0:T(8,128)(2,1)S(1)} %shard_map.68.old), channel_id=1, source_target_pairs={{0,224},{32,192},{64,160},{96,128},{128,96},{160,64},{192,32},{224... | collective-permute-start | bytes 393224 | tf_op jit(solution)/shard_map/ppermute | solution.py:273
  63.6 6.2 %collective-permute-start.18 = (bf16[256,256]{1,0:T(8,128)(2,1)S(1)}, bf16[256,256]{1,0:T(8,128)(2,1)S(1)}, u32[]{:S(2)}, u32[]{:S(2)}) collective-permute-start(bf16[256,256]{1,0:T(8,128)(2,1)S(1)} %shard_map.61.old), channel_id=1, source_target_pairs={{0,32},{32,0},{64,96},{96,64},{128,160},{160,128},{192,224},{224,1... | collective-permute-start | bytes 393224 | tf_op jit(solution)/shard_map/ppermute | solution.py:273
  67.1 6.1 %collective-permute-start.25 = (bf16[256,256]{1,0:T(8,128)(2,1)S(1)}, bf16[256,256]{1,0:T(8,128)(2,1)S(1)}, u32[]{:S(2)}, u32[]{:S(2)}) collective-permute-start(bf16[256,256]{1,0:T(8,128)(2,1)S(1)} %shard_map.69.old), channel_id=1, source_target_pairs={{0,32},{32,0},{64,96},{96,64},{128,160},{160,128},{192,224},{224,1... | collective-permute-start | bytes 393224 | tf_op jit(solution)/shard_map/ppermute | solution.py:273
  69.8 5.2 %collective-permute-start.19 = (bf16[256,256]{1,0:T(8,128)(2,1)S(1)}, bf16[256,256]{1,0:T(8,128)(2,1)S(1)}, u32[]{:S(2)}, u32[]{:S(2)}) collective-permute-start(bf16[256,256]{1,0:T(8,128)(2,1)S(1)} %shard_map.62.old), channel_id=1, source_target_pairs={{0,32},{32,0},{64,96},{96,64},{128,160},{160,192},{192,224},{224,1... | collective-permute-start | bytes 393224 | tf_op jit(solution)/shard_map/ppermute | solution.py:273
  73.2 6.0 %collective-permute-start.26 = (bf16[256,256]{1,0:T(8,128)(2,1)S(1)}, bf16[256,256]{1,0:T(8,128)(2,1)S(1)}, u32[]{:S(2)}, u32[]{:S(2)}) collective-permute-start(bf16[256,256]{1,0:T(8,128)(2,1)S(1)} %shard_map.70.old), channel_id=1, source_target_pairs={{0,32},{32,0},{64,96},{96,64},{128,160},{160,192},{192,224},{224,1... | collective-permute-start | bytes 393224 | tf_op jit(solution)/shard_map/ppermute | solution.py:273
  75.0 7.2 %collective-permute-start.20 = (bf16[256,256]{1,0:T(8,128)(2,1)S(1)}, bf16[256,256]{1,0:T(8,128)(2,1)S(1)}, u32[]{:S(2)}, u32[]{:S(2)}) collective-permute-start(bf16[256,256]{1,0:T(8,128)(2,1)S(1)} %shard_map.63.old), channel_id=1, source_target_pairs={{0,32},{32,0},{64,96},{96,64},{128,160},{160,128},{192,224},{224,1... | collective-permute-start | bytes 393224 | tf_op jit(solution)/shard_map/ppermute | solution.py:273
  79.2 5.8 %collective-permute-start.27 = (bf16[256,256]{1,0:T(8,128)(2,1)S(1)}, bf16[256,256]{1,0:T(8,128)(2,1)S(1)}, u32[]{:S(2)}, u32[]{:S(2)}) collective-permute-start(bf16[256,256]{1,0:T(8,128)(2,1)S(1)} %shard_map.71.old), channel_id=1, source_target_pairs={{0,32},{32,0},{64,96},{96,64},{128,160},{160,128},{192,224},{224,1... | collective-permute-start | bytes 393224 | tf_op jit(solution)/shard_map/ppermute | solution.py:273
  (7 other events, 102.8 us)

commit v3 on v2

--- a/solution.py
+++ b/solution.py
@@ -17,37 +17,37 @@
 SMEM = pl.BlockSpec(memory_space=pltpu.SMEM)
 
 
-def across_lanes(values, bit):
+def across_lanes(values, lanes_of):
     lane = lax.broadcasted_iota(jnp.int32, values.shape, 1)
-    return jnp.take_along_axis(values, lane ^ bit, axis=1)
-
-
-def normalize(values):
+    return jnp.take_along_axis(values, lanes_of(lane), axis=1)
+
+
+def group_stats(values):
     pixels, channels = values.shape
-    origin = values[0:1]
+    halves = range(0, channels, 128)
+    top = jnp.broadcast_to(values[0:1], (8, channels))
+    origin = [across_lanes(top[:, k : k + 128], lambda lane: lane & ~(GROUP - 1)) for k in halves]
+    origin = jnp.concatenate(origin, axis=1)[0:1]
     moved = values - origin
-    total = jnp.sum(moved, axis=0, keepdims=True) * (1.0 / pixels)
-    square = jnp.sum(moved * moved, axis=0, keepdims=True) - total * total * pixels
-    means = []
-    squares = []
-    for k in range(0, channels, 128):
-        mean = jnp.broadcast_to((origin + total)[:, k : k + 128], (8, 128))
-        spread = jnp.broadcast_to(square[:, k : k + 128], (8, 128))
-        count = pixels
-        for bit in (1, 2, 4):
-            other = across_lanes(mean, bit)
-            apart = mean - other
-            spread = spread + across_lanes(spread, bit) + apart * apart * (0.5 * count)
-            mean = 0.5 * (mean + other)
-            count = 2 * count
-        means.append(mean[0:1])
-        squares.append(spread[0:1])
-    variance = jnp.maximum(jnp.concatenate(squares, axis=1) * (1.0 / count), 0.0)
-    return values - jnp.concatenate(means, axis=1), lax.rsqrt(variance + 1e-05)
-
-
-def silu(values):
-    half = 0.5 * values
+    total = jnp.sum(moved, axis=0, keepdims=True)
+    square = jnp.sum(moved * moved, axis=0, keepdims=True)
+    upper = lax.broadcasted_iota(jnp.int32, (8, channels), 0) < 4
+    both = jnp.where(upper, total, square)
+    sums = []
+    for k in halves:
+        half = both[:, k : k + 128]
+        parts = [half]
+        parts += [across_lanes(half, lambda lane, bit=bit: lane ^ bit) for bit in range(1, GROUP)]
+        while len(parts) > 1:
+            parts = [left + right for left, right in zip(parts[::2], parts[1::2])]
+        sums += parts
+    sums = jnp.concatenate(sums, axis=1) * (1.0 / (pixels * GROUP))
+    mean = sums[0:1]
+    variance = jnp.maximum(sums[4:5] - mean * mean, 0.0)
+    return origin + mean, lax.rsqrt(variance + 1e-05)
+
+
+def silu_of_twice(half):
     return half + half * jnp.tanh(half)
 
 
@@ -84,12 +84,14 @@
         block_in = entering[...].astype(jnp.float32)
         if skip is not None:
             block_in = (block_in + skip[...].astype(jnp.float32)) * RESCALE
-        centred, inverse = normalize(block_in)
-        hidden = conv(silu(centred * inverse), rows, weights.at[pl.ds(0, depth), :])
-        centred, inverse = normalize(hidden)
+        mean, inverse = group_stats(block_in)
+        first = silu_of_twice((block_in - mean) * (0.5 * inverse))
+        hidden = conv(first, rows, weights.at[pl.ds(0, depth), :])
+        mean, inverse = group_stats(hidden)
         scale = modulation[:, :channels]
         shift = modulation[:, channels:]
-        second = silu(centred * (inverse * (1.0 + scale)) + shift)
+        gain = (0.5 * inverse) * (1.0 + scale)
+        second = silu_of_twice((hidden - mean) * gain + 0.5 * shift)
         branch = conv(second, rows, weights.at[pl.ds(depth, depth), :])
         out[...] = (block_in + branch).astype(jnp.bfloat16)
 
@@ -241,19 +243,24 @@
     return weights.reshape(-1, channels), features, timesteps
 
 
-def route(step, sections):
+def route(step, sections, count):
     half = sections // 2
+    partner = {step: step + 1, step + 1: step}
     if step == half - 1:
-        return [(s, sections - 1 - s) for s in range(sections)]
-    pairs = {s: s ^ 1 for s in range(sections)}
-    if step % 2:
-        first = step // half * half
-        pairs.update({first + k: first + (k + 1) % half for k in range(half)})
-    return list(pairs.items())
+        partner.update({half - 2: half + 1, half + 1: half - 2})
+    if step == half:
+        partner.update({s: sections - 1 - s for s in range(sections) if s < half - 2 or s > half + 1})
+    pairs = []
+    for s in range(sections):
+        for d in range(count):
+            other = (partner[s], d) if s in partner else (s, d ^ 1)
+            pairs.append((s * count + d, other[0] * count + other[1]))
+    return pairs
 
 
 def shards(features, timesteps, codes, scales, time_weight):
     sections = lax.axis_size("section")
+    count = lax.axis_size("dp")
     micros = features.shape[0]
     channels = features.shape[4]
     pixels = SIDE * SIDE
@@ -263,16 +270,20 @@
     modulation = jnp.dot(embedding, time_weight[0], preferred_element_type=jnp.float32)
     entering = [features[m].reshape(pixels, channels) for m in range(micros)]
     outs = list(entering)
-    skips = None
+    near = far = None
     for step in range(sections):
         sent = []
         for m in range(micros):
-            skip = None if step < half else entering[m] if step == half else skips[m]
+            skip = None
+            if step >= half:
+                skip = (entering, near, far)[min(step - half, 2)][m]
             outs[m] = res_block(step, entering[m], skip, modulation[m : m + 1], weights, outs[m])
             if step < sections - 1:
-                sent.append(lax.ppermute(outs[m], "section", route(step, sections)))
+                sent.append(lax.ppermute(outs[m], ("section", "dp"), route(step, sections, count)))
         if step == half - 1:
-            skips = sent
+            near = sent
+        if step == half:
+            far = sent
         entering = sent
     return jnp.stack(outs).reshape((1, micros, 1, SIDE, SIDE, channels))
 

time: 88 us -> 85.6 us (0.973)
  waiting for transfers between devices: 35.9 us -> 23.8 us
  starting transfers between devices: 44.1 us -> 54.5 us
    ppermute x14, waiting for transfers between devices: 23.8 us -> 11.7 us  [shards(): lax.ppermute(outs[m], ('section', 'dp'), route(step, sections, count))]
    ppermute x14, starting transfers between devices: 22.1 us -> 32.5 us  [shards(): lax.ppermute(outs[m], ('section', 'dp'), route(step, sections, count))]
  transfers between devices with their start and end apart: 28 -> 28, of which waited for: 18 -> 17; matrix products, arithmetic and copies ran while one was open for 1% -> 2% of each run, Pallas kernels for 2% -> 2%
where the time goes in v3:
time: 85.6 us; the launch traced here: 85.5 us
  starting transfers between devices  54.5 us (64%)
  waiting for transfers between devices  23.8 us (28%)
  Pallas kernels  4 us (5%)
  other arithmetic  2.48 us (3%)
    ppermute x14, starting transfers between devices, shards(): lax.ppermute(outs[m], ('section', 'dp'), route(step, sections, count))  32.5 us
    ppermute x5, starting transfers between devices, along_ring(): lax.ppermute(value, 'dp', [(i, onward(i, hops)) for i in range(count)])  16.7 us
    ppermute x14, waiting for transfers between devices, shards(): lax.ppermute(outs[m], ('section', 'dp'), route(step, sections, count))  11.7 us
    ppermute x5, waiting for transfers between devices, along_ring(): lax.ppermute(value, 'dp', [(i, onward(i, hops)) for i in range(count)])  9.49 us
    ppermute x2, starting transfers between devices, facing_side(): return lax.ppermute(value, 'dp', [(i, i ^ 2 * RING) for i in range(count)])  3.7 us
    pallas_call x16, Pallas kernels, res_block(): pl.pallas_call(functools.partial(block_kernel, step), out_shape=jax.Shape...  3.15 us
    ppermute x7, waiting for transfers between devices, other_core(): return lax.ppermute(value, 'dp', [(i, i ^ 1) for i in range(count)])  2.33 us
  transfers between devices with their start and end apart: 28, of which 17 were waited for; matrix products, arithmetic and copies ran while one was open for 2% of the time, Pallas kernels for 2%

profile of v3, /device:TPU:26, one launch (start us, length us, event | category | flops | bytes accessed | tf_op | source)
XLA Modules:
  0.0 85.5 jit_solution(15768688674918805968)
XLA Ops:
  0.1 1.5 %collective-permute-done = bf16[2,72,256]{2,1,0:T(8,128)(2,1)S(1)} collective-permute-done((bf16[2,72,256]{2,1,0:T(8,128)(2,1)}, bf16[2,72,256]{2,1,0:T(8,128)(2,1)S(1)}, u32[]{:S(2)}, u32[]{:S(2)}) %collective-permute-start) | collective-permute-done | bytes 73760 | tf_op jit(solution)/shard_map/ppermute | solution.py:201
  1.6 0.9 %broadcast_select_fusion = (bf16[2,72,256]{2,1,0:T(8,128)(2,1)S(1)}, bf16[2,72,256]{2,1,0:T(8,128)(2,1)S(1)}) fusion(bf16[2,72,256]{2,1,0:T(8,128)(2,1)S(1)} %collective-permute-done, pred[]{:T(512)S(6)} %eq.4, bf16[1,2,72,256]{3,2,1,0:T(8,128)(2,1)} %param.7), kind=kLoop, calls=%fused_computation.14 | loop fusion | flops 73728 | bytes 294913 | tf_op jit(solution)/shard_map/jit(_where)/select_n | solution.py:206
  2.5 2.2 %collective-permute-start.4 = (bf16[2,144,256]{2,1,0:T(8,128)(2,1)S(1)}, bf16[2,144,256]{2,1,0:T(8,128)(2,1)S(1)}, u32[]{:S(2)}, u32[]{:S(2)}) collective-permute-start(bf16[2,144,256]{2,1,0:T(8,128)(2,1)S(1)} %pad_maximum_fusion.3), channel_id=1, source_target_pairs={{0,16},{1,17},{2,18},{3,19},{4,20},{5,21},{6,22},{7,23},{8,24},{9,... | collective-permute-start | bytes 442376 | tf_op jit(solution)/shard_map/ppermute | solution.py:198
  4.7 6.7 %collective-permute-start.2 = (bf16[2,144,256]{2,1,0:T(8,128)(2,1)S(1)}, bf16[2,144,256]{2,1,0:T(8,128)(2,1)S(1)}, u32[]{:S(2)}, u32[]{:S(2)}) collective-permute-start(bf16[2,144,256]{2,1,0:T(8,128)(2,1)S(1)} %pad_maximum_fusion.3), channel_id=1, source_target_pairs={{0,10},{1,7},{2,12},{3,9},{4,14},{5,11},{6,0},{7,13},{8,2},{9,15},... | collective-permute-start | bytes 442376 | tf_op jit(solution)/shard_map/ppermute | solution.py:195
  12.0 4.6 %collective-permute-start.1 = (bf16[144,256]{1,0:T(8,128)(2,1)S(1)}, bf16[144,256]{1,0:T(8,128)(2,1)S(1)}, u32[]{:S(2)}, u32[]{:S(2)}) collective-permute-start(bf16[144,256]{1,0:T(8,128)(2,1)S(1)} %fusion.4), channel_id=1, source_target_pairs={{0,8},{1,9},{2,10},{3,11},{4,12},{5,13},{6,14},{7,15},{8,0},{9,1},... | collective-permute-start | bytes 221192 | tf_op jit(solution)/shard_map/ppermute | solution.py:195
  16.6 7.1 %collective-permute-done.1.half = bf16[144,256]{1,0:T(8,128)(2,1)S(1)} collective-permute-done((bf16[144,256]{1,0:T(8,128)(2,1)S(1)}, bf16[144,256]{1,0:T(8,128)(2,1)S(1)}, u32[]{:S(2)}, u32[]{:S(2)}) %collective-permute-start.1) | collective-permute-done | bytes 73760 | tf_op jit(solution)/shard_map/ppermute | solution.py:195
  23.8 2.0 %collective-permute-start.5 = (bf16[4,144,256]{2,1,0:T(8,128)(2,1)S(1)}, bf16[4,144,256]{2,1,0:T(8,128)(2,1)S(1)}, u32[]{:S(2)}, u32[]{:S(2)}) collective-permute-start(bf16[4,144,256]{2,1,0:T(8,128)(2,1)S(1)} %pad_maximum_fusion.mine_0_), channel_id=1, source_target_pairs={{0,14},{1,3},{2,0},{3,5},{4,2},{5,7},{6,4},{7,9},{8,6},{9,11},{10,... | collective-permute-start | bytes 884744 | tf_op jit(solution)/shard_map/ppermute | solution.py:195
  26.4 1.5 %collective-permute-start.7 = (bf16[3,144,256]{2,1,0:T(8,128)(2,1)S(1)}, bf16[3,144,256]{2,1,0:T(8,128)(2,1)S(1)}, u32[]{:S(2)}, u32[]{:S(2)}) collective-permute-start(bf16[3,144,256]{2,1,0:T(8,128)(2,1)S(1)} %pad_maximum_fusion.2), channel_id=1, source_target_pairs={{0,16},{1,17},{2,18},{3,19},{4,20},{5,21},{6,22},{7,23},{8,24},{9,... | collective-permute-start | bytes 663560 | tf_op jit(solution)/shard_map/ppermute | solution.py:198
  27.8 2.9 %collective-permute-start.6 = (bf16[2,144,256]{2,1,0:T(8,128)(2,1)S(1)}, bf16[2,144,256]{2,1,0:T(8,128)(2,1)S(1)}, u32[]{:S(2)}, u32[]{:S(2)}) collective-permute-start(bf16[2,144,256]{2,1,0:T(8,128)(2,1)S(1)} %slice.18), channel_id=1, source_target_pairs={{0,12},{1,5},{2,14},{3,7},{4,0},{5,9},{6,2},{7,11},{8,4},{9,13},{1... | collective-permute-start | bytes 442376 | tf_op jit(solution)/shard_map/ppermute | solution.py:195
  32.7 2.4 %collective-permute-done.6.mine_1_ = bf16[2,144,256]{2,1,0:T(8,128)(2,1)S(1)} collective-permute-done((bf16[2,144,256]{2,1,0:T(8,128)(2,1)S(1)}, bf16[2,144,256]{2,1,0:T(8,128)(2,1)S(1)}, u32[]{:S(2)}, u32[]{:S(2)}) %collective-permute-start.6) | collective-permute-done | bytes 147488 | tf_op jit(solution)/shard_map/ppermute | solution.py:195
  38.0 0.8 collective-permute-done.14.entering
  39.3 0.8 collective-permute-done.15.entering
  40.7 0.8 collective-permute-done.16.entering
  42.0 0.8 collective-permute-done.17.entering.skip
  42.9 8.5 %collective-permute-start.18 = (bf16[256,256]{1,0:T(8,128)(2,1)S(1)}, bf16[256,256]{1,0:T(8,128)(2,1)S(1)}, u32[]{:S(2)}, u32[]{:S(2)}) collective-permute-start(bf16[256,256]{1,0:T(8,128)(2,1)S(1)} %shard_map.61.old), channel_id=1, source_target_pairs={{0,224},{1,225},{2,226},{3,227},{4,228},{5,229},{6,230},{7,231},{8... | collective-permute-start | bytes 393224 | tf_op jit(solution)/shard_map/ppermute | solution.py:282
  51.3 1.2 %collective-permute-start.25 = (bf16[256,256]{1,0:T(8,128)(2,1)S(1)}, bf16[256,256]{1,0:T(8,128)(2,1)S(1)}, u32[]{:S(2)}, u32[]{:S(2)}) collective-permute-start(bf16[256,256]{1,0:T(8,128)(2,1)S(1)} %shard_map.69.old), channel_id=1, source_target_pairs={{0,224},{1,225},{2,226},{3,227},{4,228},{5,229},{6,230},{7,231},{8... | collective-permute-start | bytes 393224 | tf_op jit(solution)/shard_map/ppermute | solution.py:282
  52.5 2.8 %collective-permute-done.18.entering.skip = bf16[256,256]{1,0:T(8,128)(2,1)S(1)} collective-permute-done((bf16[256,256]{1,0:T(8,128)(2,1)S(1)}, bf16[256,256]{1,0:T(8,128)(2,1)S(1)}, u32[]{:S(2)}, u32[]{:S(2)}) %collective-permute-start.18) | collective-permute-done | bytes 131104 | tf_op jit(solution)/shard_map/ppermute | solution.py:282
  55.3 3.6 %collective-permute-done.25.entering.skip = bf16[256,256]{1,0:T(8,128)(2,1)S(1)} collective-permute-done((bf16[256,256]{1,0:T(8,128)(2,1)S(1)}, bf16[256,256]{1,0:T(8,128)(2,1)S(1)}, u32[]{:S(2)}, u32[]{:S(2)}) %collective-permute-start.25) | collective-permute-done | bytes 131104 | tf_op jit(solution)/shard_map/ppermute | solution.py:282
  58.9 19.3 %collective-permute-start.20 = (bf16[256,256]{1,0:T(8,128)(2,1)S(1)}, bf16[256,256]{1,0:T(8,128)(2,1)S(1)}, u32[]{:S(2)}, u32[]{:S(2)}) collective-permute-start(bf16[256,256]{1,0:T(8,128)(2,1)S(1)} %shard_map.63.old), channel_id=1, source_target_pairs={{0,1},{1,0},{2,3},{3,2},{4,5},{5,4},{6,7},{7,6},{8,9},{9,8},{10,11... | collective-permute-start | bytes 393224 | tf_op jit(solution)/shard_map/ppermute | solution.py:282
  78.3 1.7 %collective-permute-start.27 = (bf16[256,256]{1,0:T(8,128)(2,1)S(1)}, bf16[256,256]{1,0:T(8,128)(2,1)S(1)}, u32[]{:S(2)}, u32[]{:S(2)}) collective-permute-start(bf16[256,256]{1,0:T(8,128)(2,1)S(1)} %shard_map.71.old), channel_id=1, source_target_pairs={{0,1},{1,0},{2,3},{3,2},{4,5},{5,4},{6,7},{7,6},{8,9},{9,8},{10,11... | collective-permute-start | bytes 393224 | tf_op jit(solution)/shard_map/ppermute | solution.py:282
  79.9 1.5 %collective-permute-done.20.entering = bf16[256,256]{1,0:T(8,128)(2,1)S(1)} collective-permute-done((bf16[256,256]{1,0:T(8,128)(2,1)S(1)}, bf16[256,256]{1,0:T(8,128)(2,1)S(1)}, u32[]{:S(2)}, u32[]{:S(2)}) %collective-permute-start.20) | collective-permute-done | bytes 131104 | tf_op jit(solution)/shard_map/ppermute | solution.py:282
  81.5 1.6 %shard_map.64 = bf16[256,256]{1,0:T(8,128)(2,1)S(1)} custom-call(bf16[256,256]{1,0:T(8,128)(2,1)S(1)} %collective-permute-done.20.entering, bf16[256,256]{1,0:T(8,128)(2,1)S(1)} %collective-permute-done.18.entering.skip, f32[1,512]{1,0:T(1,128)S(1)} %get-tuple-element.23.modulation, bf16[4608,256]{1,0:T(8,128)(2,1)S(1)} %bitcast.33, ...), custom_call_target="tpu_custom_call", output_to_operand_aliasing={{}: (4, {})} | custom-call | flops 603979776 | bytes 3000000 | tf_op jit(solution)/shard_map/pallas_call | solution.py:101
  83.2 1.6 %shard_map.72 = bf16[256,256]{1,0:T(8,128)(2,1)S(1)} custom-call(bf16[256,256]{1,0:T(8,128)(2,1)S(1)} %collective-permute-done.27.entering, bf16[256,256]{1,0:T(8,128)(2,1)S(1)} %collective-permute-done.25.entering.skip, f32[1,512]{1,0:T(1,128)S(1)} %get-tuple-element.24.modulation, bf16[4608,256]{1,0:T(8,128)(2,1)S(1)} %bitcast.34, ...), custom_call_target="tpu_custom_call", output_to_operand_aliasing={{}: (4, {})} | custom-call | flops 603979776 | bytes 3000000 | tf_op jit(solution)/shard_map/pallas_call | solution.py:101
  84.8 0.7 pad_maximum_fusion.1
  (76 shorter events, 7.9 us)
Async XLA Ops:
  0.0 1.6 %collective-permute-start = (bf16[2,72,256]{2,1,0:T(8,128)(2,1)}, bf16[2,72,256]{2,1,0:T(8,128)(2,1)S(1)}, u32[]{:S(2)}, u32[]{:S(2)}) collective-permute-start(bf16[2,72,256]{2,1,0:T(8,128)(2,1)} %bitcast.42), channel_id=1, source_target_pairs={{0,1},{1,0},{2,3},{3,2},{4,5},{5,4},{6,7},{7,6},{8,9},{9,8},{10,11... | collective-permute-start | bytes 221192 | tf_op jit(solution)/shard_map/ppermute | solution.py:201
  2.5 14.1 %collective-permute-start.4 = (bf16[2,144,256]{2,1,0:T(8,128)(2,1)S(1)}, bf16[2,144,256]{2,1,0:T(8,128)(2,1)S(1)}, u32[]{:S(2)}, u32[]{:S(2)}) collective-permute-start(bf16[2,144,256]{2,1,0:T(8,128)(2,1)S(1)} %pad_maximum_fusion.3), channel_id=1, source_target_pairs={{0,16},{1,17},{2,18},{3,19},{4,20},{5,21},{6,22},{7,23},{8,24},{9,... | collective-permute-start | bytes 442376 | tf_op jit(solution)/shard_map/ppermute | solution.py:198
  4.7 19.0 %collective-permute-start.2 = (bf16[2,144,256]{2,1,0:T(8,128)(2,1)S(1)}, bf16[2,144,256]{2,1,0:T(8,128)(2,1)S(1)}, u32[]{:S(2)}, u32[]{:S(2)}) collective-permute-start(bf16[2,144,256]{2,1,0:T(8,128)(2,1)S(1)} %pad_maximum_fusion.3), channel_id=1, source_target_pairs={{0,10},{1,7},{2,12},{3,9},{4,14},{5,11},{6,0},{7,13},{8,2},{9,15},... | collective-permute-start | bytes 442376 | tf_op jit(solution)/shard_map/ppermute | solution.py:195
  11.5 12.3 %collective-permute-start.3 = (bf16[2,144,256]{2,1,0:T(8,128)(2,1)S(1)}, bf16[2,144,256]{2,1,0:T(8,128)(2,1)S(1)}, u32[]{:S(2)}, u32[]{:S(2)}) collective-permute-start(bf16[2,144,256]{2,1,0:T(8,128)(2,1)S(1)} %pad_maximum_fusion.3), channel_id=1, source_target_pairs={{0,12},{1,5},{2,14},{3,7},{4,0},{5,9},{6,2},{7,11},{8,4},{9,13},{1... | collective-permute-start | bytes 442376 | tf_op jit(solution)/shard_map/ppermute | solution.py:195
  12.0 11.7 %collective-permute-start.1 = (bf16[144,256]{1,0:T(8,128)(2,1)S(1)}, bf16[144,256]{1,0:T(8,128)(2,1)S(1)}, u32[]{:S(2)}, u32[]{:S(2)}) collective-permute-start(bf16[144,256]{1,0:T(8,128)(2,1)S(1)} %fusion.4), channel_id=1, source_target_pairs={{0,8},{1,9},{2,10},{3,11},{4,12},{5,13},{6,14},{7,15},{8,0},{9,1},... | collective-permute-start | bytes 221192 | tf_op jit(solution)/shard_map/ppermute | solution.py:195
  23.8 7.8 %collective-permute-start.5 = (bf16[4,144,256]{2,1,0:T(8,128)(2,1)S(1)}, bf16[4,144,256]{2,1,0:T(8,128)(2,1)S(1)}, u32[]{:S(2)}, u32[]{:S(2)}) collective-permute-start(bf16[4,144,256]{2,1,0:T(8,128)(2,1)S(1)} %pad_maximum_fusion.mine_0_), channel_id=1, source_target_pairs={{0,14},{1,3},{2,0},{3,5},{4,2},{5,7},{6,4},{7,9},{8,6},{9,11},{10,... | collective-permute-start | bytes 884744 | tf_op jit(solution)/shard_map/ppermute | solution.py:195
  25.7 9.9 %collective-permute-start.12 = (bf16[2,144,256]{2,1,0:T(8,128)(2,1)S(1)}, bf16[2,144,256]{2,1,0:T(8,128)(2,1)S(1)}, u32[]{:S(2)}, u32[]{:S(2)}) collective-permute-start(bf16[2,144,256]{2,1,0:T(8,128)(2,1)S(1)} %collective-permute-done.2.mine_2_), channel_id=1, source_target_pairs={{0,1},{1,0},{2,3},{3,2},{4,5},{5,4},{6,7},{7,6},{8,9},{9,8},{10,11... | collective-permute-start | bytes 442376 | tf_op jit(solution)/shard_map/ppermute | solution.py:201
  25.8 6.3 %collective-permute-start.13 = (bf16[144,256]{1,0:T(8,128)(2,1)S(1)}, bf16[144,256]{1,0:T(8,128)(2,1)S(1)}, u32[]{:S(2)}, u32[]{:S(2)}) collective-permute-start(bf16[144,256]{1,0:T(8,128)(2,1)S(1)} %collective-permute-done.1.half), channel_id=1, source_target_pairs={{0,1},{1,0},{2,3},{3,2},{4,5},{5,4},{6,7},{7,6},{8,9},{9,8},{10,11... | collective-permute-start | bytes 221192 | tf_op jit(solution)/shard_map/ppermute | solution.py:201
  26.4 9.0 %collective-permute-start.7 = (bf16[3,144,256]{2,1,0:T(8,128)(2,1)S(1)}, bf16[3,144,256]{2,1,0:T(8,128)(2,1)S(1)}, u32[]{:S(2)}, u32[]{:S(2)}) collective-permute-start(bf16[3,144,256]{2,1,0:T(8,128)(2,1)S(1)} %pad_maximum_fusion.2), channel_id=1, source_target_pairs={{0,16},{1,17},{2,18},{3,19},{4,20},{5,21},{6,22},{7,23},{8,24},{9,... | collective-permute-start | bytes 663560 | tf_op jit(solution)/shard_map/ppermute | solution.py:198
  27.8 7.2 %collective-permute-start.6 = (bf16[2,144,256]{2,1,0:T(8,128)(2,1)S(1)}, bf16[2,144,256]{2,1,0:T(8,128)(2,1)S(1)}, u32[]{:S(2)}, u32[]{:S(2)}) collective-permute-start(bf16[2,144,256]{2,1,0:T(8,128)(2,1)S(1)} %slice.18), channel_id=1, source_target_pairs={{0,12},{1,5},{2,14},{3,7},{4,0},{5,9},{6,2},{7,11},{8,4},{9,13},{1... | collective-permute-start | bytes 442376 | tf_op jit(solution)/shard_map/ppermute | solution.py:195
  31.5 5.3 %collective-permute-start.8 = (bf16[4,144,256]{2,1,0:T(8,128)(2,1)S(1)}, bf16[4,144,256]{2,1,0:T(8,128)(2,1)S(1)}, u32[]{:S(2)}, u32[]{:S(2)}) collective-permute-start(bf16[4,144,256]{2,1,0:T(8,128)(2,1)S(1)} %collective-permute-done.5.mine_0_), channel_id=1, source_target_pairs={{0,1},{1,0},{2,3},{3,2},{4,5},{5,4},{6,7},{7,6},{8,9},{9,8},{10,11... | collective-permute-start | bytes 884744 | tf_op jit(solution)/shard_map/ppermute | solution.py:201
  32.1 3.5 %collective-permute-start.11 = (bf16[2,144,256]{2,1,0:T(8,128)(2,1)S(1)}, bf16[2,144,256]{2,1,0:T(8,128)(2,1)S(1)}, u32[]{:S(2)}, u32[]{:S(2)}) collective-permute-start(bf16[2,144,256]{2,1,0:T(8,128)(2,1)S(1)} %collective-permute-done.3.mine_1_), channel_id=1, source_target_pairs={{0,1},{1,0},{2,3},{3,2},{4,5},{5,4},{6,7},{7,6},{8,9},{9,8},{10,11... | collective-permute-start | bytes 442376 | tf_op jit(solution)/shard_map/ppermute | solution.py:201
  35.1 1.4 %collective-permute-start.9 = (bf16[2,144,256]{2,1,0:T(8,128)(2,1)S(1)}, bf16[2,144,256]{2,1,0:T(8,128)(2,1)S(1)}, u32[]{:S(2)}, u32[]{:S(2)}) collective-permute-start(bf16[2,144,256]{2,1,0:T(8,128)(2,1)S(1)} %collective-permute-done.6.mine_1_), channel_id=1, source_target_pairs={{0,1},{1,0},{2,3},{3,2},{4,5},{5,4},{6,7},{7,6},{8,9},{9,8},{10,11... | collective-permute-start | bytes 442376 | tf_op jit(solution)/shard_map/ppermute | solution.py:201
  35.4 1.5 %collective-permute-start.10 = (bf16[3,144,256]{2,1,0:T(8,128)(2,1)S(1)}, bf16[3,144,256]{2,1,0:T(8,128)(2,1)S(1)}, u32[]{:S(2)}, u32[]{:S(2)}) collective-permute-start(bf16[3,144,256]{2,1,0:T(8,128)(2,1)S(1)} %collective-permute-done.7.mine_2_), channel_id=1, source_target_pairs={{0,1},{1,0},{2,3},{3,2},{4,5},{5,4},{6,7},{7,6},{8,9},{9,8},{10,11... | collective-permute-start | bytes 663560 | tf_op jit(solution)/shard_map/ppermute | solution.py:201
  37.4 1.4 %collective-permute-start.14 = (bf16[256,256]{1,0:T(8,128)(2,1)S(1)}, bf16[256,256]{1,0:T(8,128)(2,1)S(1)}, u32[]{:S(2)}, u32[]{:S(2)}) collective-permute-start(bf16[256,256]{1,0:T(8,128)(2,1)S(1)} %shard_map.57.old), channel_id=1, source_target_pairs={{0,32},{1,33},{2,34},{3,35},{4,36},{5,37},{6,38},{7,39},{8,40},{9,... | collective-permute-start | bytes 393224 | tf_op jit(solution)/shard_map/ppermute | solution.py:282
  37.7 1.4 %collective-permute-start.21 = (bf16[256,256]{1,0:T(8,128)(2,1)S(1)}, bf16[256,256]{1,0:T(8,128)(2,1)S(1)}, u32[]{:S(2)}, u32[]{:S(2)}) collective-permute-start(bf16[256,256]{1,0:T(8,128)(2,1)S(1)} %shard_map.65.old), channel_id=1, source_target_pairs={{0,32},{1,33},{2,34},{3,35},{4,36},{5,37},{6,38},{7,39},{8,40},{9,... | collective-permute-start | bytes 393224 | tf_op jit(solution)/shard_map/ppermute | solution.py:282
  38.8 1.3 %collective-permute-start.15 = (bf16[256,256]{1,0:T(8,128)(2,1)S(1)}, bf16[256,256]{1,0:T(8,128)(2,1)S(1)}, u32[]{:S(2)}, u32[]{:S(2)}) collective-permute-start(bf16[256,256]{1,0:T(8,128)(2,1)S(1)} %shard_map.58.old), channel_id=1, source_target_pairs={{0,1},{1,0},{2,3},{3,2},{4,5},{5,4},{6,7},{7,6},{8,9},{9,8},{10,11... | collective-permute-start | bytes 393224 | tf_op jit(solution)/shard_map/ppermute | solution.py:282
  41.8 9.5 %collective-permute-start.24 = (bf16[256,256]{1,0:T(8,128)(2,1)S(1)}, bf16[256,256]{1,0:T(8,128)(2,1)S(1)}, u32[]{:S(2)}, u32[]{:S(2)}) collective-permute-start(bf16[256,256]{1,0:T(8,128)(2,1)S(1)} %shard_map.68.old), channel_id=1, source_target_pairs={{0,1},{1,0},{2,3},{3,2},{4,5},{5,4},{6,7},{7,6},{8,9},{9,8},{10,11... | collective-permute-start | bytes 393224 | tf_op jit(solution)/shard_map/ppermute | solution.py:282
  42.9 12.5 %collective-permute-start.18 = (bf16[256,256]{1,0:T(8,128)(2,1)S(1)}, bf16[256,256]{1,0:T(8,128)(2,1)S(1)}, u32[]{:S(2)}, u32[]{:S(2)}) collective-permute-start(bf16[256,256]{1,0:T(8,128)(2,1)S(1)} %shard_map.61.old), channel_id=1, source_target_pairs={{0,224},{1,225},{2,226},{3,227},{4,228},{5,229},{6,230},{7,231},{8... | collective-permute-start | bytes 393224 | tf_op jit(solution)/shard_map/ppermute | solution.py:282
  51.3 7.6 %collective-permute-start.25 = (bf16[256,256]{1,0:T(8,128)(2,1)S(1)}, bf16[256,256]{1,0:T(8,128)(2,1)S(1)}, u32[]{:S(2)}, u32[]{:S(2)}) collective-permute-start(bf16[256,256]{1,0:T(8,128)(2,1)S(1)} %shard_map.69.old), channel_id=1, source_target_pairs={{0,224},{1,225},{2,226},{3,227},{4,228},{5,229},{6,230},{7,231},{8... | collective-permute-start | bytes 393224 | tf_op jit(solution)/shard_map/ppermute | solution.py:282
  55.3 3.6 %collective-permute-start.19 = (bf16[256,256]{1,0:T(8,128)(2,1)S(1)}, bf16[256,256]{1,0:T(8,128)(2,1)S(1)}, u32[]{:S(2)}, u32[]{:S(2)}) collective-permute-start(bf16[256,256]{1,0:T(8,128)(2,1)S(1)} %shard_map.62.old), channel_id=1, source_target_pairs={{0,1},{1,0},{2,3},{3,2},{4,5},{5,4},{6,7},{7,6},{8,9},{9,8},{10,11... | collective-permute-start | bytes 393224 | tf_op jit(solution)/shard_map/ppermute | solution.py:282
  58.9 19.4 %collective-permute-start.26 = (bf16[256,256]{1,0:T(8,128)(2,1)S(1)}, bf16[256,256]{1,0:T(8,128)(2,1)S(1)}, u32[]{:S(2)}, u32[]{:S(2)}) collective-permute-start(bf16[256,256]{1,0:T(8,128)(2,1)S(1)} %shard_map.70.old), channel_id=1, source_target_pairs={{0,1},{1,0},{2,3},{3,2},{4,5},{5,4},{6,7},{7,6},{8,9},{9,8},{10,11... | collective-permute-start | bytes 393224 | tf_op jit(solution)/shard_map/ppermute | solution.py:282
  58.9 22.5 %collective-permute-start.20 = (bf16[256,256]{1,0:T(8,128)(2,1)S(1)}, bf16[256,256]{1,0:T(8,128)(2,1)S(1)}, u32[]{:S(2)}, u32[]{:S(2)}) collective-permute-start(bf16[256,256]{1,0:T(8,128)(2,1)S(1)} %shard_map.63.old), channel_id=1, source_target_pairs={{0,1},{1,0},{2,3},{3,2},{4,5},{5,4},{6,7},{7,6},{8,9},{9,8},{10,11... | collective-permute-start | bytes 393224 | tf_op jit(solution)/shard_map/ppermute | solution.py:282
  78.3 5.0 %collective-permute-start.27 = (bf16[256,256]{1,0:T(8,128)(2,1)S(1)}, bf16[256,256]{1,0:T(8,128)(2,1)S(1)}, u32[]{:S(2)}, u32[]{:S(2)}) collective-permute-start(bf16[256,256]{1,0:T(8,128)(2,1)S(1)} %shard_map.71.old), channel_id=1, source_target_pairs={{0,1},{1,0},{2,3},{3,2},{4,5},{5,4},{6,7},{7,6},{8,9},{9,8},{10,11... | collective-permute-start | bytes 393224 | tf_op jit(solution)/shard_map/ppermute | solution.py:282
  (7 other events, 100.3 us)

commit v4 on v3

--- a/solution.py
+++ b/solution.py
@@ -126,10 +126,11 @@
     return position // (2 * RING), position // 2 % RING, position % 2
 
 
-def assemble_kernel(there, chips, scales, mine, theirs, half, half_other, old, out):
+def assemble_kernel(there, scales, mine, theirs, old, out):
     far, along, core = dp_place()
     ahead = 1 - 2 * core
     rows, channels = out.shape[1] // (2 * RING), out.shape[2]
+    convs = out.shape[0]
     row = lax.broadcasted_iota(jnp.int32, (rows, channels), 0)
 
     def place(block, facing, where, number):
@@ -143,49 +144,35 @@
         scaled = (block.astype(jnp.float32) * scale).astype(jnp.bfloat16)
         out[number, pl.ds(start, rows), :] = scaled
 
-    convs = out.shape[0]
-
-    def spread(block, facing, where):
-        for number in range(block.shape[0]):
-            if number < convs:
-                place(block[number], facing, where, number)
-            elif block.shape[0] == 2 * convs:
-                place(block[number], not facing, where, number - convs)
+    def spread(block, facing, hops, half):
+        count = block.shape[0]
+        for n in range(count - count % 2):
+            place(block[n], facing if count == convs else n >= convs, along + hops, n % convs)
+        if count % 2:
+            place(block[count - 1], facing, along + RING // 2, half)
 
     for (facing, hops), block in zip(there, mine):
-        spread(block, facing, along + ahead * hops)
+        spread(block, facing, ahead * hops, core)
     for (facing, hops), block in zip(there[len(there) - len(theirs) :], theirs):
-        spread(block, facing, along - ahead * hops)
-    if half is None:
-        half, half_other = mine[-1].at[convs], theirs[-1].at[convs]
-    place(half[...], chips, along + RING // 2, core)
-    place(half_other[...], chips, along + RING // 2, 1 - core)
-
-
-def assembled(there, facing, scales, mine, theirs, half, half_other, old):
+        spread(block, facing, -ahead * hops, 1 - core)
+
+
+def assembled(there, scales, mine, theirs, old):
     rows, channels = mine[0].shape[1:]
     shape = (scales.shape[0], 2 * RING * rows, channels)
     return pl.pallas_call(
-        functools.partial(assemble_kernel, there, facing),
+        functools.partial(assemble_kernel, there),
         out_shape=jax.ShapeDtypeStruct(shape, jnp.bfloat16),
-        in_specs=[
-            VMEM,
-            [VMEM] * len(mine),
-            [VMEM] * len(theirs),
-            None if half is None else VMEM,
-            None if half is None else VMEM,
-            None if old is None else VMEM,
-        ],
+        in_specs=[VMEM, [VMEM] * len(mine), [VMEM] * len(theirs), None if old is None else VMEM],
         out_specs=VMEM,
         input_output_aliases={} if old is None else {1 + len(mine) + len(theirs): 0},
         compiler_params=pltpu.CompilerParams(vmem_limit_bytes=16 * 1024 * 1024),
-    )(scales, mine, theirs, half, half_other, old)
+    )(scales, mine, theirs, old)
 
 
 def gathered_weights(codes, scales, features, timesteps):
     count = lax.axis_size("dp")
     _, _, core = dp_place()
-    convs, rows, channels = codes.shape
 
     def onward(i, hops):
         step = hops * (2 * (i % 2) - 1)
@@ -200,47 +187,37 @@
     def other_core(value):
         return lax.ppermute(value, "dp", [(i, i ^ 1) for i in range(count)])
 
-    def merged(mine, theirs):
-        axis = mine.ndim - 2
-        even = jnp.where(core == 0, mine, theirs)
-        odd = jnp.where(core == 0, theirs, mine)
-        return jnp.concatenate([even, odd], axis=axis)
-
-    own = merged(codes, other_core(codes))
-    part = jnp.where(core == 0, own[0], own[1])
+    def one_conv(value):
+        return jnp.where(core == 0, value[0:1], value[1:2])
+
+    other = other_core(codes)
+    even = jnp.where(core == 0, codes, other)
+    odd = jnp.where(core == 0, other, codes)
+    own = jnp.concatenate([even, odd], axis=1)
     facing = facing_side(own)
     third = along_ring(own, 3)
     second = along_ring(own, 2)
-    far_part = along_ring(part, RING // 2)
-    column = jnp.concatenate([own, facing])
-    far_part, third, second, column, scales, features, timesteps = lax.optimization_barrier(
-        (far_part, third, second, column, scales, features, timesteps)
+    column = jnp.concatenate([own, facing, one_conv(third)])
+    third, second, column, scales, features, timesteps = lax.optimization_barrier(
+        (third, second, column, scales, features, timesteps)
     )
     first = along_ring(column, 1)
-    facing_second = along_ring(column[convs:], 2)
-    late = facing_side(jnp.concatenate([third, far_part[None]]))
+    facing_second = along_ring(column[2:4], 2)
+    facing_third = facing_side(third)
     wide = jnp.repeat(jnp.pad(scales, ((0, 0), (0, 1), (0, 0))), QB, axis=2)
     weights = assembled(
         [(False, 0), (False, 2), (False, 3)],
-        False,
         wide,
-        [column, second, third],
+        [column[:4], second, third],
         [other_core(second), other_core(third)],
-        far_part,
-        other_core(far_part),
         None,
     )
-    weights = assembled(
-        [(False, 1), (True, 2), (True, 3)],
-        True,
-        wide,
-        [first, facing_second, late],
-        [other_core(first), other_core(facing_second), other_core(late)],
-        None,
-        None,
-        weights,
-    )
-    return weights.reshape(-1, channels), features, timesteps
+    last = along_ring(one_conv(facing_third), 1)
+    there = [(False, 1), (True, 2), (True, 3)]
+    mine = [first, facing_second, facing_third]
+    weights = assembled(there, wide, mine, [other_core(block) for block in mine], weights)
+    weights = assembled([(True, 4)], wide, [last], [other_core(last)], weights)
+    return weights.reshape(-1, weights.shape[2]), features, timesteps
 
 
 def route(step, sections, count):

time: 85.6 us -> 82.1 us (0.959)
  starting transfers between devices: 54.5 us -> 52 us
  waiting for transfers between devices: 23.8 us -> 22.3 us
  local copies, waits for them, and re-layouts: 0.34 us -> 1.32 us
    ppermute x2, waiting for transfers between devices: 0.3 us -> 1.98 us  [facing_side(): return lax.ppermute(value, 'dp', [(i, i ^ 2 * RING) for i in range(count)])]
    ppermute x5, waiting for transfers between devices: 9.49 us -> 8.01 us  [along_ring(): lax.ppermute(value, 'dp', [(i, onward(i, hops)) for i in range(count)])]
    ppermute x5, starting transfers between devices: 16.7 us -> 15.2 us  [along_ring(): lax.ppermute(value, 'dp', [(i, onward(i, hops)) for i in range(count)])]
    slice x1, local copies, waits for them, and re-layouts: 0.02 us -> 0.98 us  [shards(): entering = [features[m].reshape(pixels, channels) for m in range(micros)]]
    ppermute x14, waiting for transfers between devices: 11.7 us -> 10.8 us  [shards(): lax.ppermute(outs[m], ('section', 'dp'), route(step, sections, count))]
  transfers between devices with their start and end apart: 28 -> 28, of which waited for: 17 -> 13; matrix products, arithmetic and copies ran while one was open for 2% -> 2% of each run, Pallas kernels for 2% -> 3%
where the time goes in v4:
time: 82.1 us; the launch traced here: 81.9 us
  starting transfers between devices  52 us (63%)
  waiting for transfers between devices  22.3 us (27%)
  Pallas kernels  4.05 us (5%)
  other arithmetic  1.81 us (2%)
  local copies, waits for them, and re-layouts  1.32 us (2%)
    ppermute x14, starting transfers between devices, shards(): lax.ppermute(outs[m], ('section', 'dp'), route(step, sections, count))  32.3 us
    ppermute x5, starting transfers between devices, along_ring(): lax.ppermute(value, 'dp', [(i, onward(i, hops)) for i in range(count)])  15.2 us
    ppermute x14, waiting for transfers between devices, shards(): lax.ppermute(outs[m], ('section', 'dp'), route(step, sections, count))  10.8 us
    ppermute x5, waiting for transfers between devices, along_ring(): lax.ppermute(value, 'dp', [(i, onward(i, hops)) for i in range(count)])  8.01 us
    ppermute x2, starting transfers between devices, facing_side(): return lax.ppermute(value, 'dp', [(i, i ^ 2 * RING) for i in range(count)])  3.47 us
    pallas_call x16, Pallas kernels, res_block(): pl.pallas_call(functools.partial(block_kernel, step), out_shape=jax.Shape...  3.16 us
    ppermute x2, waiting for transfers between devices, facing_side(): return lax.ppermute(value, 'dp', [(i, i ^ 2 * RING) for i in range(count)])  1.98 us
  transfers between devices with their start and end apart: 28, of which 13 were waited for; matrix products, arithmetic and copies ran while one was open for 2% of the time, Pallas kernels for 3%

profile of v4, /device:TPU:26, one launch (start us, length us, event | category | flops | bytes accessed | tf_op | source)
XLA Modules:
  0.0 81.9 jit_solution(15252505346486341723)
XLA Ops:
  0.1 1.5 %collective-permute-done = bf16[2,72,256]{2,1,0:T(8,128)(2,1)S(1)} collective-permute-done((bf16[2,72,256]{2,1,0:T(8,128)(2,1)}, bf16[2,72,256]{2,1,0:T(8,128)(2,1)S(1)}, u32[]{:S(2)}, u32[]{:S(2)}) %collective-permute-start) | collective-permute-done | bytes 73760 | tf_op jit(solution)/shard_map/ppermute | solution.py:188
  1.6 0.9 %broadcast_select_fusion.1 = (bf16[2,72,256]{2,1,0:T(8,128)(2,1)S(1)}, bf16[2,72,256]{2,1,0:T(8,128)(2,1)S(1)}) fusion(bf16[2,72,256]{2,1,0:T(8,128)(2,1)S(1)} %collective-permute-done, pred[]{:T(512)S(6)} %eq.4, bf16[1,2,72,256]{3,2,1,0:T(8,128)(2,1)} %param.7), kind=kLoop, calls=%fused_computation.8 | loop fusion | flops 73728 | bytes 294913 | tf_op jit(solution)/shard_map/jit(_where)/select_n | solution.py:194
  2.5 6.8 %collective-permute-start.1 = (bf16[2,144,256]{2,1,0:T(8,128)(2,1)S(1)}, bf16[2,144,256]{2,1,0:T(8,128)(2,1)S(1)}, u32[]{:S(2)}, u32[]{:S(2)}) collective-permute-start(bf16[2,144,256]{2,1,0:T(8,128)(2,1)S(1)} %pad_maximum_fusion.2), channel_id=1, source_target_pairs={{0,10},{1,7},{2,12},{3,9},{4,14},{5,11},{6,0},{7,13},{8,2},{9,15},... | collective-permute-start | bytes 442376 | tf_op jit(solution)/shard_map/ppermute | solution.py:182
  9.3 2.1 %collective-permute-start.3 = (bf16[2,144,256]{2,1,0:T(8,128)(2,1)S(1)}, bf16[2,144,256]{2,1,0:T(8,128)(2,1)S(1)}, u32[]{:S(2)}, u32[]{:S(2)}) collective-permute-start(bf16[2,144,256]{2,1,0:T(8,128)(2,1)S(1)} %pad_maximum_fusion.2), channel_id=1, source_target_pairs={{0,16},{1,17},{2,18},{3,19},{4,20},{5,21},{6,22},{7,23},{8,24},{9,... | collective-permute-start | bytes 442376 | tf_op jit(solution)/shard_map/ppermute | solution.py:185
  12.0 3.7 %collective-permute-done.1.mine_2_ = bf16[2,144,256]{2,1,0:T(8,128)(2,1)S(1)} collective-permute-done((bf16[2,144,256]{2,1,0:T(8,128)(2,1)S(1)}, bf16[2,144,256]{2,1,0:T(8,128)(2,1)S(1)}, u32[]{:S(2)}, u32[]{:S(2)}) %collective-permute-start.1) | collective-permute-done | bytes 147488 | tf_op jit(solution)/shard_map/ppermute | solution.py:182
  16.0 3.1 %collective-permute-done.2.mine_1_ = bf16[2,144,256]{2,1,0:T(8,128)(2,1)S(1)} collective-permute-done((bf16[2,144,256]{2,1,0:T(8,128)(2,1)S(1)}, bf16[2,144,256]{2,1,0:T(8,128)(2,1)S(1)}, u32[]{:S(2)}, u32[]{:S(2)}) %collective-permute-start.2) | collective-permute-done | bytes 147488 | tf_op jit(solution)/shard_map/ppermute | solution.py:182
  19.1 1.3 %collective-permute-start.7 = (bf16[5,144,256]{2,1,0:T(8,128)(2,1)S(1)}, bf16[5,144,256]{2,1,0:T(8,128)(2,1)S(1)}, u32[]{:S(2)}, u32[]{:S(2)}) collective-permute-start(bf16[5,144,256]{2,1,0:T(8,128)(2,1)S(1)} %pad_maximum_fusion), channel_id=1, source_target_pairs={{0,14},{1,3},{2,0},{3,5},{4,2},{5,7},{6,4},{7,9},{8,6},{9,11},{10,... | collective-permute-start | bytes 1105928 | tf_op jit(solution)/shard_map/ppermute | solution.py:182
  20.5 1.3 %collective-permute-start.4 = (bf16[2,144,256]{2,1,0:T(8,128)(2,1)S(1)}, bf16[2,144,256]{2,1,0:T(8,128)(2,1)S(1)}, u32[]{:S(2)}, u32[]{:S(2)}) collective-permute-start(bf16[2,144,256]{2,1,0:T(8,128)(2,1)S(1)} %collective-permute-done.1.mine_2_), channel_id=1, source_target_pairs={{0,16},{1,17},{2,18},{3,19},{4,20},{5,21},{6,22},{7,23},{8,24},{9,... | collective-permute-start | bytes 442376 | tf_op jit(solution)/shard_map/ppermute | solution.py:185
  22.0 3.4 %collective-permute-start.8 = (bf16[2,144,256]{2,1,0:T(8,128)(2,1)S(1)}, bf16[2,144,256]{2,1,0:T(8,128)(2,1)S(1)}, u32[]{:S(2)}, u32[]{:S(2)}) collective-permute-start(bf16[2,144,256]{2,1,0:T(8,128)(2,1)S(1)} %slice.50), channel_id=1, source_target_pairs={{0,12},{1,5},{2,14},{3,7},{4,0},{5,9},{6,2},{7,11},{8,4},{9,13},{1... | collective-permute-start | bytes 442376 | tf_op jit(solution)/shard_map/ppermute | solution.py:182
  25.4 1.0 %fusion.7 = (bf16[1,1,16,16,256]{4,3,2,1,0:T(8,128)(2,1)S(1)}, bf16[1,1,16,16,256]{4,3,2,1,0:T(8,128)(2,1)S(1)}) fusion(bf16[2,1,16,16,256]{4,3,2,1,0:T(8,128)(2,1)} %param.5), kind=kLoop, calls=%fused_computation.19 | loop fusion | bytes 524288 | tf_op jit(solution)/shard_map/slice | solution.py:248
  26.5 1.7 %collective-permute-done.4.mine_2_ = bf16[2,144,256]{2,1,0:T(8,128)(2,1)S(1)} collective-permute-done((bf16[2,144,256]{2,1,0:T(8,128)(2,1)S(1)}, bf16[2,144,256]{2,1,0:T(8,128)(2,1)S(1)}, u32[]{:S(2)}, u32[]{:S(2)}) %collective-permute-start.4) | collective-permute-done | bytes 147488 | tf_op jit(solution)/shard_map/ppermute | solution.py:185
  28.3 3.2 %collective-permute-start.5 = (bf16[1,144,256]{2,1,0:T(8,128)(2,1)S(1)}, bf16[1,144,256]{2,1,0:T(8,128)(2,1)S(1)}, u32[]{:S(2)}, u32[]{:S(2)}) collective-permute-start(bf16[1,144,256]{2,1,0:T(8,128)(2,1)S(1)} %slice_select_fusion), channel_id=1, source_target_pairs={{0,14},{1,3},{2,0},{3,5},{4,2},{5,7},{6,4},{7,9},{8,6},{9,11},{10,... | collective-permute-start | bytes 221192 | tf_op jit(solution)/shard_map/ppermute | solution.py:182
  32.2 1.2 %collective-permute-done.5.mine_0_ = bf16[1,144,256]{2,1,0:T(8,128)(2,1)S(1)} collective-permute-done((bf16[1,144,256]{2,1,0:T(8,128)(2,1)S(1)}, bf16[1,144,256]{2,1,0:T(8,128)(2,1)S(1)}, u32[]{:S(2)}, u32[]{:S(2)}) %collective-permute-start.5) | collective-permute-done | bytes 73760 | tf_op jit(solution)/shard_map/ppermute | solution.py:182
  35.7 0.7 collective-permute-done.14.entering
  40.4 7.9 %collective-permute-start.18 = (bf16[256,256]{1,0:T(8,128)(2,1)S(1)}, bf16[256,256]{1,0:T(8,128)(2,1)S(1)}, u32[]{:S(2)}, u32[]{:S(2)}) collective-permute-start(bf16[256,256]{1,0:T(8,128)(2,1)S(1)} %shard_map.62.old), channel_id=1, source_target_pairs={{0,224},{1,225},{2,226},{3,227},{4,228},{5,229},{6,230},{7,231},{8... | collective-permute-start | bytes 393224 | tf_op jit(solution)/shard_map/ppermute | solution.py:259
  48.3 1.2 %collective-permute-start.25 = (bf16[256,256]{1,0:T(8,128)(2,1)S(1)}, bf16[256,256]{1,0:T(8,128)(2,1)S(1)}, u32[]{:S(2)}, u32[]{:S(2)}) collective-permute-start(bf16[256,256]{1,0:T(8,128)(2,1)S(1)} %shard_map.70.old), channel_id=1, source_target_pairs={{0,224},{1,225},{2,226},{3,227},{4,228},{5,229},{6,230},{7,231},{8... | collective-permute-start | bytes 393224 | tf_op jit(solution)/shard_map/ppermute | solution.py:259
  49.5 2.8 %collective-permute-done.18.entering.skip = bf16[256,256]{1,0:T(8,128)(2,1)S(1)} collective-permute-done((bf16[256,256]{1,0:T(8,128)(2,1)S(1)}, bf16[256,256]{1,0:T(8,128)(2,1)S(1)}, u32[]{:S(2)}, u32[]{:S(2)}) %collective-permute-start.18) | collective-permute-done | bytes 131104 | tf_op jit(solution)/shard_map/ppermute | solution.py:259
  52.3 3.6 %collective-permute-done.25.entering.skip = bf16[256,256]{1,0:T(8,128)(2,1)S(1)} collective-permute-done((bf16[256,256]{1,0:T(8,128)(2,1)S(1)}, bf16[256,256]{1,0:T(8,128)(2,1)S(1)}, u32[]{:S(2)}, u32[]{:S(2)}) %collective-permute-start.25) | collective-permute-done | bytes 131104 | tf_op jit(solution)/shard_map/ppermute | solution.py:259
  55.9 18.6 %collective-permute-start.20 = (bf16[256,256]{1,0:T(8,128)(2,1)S(1)}, bf16[256,256]{1,0:T(8,128)(2,1)S(1)}, u32[]{:S(2)}, u32[]{:S(2)}) collective-permute-start(bf16[256,256]{1,0:T(8,128)(2,1)S(1)} %shard_map.64.old), channel_id=1, source_target_pairs={{0,1},{1,0},{2,3},{3,2},{4,5},{5,4},{6,7},{7,6},{8,9},{9,8},{10,11... | collective-permute-start | bytes 393224 | tf_op jit(solution)/shard_map/ppermute | solution.py:259
  74.5 1.8 %collective-permute-start.27 = (bf16[256,256]{1,0:T(8,128)(2,1)S(1)}, bf16[256,256]{1,0:T(8,128)(2,1)S(1)}, u32[]{:S(2)}, u32[]{:S(2)}) collective-permute-start(bf16[256,256]{1,0:T(8,128)(2,1)S(1)} %shard_map.72.old), channel_id=1, source_target_pairs={{0,1},{1,0},{2,3},{3,2},{4,5},{5,4},{6,7},{7,6},{8,9},{9,8},{10,11... | collective-permute-start | bytes 393224 | tf_op jit(solution)/shard_map/ppermute | solution.py:259
  76.3 1.7 %collective-permute-done.20.entering = bf16[256,256]{1,0:T(8,128)(2,1)S(1)} collective-permute-done((bf16[256,256]{1,0:T(8,128)(2,1)S(1)}, bf16[256,256]{1,0:T(8,128)(2,1)S(1)}, u32[]{:S(2)}, u32[]{:S(2)}) %collective-permute-start.20) | collective-permute-done | bytes 131104 | tf_op jit(solution)/shard_map/ppermute | solution.py:259
  78.0 1.6 %shard_map.65 = bf16[256,256]{1,0:T(8,128)(2,1)S(1)} custom-call(bf16[256,256]{1,0:T(8,128)(2,1)S(1)} %collective-permute-done.20.entering, bf16[256,256]{1,0:T(8,128)(2,1)S(1)} %collective-permute-done.18.entering.skip, f32[1,512]{1,0:T(1,128)S(1)} %get-tuple-element.21.modulation, bf16[4608,256]{1,0:T(8,128)(2,1)S(1)} %bitcast.30, ...), custom_call_target="tpu_custom_call", output_to_operand_aliasing={{}: (4, {})} | custom-call | flops 603979776 | bytes 3000000 | tf_op jit(solution)/shard_map/pallas_call | solution.py:101
  79.6 1.6 %shard_map.73 = bf16[256,256]{1,0:T(8,128)(2,1)S(1)} custom-call(bf16[256,256]{1,0:T(8,128)(2,1)S(1)} %collective-permute-done.27.entering, bf16[256,256]{1,0:T(8,128)(2,1)S(1)} %collective-permute-done.25.entering.skip, f32[1,512]{1,0:T(1,128)S(1)} %get-tuple-element.22.modulation, bf16[4608,256]{1,0:T(8,128)(2,1)S(1)} %bitcast.31, ...), custom_call_target="tpu_custom_call", output_to_operand_aliasing={{}: (4, {})} | custom-call | flops 603979776 | bytes 3000000 | tf_op jit(solution)/shard_map/pallas_call | solution.py:101
  81.1 0.7 pad_maximum_fusion.1
  (78 shorter events, 8.3 us)
Async XLA Ops:
  0.0 1.6 %collective-permute-start = (bf16[2,72,256]{2,1,0:T(8,128)(2,1)}, bf16[2,72,256]{2,1,0:T(8,128)(2,1)S(1)}, u32[]{:S(2)}, u32[]{:S(2)}) collective-permute-start(bf16[2,72,256]{2,1,0:T(8,128)(2,1)} %bitcast.38), channel_id=1, source_target_pairs={{0,1},{1,0},{2,3},{3,2},{4,5},{5,4},{6,7},{7,6},{8,9},{9,8},{10,11... | collective-permute-start | bytes 221192 | tf_op jit(solution)/shard_map/ppermute | solution.py:188
  2.5 13.2 %collective-permute-start.1 = (bf16[2,144,256]{2,1,0:T(8,128)(2,1)S(1)}, bf16[2,144,256]{2,1,0:T(8,128)(2,1)S(1)}, u32[]{:S(2)}, u32[]{:S(2)}) collective-permute-start(bf16[2,144,256]{2,1,0:T(8,128)(2,1)S(1)} %pad_maximum_fusion.2), channel_id=1, source_target_pairs={{0,10},{1,7},{2,12},{3,9},{4,14},{5,11},{6,0},{7,13},{8,2},{9,15},... | collective-permute-start | bytes 442376 | tf_op jit(solution)/shard_map/ppermute | solution.py:182
  9.3 6.7 %collective-permute-start.3 = (bf16[2,144,256]{2,1,0:T(8,128)(2,1)S(1)}, bf16[2,144,256]{2,1,0:T(8,128)(2,1)S(1)}, u32[]{:S(2)}, u32[]{:S(2)}) collective-permute-start(bf16[2,144,256]{2,1,0:T(8,128)(2,1)S(1)} %pad_maximum_fusion.2), channel_id=1, source_target_pairs={{0,16},{1,17},{2,18},{3,19},{4,20},{5,21},{6,22},{7,23},{8,24},{9,... | collective-permute-start | bytes 442376 | tf_op jit(solution)/shard_map/ppermute | solution.py:185
  11.5 7.6 %collective-permute-start.2 = (bf16[2,144,256]{2,1,0:T(8,128)(2,1)S(1)}, bf16[2,144,256]{2,1,0:T(8,128)(2,1)S(1)}, u32[]{:S(2)}, u32[]{:S(2)}) collective-permute-start(bf16[2,144,256]{2,1,0:T(8,128)(2,1)S(1)} %pad_maximum_fusion.2), channel_id=1, source_target_pairs={{0,12},{1,5},{2,14},{3,7},{4,0},{5,9},{6,2},{7,11},{8,4},{9,13},{1... | collective-permute-start | bytes 442376 | tf_op jit(solution)/shard_map/ppermute | solution.py:182
  19.1 12.4 %collective-permute-start.7 = (bf16[5,144,256]{2,1,0:T(8,128)(2,1)S(1)}, bf16[5,144,256]{2,1,0:T(8,128)(2,1)S(1)}, u32[]{:S(2)}, u32[]{:S(2)}) collective-permute-start(bf16[5,144,256]{2,1,0:T(8,128)(2,1)S(1)} %pad_maximum_fusion), channel_id=1, source_target_pairs={{0,14},{1,3},{2,0},{3,5},{4,2},{5,7},{6,4},{7,9},{8,6},{9,11},{10,... | collective-permute-start | bytes 1105928 | tf_op jit(solution)/shard_map/ppermute | solution.py:182
  20.4 13.4 %collective-permute-start.13 = (bf16[2,144,256]{2,1,0:T(8,128)(2,1)S(1)}, bf16[2,144,256]{2,1,0:T(8,128)(2,1)S(1)}, u32[]{:S(2)}, u32[]{:S(2)}) collective-permute-start(bf16[2,144,256]{2,1,0:T(8,128)(2,1)S(1)} %collective-permute-done.1.mine_2_), channel_id=1, source_target_pairs={{0,1},{1,0},{2,3},{3,2},{4,5},{5,4},{6,7},{7,6},{8,9},{9,8},{10,11... | collective-permute-start | bytes 442376 | tf_op jit(solution)/shard_map/ppermute | solution.py:188
  20.5 7.8 %collective-permute-start.4 = (bf16[2,144,256]{2,1,0:T(8,128)(2,1)S(1)}, bf16[2,144,256]{2,1,0:T(8,128)(2,1)S(1)}, u32[]{:S(2)}, u32[]{:S(2)}) collective-permute-start(bf16[2,144,256]{2,1,0:T(8,128)(2,1)S(1)} %collective-permute-done.1.mine_2_), channel_id=1, source_target_pairs={{0,16},{1,17},{2,18},{3,19},{4,20},{5,21},{6,22},{7,23},{8,24},{9,... | collective-permute-start | bytes 442376 | tf_op jit(solution)/shard_map/ppermute | solution.py:185
  21.8 9.8 %collective-permute-start.12 = (bf16[2,144,256]{2,1,0:T(8,128)(2,1)S(1)}, bf16[2,144,256]{2,1,0:T(8,128)(2,1)S(1)}, u32[]{:S(2)}, u32[]{:S(2)}) collective-permute-start(bf16[2,144,256]{2,1,0:T(8,128)(2,1)S(1)} %collective-permute-done.2.mine_1_), channel_id=1, source_target_pairs={{0,1},{1,0},{2,3},{3,2},{4,5},{5,4},{6,7},{7,6},{8,9},{9,8},{10,11... | collective-permute-start | bytes 442376 | tf_op jit(solution)/shard_map/ppermute | solution.py:188
  22.0 10.1 %collective-permute-start.8 = (bf16[2,144,256]{2,1,0:T(8,128)(2,1)S(1)}, bf16[2,144,256]{2,1,0:T(8,128)(2,1)S(1)}, u32[]{:S(2)}, u32[]{:S(2)}) collective-permute-start(bf16[2,144,256]{2,1,0:T(8,128)(2,1)S(1)} %slice.50), channel_id=1, source_target_pairs={{0,12},{1,5},{2,14},{3,7},{4,0},{5,9},{6,2},{7,11},{8,4},{9,13},{1... | collective-permute-start | bytes 442376 | tf_op jit(solution)/shard_map/ppermute | solution.py:182
  28.3 5.1 %collective-permute-start.5 = (bf16[1,144,256]{2,1,0:T(8,128)(2,1)S(1)}, bf16[1,144,256]{2,1,0:T(8,128)(2,1)S(1)}, u32[]{:S(2)}, u32[]{:S(2)}) collective-permute-start(bf16[1,144,256]{2,1,0:T(8,128)(2,1)S(1)} %slice_select_fusion), channel_id=1, source_target_pairs={{0,14},{1,3},{2,0},{3,5},{4,2},{5,7},{6,4},{7,9},{8,6},{9,11},{10,... | collective-permute-start | bytes 221192 | tf_op jit(solution)/shard_map/ppermute | solution.py:182
  31.4 2.7 %collective-permute-start.9 = (bf16[5,144,256]{2,1,0:T(8,128)(2,1)S(1)}, bf16[5,144,256]{2,1,0:T(8,128)(2,1)S(1)}, u32[]{:S(2)}, u32[]{:S(2)}) collective-permute-start(bf16[5,144,256]{2,1,0:T(8,128)(2,1)S(1)} %collective-permute-done.7.mine_0_), channel_id=1, source_target_pairs={{0,1},{1,0},{2,3},{3,2},{4,5},{5,4},{6,7},{7,6},{8,9},{9,8},{10,11... | collective-permute-start | bytes 1105928 | tf_op jit(solution)/shard_map/ppermute | solution.py:188
  31.6 2.6 %collective-permute-start.11 = (bf16[2,144,256]{2,1,0:T(8,128)(2,1)S(1)}, bf16[2,144,256]{2,1,0:T(8,128)(2,1)S(1)}, u32[]{:S(2)}, u32[]{:S(2)}) collective-permute-start(bf16[2,144,256]{2,1,0:T(8,128)(2,1)S(1)} %collective-permute-done.4.mine_2_), channel_id=1, source_target_pairs={{0,1},{1,0},{2,3},{3,2},{4,5},{5,4},{6,7},{7,6},{8,9},{9,8},{10,11... | collective-permute-start | bytes 442376 | tf_op jit(solution)/shard_map/ppermute | solution.py:188
  32.1 2.0 %collective-permute-start.10 = (bf16[2,144,256]{2,1,0:T(8,128)(2,1)S(1)}, bf16[2,144,256]{2,1,0:T(8,128)(2,1)S(1)}, u32[]{:S(2)}, u32[]{:S(2)}) collective-permute-start(bf16[2,144,256]{2,1,0:T(8,128)(2,1)S(1)} %collective-permute-done.8.mine_1_), channel_id=1, source_target_pairs={{0,1},{1,0},{2,3},{3,2},{4,5},{5,4},{6,7},{7,6},{8,9},{9,8},{10,11... | collective-permute-start | bytes 442376 | tf_op jit(solution)/shard_map/ppermute | solution.py:188
  34.8 1.6 %collective-permute-start.14 = (bf16[256,256]{1,0:T(8,128)(2,1)S(1)}, bf16[256,256]{1,0:T(8,128)(2,1)S(1)}, u32[]{:S(2)}, u32[]{:S(2)}) collective-permute-start(bf16[256,256]{1,0:T(8,128)(2,1)S(1)} %shard_map.58.old), channel_id=1, source_target_pairs={{0,32},{1,33},{2,34},{3,35},{4,36},{5,37},{6,38},{7,39},{8,40},{9,... | collective-permute-start | bytes 393224 | tf_op jit(solution)/shard_map/ppermute | solution.py:259
  35.4 1.4 %collective-permute-start.21 = (bf16[256,256]{1,0:T(8,128)(2,1)S(1)}, bf16[256,256]{1,0:T(8,128)(2,1)S(1)}, u32[]{:S(2)}, u32[]{:S(2)}) collective-permute-start(bf16[256,256]{1,0:T(8,128)(2,1)S(1)} %shard_map.66.old), channel_id=1, source_target_pairs={{0,32},{1,33},{2,34},{3,35},{4,36},{5,37},{6,38},{7,39},{8,40},{9,... | collective-permute-start | bytes 393224 | tf_op jit(solution)/shard_map/ppermute | solution.py:259
  36.4 1.3 %collective-permute-start.15 = (bf16[256,256]{1,0:T(8,128)(2,1)S(1)}, bf16[256,256]{1,0:T(8,128)(2,1)S(1)}, u32[]{:S(2)}, u32[]{:S(2)}) collective-permute-start(bf16[256,256]{1,0:T(8,128)(2,1)S(1)} %shard_map.59.old), channel_id=1, source_target_pairs={{0,1},{1,0},{2,3},{3,2},{4,5},{5,4},{6,7},{7,6},{8,9},{9,8},{10,11... | collective-permute-start | bytes 393224 | tf_op jit(solution)/shard_map/ppermute | solution.py:259
  36.7 1.3 %collective-permute-start.22 = (bf16[256,256]{1,0:T(8,128)(2,1)S(1)}, bf16[256,256]{1,0:T(8,128)(2,1)S(1)}, u32[]{:S(2)}, u32[]{:S(2)}) collective-permute-start(bf16[256,256]{1,0:T(8,128)(2,1)S(1)} %shard_map.67.old), channel_id=1, source_target_pairs={{0,1},{1,0},{2,3},{3,2},{4,5},{5,4},{6,7},{7,6},{8,9},{9,8},{10,11... | collective-permute-start | bytes 393224 | tf_op jit(solution)/shard_map/ppermute | solution.py:259
  39.4 8.9 %collective-permute-start.24 = (bf16[256,256]{1,0:T(8,128)(2,1)S(1)}, bf16[256,256]{1,0:T(8,128)(2,1)S(1)}, u32[]{:S(2)}, u32[]{:S(2)}) collective-permute-start(bf16[256,256]{1,0:T(8,128)(2,1)S(1)} %shard_map.69.old), channel_id=1, source_target_pairs={{0,1},{1,0},{2,3},{3,2},{4,5},{5,4},{6,7},{7,6},{8,9},{9,8},{10,11... | collective-permute-start | bytes 393224 | tf_op jit(solution)/shard_map/ppermute | solution.py:259
  40.4 11.9 %collective-permute-start.18 = (bf16[256,256]{1,0:T(8,128)(2,1)S(1)}, bf16[256,256]{1,0:T(8,128)(2,1)S(1)}, u32[]{:S(2)}, u32[]{:S(2)}) collective-permute-start(bf16[256,256]{1,0:T(8,128)(2,1)S(1)} %shard_map.62.old), channel_id=1, source_target_pairs={{0,224},{1,225},{2,226},{3,227},{4,228},{5,229},{6,230},{7,231},{8... | collective-permute-start | bytes 393224 | tf_op jit(solution)/shard_map/ppermute | solution.py:259
  48.3 7.6 %collective-permute-start.25 = (bf16[256,256]{1,0:T(8,128)(2,1)S(1)}, bf16[256,256]{1,0:T(8,128)(2,1)S(1)}, u32[]{:S(2)}, u32[]{:S(2)}) collective-permute-start(bf16[256,256]{1,0:T(8,128)(2,1)S(1)} %shard_map.70.old), channel_id=1, source_target_pairs={{0,224},{1,225},{2,226},{3,227},{4,228},{5,229},{6,230},{7,231},{8... | collective-permute-start | bytes 393224 | tf_op jit(solution)/shard_map/ppermute | solution.py:259
  52.3 3.6 %collective-permute-start.19 = (bf16[256,256]{1,0:T(8,128)(2,1)S(1)}, bf16[256,256]{1,0:T(8,128)(2,1)S(1)}, u32[]{:S(2)}, u32[]{:S(2)}) collective-permute-start(bf16[256,256]{1,0:T(8,128)(2,1)S(1)} %shard_map.63.old), channel_id=1, source_target_pairs={{0,1},{1,0},{2,3},{3,2},{4,5},{5,4},{6,7},{7,6},{8,9},{9,8},{10,11... | collective-permute-start | bytes 393224 | tf_op jit(solution)/shard_map/ppermute | solution.py:259
  55.9 18.6 %collective-permute-start.26 = (bf16[256,256]{1,0:T(8,128)(2,1)S(1)}, bf16[256,256]{1,0:T(8,128)(2,1)S(1)}, u32[]{:S(2)}, u32[]{:S(2)}) collective-permute-start(bf16[256,256]{1,0:T(8,128)(2,1)S(1)} %shard_map.71.old), channel_id=1, source_target_pairs={{0,1},{1,0},{2,3},{3,2},{4,5},{5,4},{6,7},{7,6},{8,9},{9,8},{10,11... | collective-permute-start | bytes 393224 | tf_op jit(solution)/shard_map/ppermute | solution.py:259
  55.9 22.1 %collective-permute-start.20 = (bf16[256,256]{1,0:T(8,128)(2,1)S(1)}, bf16[256,256]{1,0:T(8,128)(2,1)S(1)}, u32[]{:S(2)}, u32[]{:S(2)}) collective-permute-start(bf16[256,256]{1,0:T(8,128)(2,1)S(1)} %shard_map.64.old), channel_id=1, source_target_pairs={{0,1},{1,0},{2,3},{3,2},{4,5},{5,4},{6,7},{7,6},{8,9},{9,8},{10,11... | collective-permute-start | bytes 393224 | tf_op jit(solution)/shard_map/ppermute | solution.py:259
  74.5 5.1 %collective-permute-start.27 = (bf16[256,256]{1,0:T(8,128)(2,1)S(1)}, bf16[256,256]{1,0:T(8,128)(2,1)S(1)}, u32[]{:S(2)}, u32[]{:S(2)}) collective-permute-start(bf16[256,256]{1,0:T(8,128)(2,1)S(1)} %shard_map.72.old), channel_id=1, source_target_pairs={{0,1},{1,0},{2,3},{3,2},{4,5},{5,4},{6,7},{7,6},{8,9},{9,8},{10,11... | collective-permute-start | bytes 393224 | tf_op jit(solution)/shard_map/ppermute | solution.py:259
  (7 other events, 96.6 us)

commit v5 on v4

--- a/solution.py
+++ b/solution.py
@@ -262,7 +262,10 @@
         if step == half:
             far = sent
         entering = sent
-    return jnp.stack(outs).reshape((1, micros, 1, SIDE, SIDE, channels))
+    whole = features.reshape(micros, pixels, channels)
+    for m in range(micros):
+        whole = lax.dynamic_update_index_in_dim(whole, outs[m], m, 0)
+    return whole.reshape((1, micros, 1, SIDE, SIDE, channels))
 
 
 def solution(mesh):

time: 82.1 us -> 83.2 us (1.013)
  waiting for transfers between devices: 22.3 us -> 23.7 us
    optimization_barrier x0 -> x1, local copies, waits for them, and re-layouts: none -> 1 us  [gathered_weights(): lax.optimization_barrier((third, second, column, scales, features, timest...]
    ppermute x2, waiting for transfers between devices: 1.98 us -> 2.95 us  [facing_side(): return lax.ppermute(value, 'dp', [(i, i ^ 2 * RING) for i in range(count)])]
    slice x1, local copies, waits for them, and re-layouts: 0.98 us -> 0.02 us  [shards(): entering = [features[m].reshape(pixels, channels) for m in range(micros)]]
  transfers between devices with their start and end apart: 28 -> 28, of which waited for: 13 -> 17; matrix products, arithmetic and copies ran while one was open for 2% -> 1% of each run, Pallas kernels for 3% -> 3%
where the time goes in v5:
time: 83.2 us; the launch traced here: 82.9 us
  starting transfers between devices  51.4 us (62%)
  waiting for transfers between devices  23.7 us (28%)
  Pallas kernels  4.23 us (5%)
  local copies, waits for them, and re-layouts  2.07 us (2%)
  other arithmetic  1.08 us (1%)
    ppermute x14, starting transfers between devices, shards(): lax.ppermute(outs[m], ('section', 'dp'), route(step, sections, count))  31.8 us
    ppermute x5, starting transfers between devices, along_ring(): lax.ppermute(value, 'dp', [(i, onward(i, hops)) for i in range(count)])  15.2 us
    ppermute x14, waiting for transfers between devices, shards(): lax.ppermute(outs[m], ('section', 'dp'), route(step, sections, count))  11.3 us
    ppermute x5, waiting for transfers between devices, along_ring(): lax.ppermute(value, 'dp', [(i, onward(i, hops)) for i in range(count)])  8.01 us
    ppermute x2, starting transfers between devices, facing_side(): return lax.ppermute(value, 'dp', [(i, i ^ 2 * RING) for i in range(count)])  3.47 us
    pallas_call x16, Pallas kernels, res_block(): pl.pallas_call(functools.partial(block_kernel, step), out_shape=jax.Shape...  3.35 us
    ppermute x2, waiting for transfers between devices, facing_side(): return lax.ppermute(value, 'dp', [(i, i ^ 2 * RING) for i in range(count)])  2.95 us
  transfers between devices with their start and end apart: 28, of which 17 were waited for; matrix products, arithmetic and copies ran while one was open for 1% of the time, Pallas kernels for 3%

profile of v5, /device:TPU:26, one launch (start us, length us, event | category | flops | bytes accessed | tf_op | source)
XLA Modules:
  0.0 82.9 jit_solution(6650492326079991205)
XLA Ops:
  0.0 1.0 %copy.51 = bf16[2,1,16,16,256]{4,3,2,1,0:T(8,128)(2,1)S(1)} copy(bf16[2,1,16,16,256]{4,3,2,1,0:T(8,128)(2,1)} %param.5) | data formatting | bytes 524288 | tf_op jit(solution)/shard_map/optimization_barrier | solution.py:201
  1.0 1.5 %collective-permute-done = bf16[2,72,256]{2,1,0:T(8,128)(2,1)S(1)} collective-permute-done((bf16[2,72,256]{2,1,0:T(8,128)(2,1)}, bf16[2,72,256]{2,1,0:T(8,128)(2,1)S(1)}, u32[]{:S(2)}, u32[]{:S(2)}) %collective-permute-start) | collective-permute-done | bytes 73760 | tf_op jit(solution)/shard_map/ppermute | solution.py:188
  2.5 0.9 %broadcast_select_fusion.1 = (bf16[2,72,256]{2,1,0:T(8,128)(2,1)S(1)}, bf16[2,72,256]{2,1,0:T(8,128)(2,1)S(1)}) fusion(bf16[2,72,256]{2,1,0:T(8,128)(2,1)S(1)} %collective-permute-done, pred[]{:T(512)S(6)} %eq.4, bf16[1,2,72,256]{3,2,1,0:T(8,128)(2,1)} %param.7), kind=kLoop, calls=%fused_computation.9 | loop fusion | flops 73728 | bytes 294913 | tf_op jit(solution)/shard_map/jit(_where)/select_n | solution.py:194
  3.4 6.8 %collective-permute-start.1 = (bf16[2,144,256]{2,1,0:T(8,128)(2,1)S(1)}, bf16[2,144,256]{2,1,0:T(8,128)(2,1)S(1)}, u32[]{:S(2)}, u32[]{:S(2)}) collective-permute-start(bf16[2,144,256]{2,1,0:T(8,128)(2,1)S(1)} %pad_maximum_fusion.1), channel_id=1, source_target_pairs={{0,10},{1,7},{2,12},{3,9},{4,14},{5,11},{6,0},{7,13},{8,2},{9,15},... | collective-permute-start | bytes 442376 | tf_op jit(solution)/shard_map/ppermute | solution.py:182
  10.2 2.1 %collective-permute-start.3 = (bf16[2,144,256]{2,1,0:T(8,128)(2,1)S(1)}, bf16[2,144,256]{2,1,0:T(8,128)(2,1)S(1)}, u32[]{:S(2)}, u32[]{:S(2)}) collective-permute-start(bf16[2,144,256]{2,1,0:T(8,128)(2,1)S(1)} %pad_maximum_fusion.1), channel_id=1, source_target_pairs={{0,16},{1,17},{2,18},{3,19},{4,20},{5,21},{6,22},{7,23},{8,24},{9,... | collective-permute-start | bytes 442376 | tf_op jit(solution)/shard_map/ppermute | solution.py:185
  12.9 3.7 %collective-permute-done.1.mine_2_ = bf16[2,144,256]{2,1,0:T(8,128)(2,1)S(1)} collective-permute-done((bf16[2,144,256]{2,1,0:T(8,128)(2,1)S(1)}, bf16[2,144,256]{2,1,0:T(8,128)(2,1)S(1)}, u32[]{:S(2)}, u32[]{:S(2)}) %collective-permute-start.1) | collective-permute-done | bytes 147488 | tf_op jit(solution)/shard_map/ppermute | solution.py:182
  16.9 3.1 %collective-permute-done.2.mine_1_ = bf16[2,144,256]{2,1,0:T(8,128)(2,1)S(1)} collective-permute-done((bf16[2,144,256]{2,1,0:T(8,128)(2,1)S(1)}, bf16[2,144,256]{2,1,0:T(8,128)(2,1)S(1)}, u32[]{:S(2)}, u32[]{:S(2)}) %collective-permute-start.2) | collective-permute-done | bytes 147488 | tf_op jit(solution)/shard_map/ppermute | solution.py:182
  20.0 1.3 %collective-permute-start.7 = (bf16[5,144,256]{2,1,0:T(8,128)(2,1)S(1)}, bf16[5,144,256]{2,1,0:T(8,128)(2,1)S(1)}, u32[]{:S(2)}, u32[]{:S(2)}) collective-permute-start(bf16[5,144,256]{2,1,0:T(8,128)(2,1)S(1)} %pad_maximum_fusion), channel_id=1, source_target_pairs={{0,14},{1,3},{2,0},{3,5},{4,2},{5,7},{6,4},{7,9},{8,6},{9,11},{10,... | collective-permute-start | bytes 1105928 | tf_op jit(solution)/shard_map/ppermute | solution.py:182
  21.4 1.3 %collective-permute-start.4 = (bf16[2,144,256]{2,1,0:T(8,128)(2,1)S(1)}, bf16[2,144,256]{2,1,0:T(8,128)(2,1)S(1)}, u32[]{:S(2)}, u32[]{:S(2)}) collective-permute-start(bf16[2,144,256]{2,1,0:T(8,128)(2,1)S(1)} %collective-permute-done.1.mine_2_), channel_id=1, source_target_pairs={{0,16},{1,17},{2,18},{3,19},{4,20},{5,21},{6,22},{7,23},{8,24},{9,... | collective-permute-start | bytes 442376 | tf_op jit(solution)/shard_map/ppermute | solution.py:185
  22.9 3.4 %collective-permute-start.8 = (bf16[2,144,256]{2,1,0:T(8,128)(2,1)S(1)}, bf16[2,144,256]{2,1,0:T(8,128)(2,1)S(1)}, u32[]{:S(2)}, u32[]{:S(2)}) collective-permute-start(bf16[2,144,256]{2,1,0:T(8,128)(2,1)S(1)} %slice.50), channel_id=1, source_target_pairs={{0,12},{1,5},{2,14},{3,7},{4,0},{5,9},{6,2},{7,11},{8,4},{9,13},{1... | collective-permute-start | bytes 442376 | tf_op jit(solution)/shard_map/ppermute | solution.py:182
  26.5 2.7 %collective-permute-done.4.mine_2_ = bf16[2,144,256]{2,1,0:T(8,128)(2,1)S(1)} collective-permute-done((bf16[2,144,256]{2,1,0:T(8,128)(2,1)S(1)}, bf16[2,144,256]{2,1,0:T(8,128)(2,1)S(1)}, u32[]{:S(2)}, u32[]{:S(2)}) %collective-permute-start.4) | collective-permute-done | bytes 147488 | tf_op jit(solution)/shard_map/ppermute | solution.py:185
  29.2 3.2 %collective-permute-start.5 = (bf16[1,144,256]{2,1,0:T(8,128)(2,1)S(1)}, bf16[1,144,256]{2,1,0:T(8,128)(2,1)S(1)}, u32[]{:S(2)}, u32[]{:S(2)}) collective-permute-start(bf16[1,144,256]{2,1,0:T(8,128)(2,1)S(1)} %slice_select_fusion), channel_id=1, source_target_pairs={{0,14},{1,3},{2,0},{3,5},{4,2},{5,7},{6,4},{7,9},{8,6},{9,11},{10,... | collective-permute-start | bytes 221192 | tf_op jit(solution)/shard_map/ppermute | solution.py:182
  33.1 1.2 %collective-permute-done.5.mine_0_ = bf16[1,144,256]{2,1,0:T(8,128)(2,1)S(1)} collective-permute-done((bf16[1,144,256]{2,1,0:T(8,128)(2,1)S(1)}, bf16[1,144,256]{2,1,0:T(8,128)(2,1)S(1)}, u32[]{:S(2)}, u32[]{:S(2)}) %collective-permute-start.5) | collective-permute-done | bytes 73760 | tf_op jit(solution)/shard_map/ppermute | solution.py:182
  36.6 0.7 collective-permute-done.14.entering
  41.3 7.9 %collective-permute-start.18 = (bf16[256,256]{1,0:T(8,128)(2,1)S(1)}, bf16[256,256]{1,0:T(8,128)(2,1)S(1)}, u32[]{:S(2)}, u32[]{:S(2)}) collective-permute-start(bf16[256,256]{1,0:T(8,128)(2,1)S(1)} %shard_map.62.old), channel_id=1, source_target_pairs={{0,224},{1,225},{2,226},{3,227},{4,228},{5,229},{6,230},{7,231},{8... | collective-permute-start | bytes 393224 | tf_op jit(solution)/shard_map/ppermute | solution.py:259
  49.2 1.2 %collective-permute-start.25 = (bf16[256,256]{1,0:T(8,128)(2,1)S(1)}, bf16[256,256]{1,0:T(8,128)(2,1)S(1)}, u32[]{:S(2)}, u32[]{:S(2)}) collective-permute-start(bf16[256,256]{1,0:T(8,128)(2,1)S(1)} %shard_map.70.old), channel_id=1, source_target_pairs={{0,224},{1,225},{2,226},{3,227},{4,228},{5,229},{6,230},{7,231},{8... | collective-permute-start | bytes 393224 | tf_op jit(solution)/shard_map/ppermute | solution.py:259
  50.4 2.8 %collective-permute-done.18.entering.skip = bf16[256,256]{1,0:T(8,128)(2,1)S(1)} collective-permute-done((bf16[256,256]{1,0:T(8,128)(2,1)S(1)}, bf16[256,256]{1,0:T(8,128)(2,1)S(1)}, u32[]{:S(2)}, u32[]{:S(2)}) %collective-permute-start.18) | collective-permute-done | bytes 131104 | tf_op jit(solution)/shard_map/ppermute | solution.py:259
  53.2 3.6 %collective-permute-done.25.entering.skip = bf16[256,256]{1,0:T(8,128)(2,1)S(1)} collective-permute-done((bf16[256,256]{1,0:T(8,128)(2,1)S(1)}, bf16[256,256]{1,0:T(8,128)(2,1)S(1)}, u32[]{:S(2)}, u32[]{:S(2)}) %collective-permute-start.25) | collective-permute-done | bytes 131104 | tf_op jit(solution)/shard_map/ppermute | solution.py:259
  56.8 18.8 %collective-permute-start.20 = (bf16[256,256]{1,0:T(8,128)(2,1)S(1)}, bf16[256,256]{1,0:T(8,128)(2,1)S(1)}, u32[]{:S(2)}, u32[]{:S(2)}) collective-permute-start(bf16[256,256]{1,0:T(8,128)(2,1)S(1)} %shard_map.64.old), channel_id=1, source_target_pairs={{0,1},{1,0},{2,3},{3,2},{4,5},{5,4},{6,7},{7,6},{8,9},{9,8},{10,11... | collective-permute-start | bytes 393224 | tf_op jit(solution)/shard_map/ppermute | solution.py:259
  75.6 1.7 %collective-permute-start.27 = (bf16[256,256]{1,0:T(8,128)(2,1)S(1)}, bf16[256,256]{1,0:T(8,128)(2,1)S(1)}, u32[]{:S(2)}, u32[]{:S(2)}) collective-permute-start(bf16[256,256]{1,0:T(8,128)(2,1)S(1)} %shard_map.72.old), channel_id=1, source_target_pairs={{0,1},{1,0},{2,3},{3,2},{4,5},{5,4},{6,7},{7,6},{8,9},{9,8},{10,11... | collective-permute-start | bytes 393224 | tf_op jit(solution)/shard_map/ppermute | solution.py:259
  77.3 1.6 %collective-permute-done.20.entering = bf16[256,256]{1,0:T(8,128)(2,1)S(1)} collective-permute-done((bf16[256,256]{1,0:T(8,128)(2,1)S(1)}, bf16[256,256]{1,0:T(8,128)(2,1)S(1)}, u32[]{:S(2)}, u32[]{:S(2)}) %collective-permute-start.20) | collective-permute-done | bytes 131104 | tf_op jit(solution)/shard_map/ppermute | solution.py:259
  78.9 1.6 %shard_map.65 = bf16[256,256]{1,0:T(8,128)(2,1)S(1)} custom-call(bf16[256,256]{1,0:T(8,128)(2,1)S(1)} %collective-permute-done.20.entering, bf16[256,256]{1,0:T(8,128)(2,1)S(1)} %collective-permute-done.18.entering.skip, f32[1,512]{1,0:T(1,128)S(1)} %get-tuple-element.22.modulation, bf16[4608,256]{1,0:T(8,128)(2,1)S(1)} %bitcast.34, ...), custom_call_target="tpu_custom_call", output_to_operand_aliasing={{}: (4, {})} | custom-call | flops 603979776 | bytes 3000000 | tf_op jit(solution)/shard_map/pallas_call | solution.py:101
  80.6 1.6 %shard_map.73 = bf16[256,256]{1,0:T(8,128)(2,1)S(1)} custom-call(bf16[256,256]{1,0:T(8,128)(2,1)S(1)} %collective-permute-done.27.entering, bf16[256,256]{1,0:T(8,128)(2,1)S(1)} %collective-permute-done.25.entering.skip, f32[1,512]{1,0:T(1,128)S(1)} %get-tuple-element.21.modulation, bf16[4608,256]{1,0:T(8,128)(2,1)S(1)} %bitcast.35, ...), custom_call_target="tpu_custom_call", output_to_operand_aliasing={{}: (4, {})} | custom-call | flops 603979776 | bytes 3000000 | tf_op jit(solution)/shard_map/pallas_call | solution.py:101
  82.2 0.7 copy-done.1
  (82 shorter events, 8.4 us)
Async XLA Ops:
  1.0 1.5 %collective-permute-start = (bf16[2,72,256]{2,1,0:T(8,128)(2,1)}, bf16[2,72,256]{2,1,0:T(8,128)(2,1)S(1)}, u32[]{:S(2)}, u32[]{:S(2)}) collective-permute-start(bf16[2,72,256]{2,1,0:T(8,128)(2,1)} %bitcast.41), channel_id=1, source_target_pairs={{0,1},{1,0},{2,3},{3,2},{4,5},{5,4},{6,7},{7,6},{8,9},{9,8},{10,11... | collective-permute-start | bytes 221192 | tf_op jit(solution)/shard_map/ppermute | solution.py:188
  3.4 13.2 %collective-permute-start.1 = (bf16[2,144,256]{2,1,0:T(8,128)(2,1)S(1)}, bf16[2,144,256]{2,1,0:T(8,128)(2,1)S(1)}, u32[]{:S(2)}, u32[]{:S(2)}) collective-permute-start(bf16[2,144,256]{2,1,0:T(8,128)(2,1)S(1)} %pad_maximum_fusion.1), channel_id=1, source_target_pairs={{0,10},{1,7},{2,12},{3,9},{4,14},{5,11},{6,0},{7,13},{8,2},{9,15},... | collective-permute-start | bytes 442376 | tf_op jit(solution)/shard_map/ppermute | solution.py:182
  10.2 6.7 %collective-permute-start.3 = (bf16[2,144,256]{2,1,0:T(8,128)(2,1)S(1)}, bf16[2,144,256]{2,1,0:T(8,128)(2,1)S(1)}, u32[]{:S(2)}, u32[]{:S(2)}) collective-permute-start(bf16[2,144,256]{2,1,0:T(8,128)(2,1)S(1)} %pad_maximum_fusion.1), channel_id=1, source_target_pairs={{0,16},{1,17},{2,18},{3,19},{4,20},{5,21},{6,22},{7,23},{8,24},{9,... | collective-permute-start | bytes 442376 | tf_op jit(solution)/shard_map/ppermute | solution.py:185
  12.4 7.6 %collective-permute-start.2 = (bf16[2,144,256]{2,1,0:T(8,128)(2,1)S(1)}, bf16[2,144,256]{2,1,0:T(8,128)(2,1)S(1)}, u32[]{:S(2)}, u32[]{:S(2)}) collective-permute-start(bf16[2,144,256]{2,1,0:T(8,128)(2,1)S(1)} %pad_maximum_fusion.1), channel_id=1, source_target_pairs={{0,12},{1,5},{2,14},{3,7},{4,0},{5,9},{6,2},{7,11},{8,4},{9,13},{1... | collective-permute-start | bytes 442376 | tf_op jit(solution)/shard_map/ppermute | solution.py:182
  20.0 12.4 %collective-permute-start.7 = (bf16[5,144,256]{2,1,0:T(8,128)(2,1)S(1)}, bf16[5,144,256]{2,1,0:T(8,128)(2,1)S(1)}, u32[]{:S(2)}, u32[]{:S(2)}) collective-permute-start(bf16[5,144,256]{2,1,0:T(8,128)(2,1)S(1)} %pad_maximum_fusion), channel_id=1, source_target_pairs={{0,14},{1,3},{2,0},{3,5},{4,2},{5,7},{6,4},{7,9},{8,6},{9,11},{10,... | collective-permute-start | bytes 1105928 | tf_op jit(solution)/shard_map/ppermute | solution.py:182
  21.3 13.4 %collective-permute-start.13 = (bf16[2,144,256]{2,1,0:T(8,128)(2,1)S(1)}, bf16[2,144,256]{2,1,0:T(8,128)(2,1)S(1)}, u32[]{:S(2)}, u32[]{:S(2)}) collective-permute-start(bf16[2,144,256]{2,1,0:T(8,128)(2,1)S(1)} %collective-permute-done.1.mine_2_), channel_id=1, source_target_pairs={{0,1},{1,0},{2,3},{3,2},{4,5},{5,4},{6,7},{7,6},{8,9},{9,8},{10,11... | collective-permute-start | bytes 442376 | tf_op jit(solution)/shard_map/ppermute | solution.py:188
  21.4 7.8 %collective-permute-start.4 = (bf16[2,144,256]{2,1,0:T(8,128)(2,1)S(1)}, bf16[2,144,256]{2,1,0:T(8,128)(2,1)S(1)}, u32[]{:S(2)}, u32[]{:S(2)}) collective-permute-start(bf16[2,144,256]{2,1,0:T(8,128)(2,1)S(1)} %collective-permute-done.1.mine_2_), channel_id=1, source_target_pairs={{0,16},{1,17},{2,18},{3,19},{4,20},{5,21},{6,22},{7,23},{8,24},{9,... | collective-permute-start | bytes 442376 | tf_op jit(solution)/shard_map/ppermute | solution.py:185
  22.7 9.8 %collective-permute-start.12 = (bf16[2,144,256]{2,1,0:T(8,128)(2,1)S(1)}, bf16[2,144,256]{2,1,0:T(8,128)(2,1)S(1)}, u32[]{:S(2)}, u32[]{:S(2)}) collective-permute-start(bf16[2,144,256]{2,1,0:T(8,128)(2,1)S(1)} %collective-permute-done.2.mine_1_), channel_id=1, source_target_pairs={{0,1},{1,0},{2,3},{3,2},{4,5},{5,4},{6,7},{7,6},{8,9},{9,8},{10,11... | collective-permute-start | bytes 442376 | tf_op jit(solution)/shard_map/ppermute | solution.py:188
  22.9 10.1 %collective-permute-start.8 = (bf16[2,144,256]{2,1,0:T(8,128)(2,1)S(1)}, bf16[2,144,256]{2,1,0:T(8,128)(2,1)S(1)}, u32[]{:S(2)}, u32[]{:S(2)}) collective-permute-start(bf16[2,144,256]{2,1,0:T(8,128)(2,1)S(1)} %slice.50), channel_id=1, source_target_pairs={{0,12},{1,5},{2,14},{3,7},{4,0},{5,9},{6,2},{7,11},{8,4},{9,13},{1... | collective-permute-start | bytes 442376 | tf_op jit(solution)/shard_map/ppermute | solution.py:182
  29.2 5.1 %collective-permute-start.5 = (bf16[1,144,256]{2,1,0:T(8,128)(2,1)S(1)}, bf16[1,144,256]{2,1,0:T(8,128)(2,1)S(1)}, u32[]{:S(2)}, u32[]{:S(2)}) collective-permute-start(bf16[1,144,256]{2,1,0:T(8,128)(2,1)S(1)} %slice_select_fusion), channel_id=1, source_target_pairs={{0,14},{1,3},{2,0},{3,5},{4,2},{5,7},{6,4},{7,9},{8,6},{9,11},{10,... | collective-permute-start | bytes 221192 | tf_op jit(solution)/shard_map/ppermute | solution.py:182
  32.4 2.7 %collective-permute-start.9 = (bf16[5,144,256]{2,1,0:T(8,128)(2,1)S(1)}, bf16[5,144,256]{2,1,0:T(8,128)(2,1)S(1)}, u32[]{:S(2)}, u32[]{:S(2)}) collective-permute-start(bf16[5,144,256]{2,1,0:T(8,128)(2,1)S(1)} %collective-permute-done.7.mine_0_), channel_id=1, source_target_pairs={{0,1},{1,0},{2,3},{3,2},{4,5},{5,4},{6,7},{7,6},{8,9},{9,8},{10,11... | collective-permute-start | bytes 1105928 | tf_op jit(solution)/shard_map/ppermute | solution.py:188
  32.5 2.5 %collective-permute-start.11 = (bf16[2,144,256]{2,1,0:T(8,128)(2,1)S(1)}, bf16[2,144,256]{2,1,0:T(8,128)(2,1)S(1)}, u32[]{:S(2)}, u32[]{:S(2)}) collective-permute-start(bf16[2,144,256]{2,1,0:T(8,128)(2,1)S(1)} %collective-permute-done.4.mine_2_), channel_id=1, source_target_pairs={{0,1},{1,0},{2,3},{3,2},{4,5},{5,4},{6,7},{7,6},{8,9},{9,8},{10,11... | collective-permute-start | bytes 442376 | tf_op jit(solution)/shard_map/ppermute | solution.py:188
  33.0 2.0 %collective-permute-start.10 = (bf16[2,144,256]{2,1,0:T(8,128)(2,1)S(1)}, bf16[2,144,256]{2,1,0:T(8,128)(2,1)S(1)}, u32[]{:S(2)}, u32[]{:S(2)}) collective-permute-start(bf16[2,144,256]{2,1,0:T(8,128)(2,1)S(1)} %collective-permute-done.8.mine_1_), channel_id=1, source_target_pairs={{0,1},{1,0},{2,3},{3,2},{4,5},{5,4},{6,7},{7,6},{8,9},{9,8},{10,11... | collective-permute-start | bytes 442376 | tf_op jit(solution)/shard_map/ppermute | solution.py:188
  35.7 1.6 %collective-permute-start.14 = (bf16[256,256]{1,0:T(8,128)(2,1)S(1)}, bf16[256,256]{1,0:T(8,128)(2,1)S(1)}, u32[]{:S(2)}, u32[]{:S(2)}) collective-permute-start(bf16[256,256]{1,0:T(8,128)(2,1)S(1)} %shard_map.58.old), channel_id=1, source_target_pairs={{0,32},{1,33},{2,34},{3,35},{4,36},{5,37},{6,38},{7,39},{8,40},{9,... | collective-permute-start | bytes 393224 | tf_op jit(solution)/shard_map/ppermute | solution.py:259
  36.5 1.4 %collective-permute-start.21 = (bf16[256,256]{1,0:T(8,128)(2,1)S(1)}, bf16[256,256]{1,0:T(8,128)(2,1)S(1)}, u32[]{:S(2)}, u32[]{:S(2)}) collective-permute-start(bf16[256,256]{1,0:T(8,128)(2,1)S(1)} %shard_map.66.old), channel_id=1, source_target_pairs={{0,32},{1,33},{2,34},{3,35},{4,36},{5,37},{6,38},{7,39},{8,40},{9,... | collective-permute-start | bytes 393224 | tf_op jit(solution)/shard_map/ppermute | solution.py:259
  37.9 1.3 %collective-permute-start.22 = (bf16[256,256]{1,0:T(8,128)(2,1)S(1)}, bf16[256,256]{1,0:T(8,128)(2,1)S(1)}, u32[]{:S(2)}, u32[]{:S(2)}) collective-permute-start(bf16[256,256]{1,0:T(8,128)(2,1)S(1)} %shard_map.67.old), channel_id=1, source_target_pairs={{0,1},{1,0},{2,3},{3,2},{4,5},{5,4},{6,7},{7,6},{8,9},{9,8},{10,11... | collective-permute-start | bytes 393224 | tf_op jit(solution)/shard_map/ppermute | solution.py:259
  39.3 1.3 %collective-permute-start.23 = (bf16[256,256]{1,0:T(8,128)(2,1)S(1)}, bf16[256,256]{1,0:T(8,128)(2,1)S(1)}, u32[]{:S(2)}, u32[]{:S(2)}) collective-permute-start(bf16[256,256]{1,0:T(8,128)(2,1)S(1)} %shard_map.68.old), channel_id=1, source_target_pairs={{0,1},{1,0},{2,3},{3,2},{4,5},{5,4},{6,7},{7,6},{8,9},{9,8},{10,11... | collective-permute-start | bytes 393224 | tf_op jit(solution)/shard_map/ppermute | solution.py:259
  40.6 8.6 %collective-permute-start.24 = (bf16[256,256]{1,0:T(8,128)(2,1)S(1)}, bf16[256,256]{1,0:T(8,128)(2,1)S(1)}, u32[]{:S(2)}, u32[]{:S(2)}) collective-permute-start(bf16[256,256]{1,0:T(8,128)(2,1)S(1)} %shard_map.69.old), channel_id=1, source_target_pairs={{0,1},{1,0},{2,3},{3,2},{4,5},{5,4},{6,7},{7,6},{8,9},{9,8},{10,11... | collective-permute-start | bytes 393224 | tf_op jit(solution)/shard_map/ppermute | solution.py:259
  41.3 11.9 %collective-permute-start.18 = (bf16[256,256]{1,0:T(8,128)(2,1)S(1)}, bf16[256,256]{1,0:T(8,128)(2,1)S(1)}, u32[]{:S(2)}, u32[]{:S(2)}) collective-permute-start(bf16[256,256]{1,0:T(8,128)(2,1)S(1)} %shard_map.62.old), channel_id=1, source_target_pairs={{0,224},{1,225},{2,226},{3,227},{4,228},{5,229},{6,230},{7,231},{8... | collective-permute-start | bytes 393224 | tf_op jit(solution)/shard_map/ppermute | solution.py:259
  49.2 7.6 %collective-permute-start.25 = (bf16[256,256]{1,0:T(8,128)(2,1)S(1)}, bf16[256,256]{1,0:T(8,128)(2,1)S(1)}, u32[]{:S(2)}, u32[]{:S(2)}) collective-permute-start(bf16[256,256]{1,0:T(8,128)(2,1)S(1)} %shard_map.70.old), channel_id=1, source_target_pairs={{0,224},{1,225},{2,226},{3,227},{4,228},{5,229},{6,230},{7,231},{8... | collective-permute-start | bytes 393224 | tf_op jit(solution)/shard_map/ppermute | solution.py:259
  53.2 3.6 %collective-permute-start.19 = (bf16[256,256]{1,0:T(8,128)(2,1)S(1)}, bf16[256,256]{1,0:T(8,128)(2,1)S(1)}, u32[]{:S(2)}, u32[]{:S(2)}) collective-permute-start(bf16[256,256]{1,0:T(8,128)(2,1)S(1)} %shard_map.63.old), channel_id=1, source_target_pairs={{0,1},{1,0},{2,3},{3,2},{4,5},{5,4},{6,7},{7,6},{8,9},{9,8},{10,11... | collective-permute-start | bytes 393224 | tf_op jit(solution)/shard_map/ppermute | solution.py:259
  56.8 18.9 %collective-permute-start.26 = (bf16[256,256]{1,0:T(8,128)(2,1)S(1)}, bf16[256,256]{1,0:T(8,128)(2,1)S(1)}, u32[]{:S(2)}, u32[]{:S(2)}) collective-permute-start(bf16[256,256]{1,0:T(8,128)(2,1)S(1)} %shard_map.71.old), channel_id=1, source_target_pairs={{0,1},{1,0},{2,3},{3,2},{4,5},{5,4},{6,7},{7,6},{8,9},{9,8},{10,11... | collective-permute-start | bytes 393224 | tf_op jit(solution)/shard_map/ppermute | solution.py:259
  56.8 22.1 %collective-permute-start.20 = (bf16[256,256]{1,0:T(8,128)(2,1)S(1)}, bf16[256,256]{1,0:T(8,128)(2,1)S(1)}, u32[]{:S(2)}, u32[]{:S(2)}) collective-permute-start(bf16[256,256]{1,0:T(8,128)(2,1)S(1)} %shard_map.64.old), channel_id=1, source_target_pairs={{0,1},{1,0},{2,3},{3,2},{4,5},{5,4},{6,7},{7,6},{8,9},{9,8},{10,11... | collective-permute-start | bytes 393224 | tf_op jit(solution)/shard_map/ppermute | solution.py:259
  75.6 5.0 %collective-permute-start.27 = (bf16[256,256]{1,0:T(8,128)(2,1)S(1)}, bf16[256,256]{1,0:T(8,128)(2,1)S(1)}, u32[]{:S(2)}, u32[]{:S(2)}) collective-permute-start(bf16[256,256]{1,0:T(8,128)(2,1)S(1)} %shard_map.72.old), channel_id=1, source_target_pairs={{0,1},{1,0},{2,3},{3,2},{4,5},{5,4},{6,7},{7,6},{8,9},{9,8},{10,11... | collective-permute-start | bytes 393224 | tf_op jit(solution)/shard_map/ppermute | solution.py:259
  (8 other events, 99.1 us)
